TPU v7x, 32 devices: a whole 2x2x4 slice. The times are simulated.
32 devices in a mesh: groups: 2 (over y), grid: 4 (over x, core), mesh: 4 (over z).
Axes of the slice: x: 2, y: 2, z: 4, core: 2. Of those that a mesh axis runs over, the one named last changes fastest.
Arguments:
- grid_in: bfloat16 [227, 16384], P(None, ('groups', 'grid', 'mesh')), parts along dimension 1, may hold values from -6 to 6
- grid_cot: bfloat16 [227, 16384], P(None, ('groups', 'grid', 'mesh')), parts along dimension 1, may hold values from -0.15625 to 0.15625
- enc_src: int32 [256, 4], P(('grid', 'mesh')), may hold values from 0 to 511
- enc_feat: bfloat16 [4, 1024], P(None, ('grid', 'mesh')), may hold values from -6 to 6
- enc_dst: int32 [256, 4], P(('grid', 'mesh')), may hold values from 0 to 63
- enc_count: int32 [256], P(('grid', 'mesh')), may hold values from 1 to 4, as said below
- halo_up: int32 [512], P('mesh'), may hold values from 0 to 255
- halo_down: int32 [512], P('mesh'), may hold values from 0 to 255
- proc_src: int32 [32768], P(('grid', 'mesh')), may hold values from 0 to 511
- proc_dst: int32 [32768], P(('grid', 'mesh')), may hold values from 0 to 63
- dec_send: int32 [256, 4], P(('grid', 'mesh')), may hold values from 0 to 63
- dec_row: int32 [256, 4], P(('grid', 'mesh')), may hold values from 0 to 511
- dec_count: int32 [256], P(('grid', 'mesh')), may hold values from 1 to 4, as said below
- embed_first: bfloat16 [227, 512], replicated, may hold values from -0.375 to 0.375
- embed_second: bfloat16 [512, 512], replicated, may hold values from -0.25 to 0.25
- edge_weight: bfloat16 [512, 512], replicated, may hold values from -0.25 to 0.25
- feature_weight: bfloat16 [4, 512], replicated, may hold values from -3 to 3
- layer_edge_in: bfloat16 [1, 1024, 512], replicated, may hold values from -0.1875 to 0.1875
- layer_edge_out: bfloat16 [1, 512, 512], replicated, may hold values from -0.25 to 0.25
- layer_node_in: bfloat16 [1, 1024, 512], replicated, may hold values from -0.1875 to 0.1875
- layer_node_out: bfloat16 [1, 512, 512], replicated, may hold values from -0.25 to 0.25
- out_first: bfloat16 [1024, 512], replicated, may hold values from -0.1875 to 0.1875
- out_second: bfloat16 [227, 512], replicated, may hold values from -0.25 to 0.25
Outputs:
- delta: bfloat16 [227, 16384], P(None, ('groups', 'grid', 'mesh')), parts along dimension 1
- grad_embed_first: float32 [454, 512], P('groups', ('grid', 'mesh')), parts along dimension 0
- grad_embed_second: float32 [1024, 512], P('groups', ('grid', 'mesh')), parts along dimension 0
- grad_edge: float32 [1024, 512], P('groups', ('grid', 'mesh')), parts along dimension 0
- grad_feature: float32 [8, 512], P('groups', ('grid', 'mesh')), parts along dimension 0
- grad_edge_in: float32 [2, 1024, 512], P('groups', None, ('grid', 'mesh')), parts along dimension 0
- grad_edge_out: float32 [2, 512, 512], P('groups', None, ('grid', 'mesh')), parts along dimension 0
- grad_node_in: float32 [2, 1024, 512], P('groups', None, ('grid', 'mesh')), parts along dimension 0
- grad_node_out: float32 [2, 512, 512], P('groups', None, ('grid', 'mesh')), parts along dimension 0
- grad_out_first: float32 [2048, 512], P('groups', ('grid', 'mesh')), parts along dimension 0
- grad_out_second: float32 [454, 512], P('groups', ('grid', 'mesh')), parts along dimension 0
There are 2 independent parts, one for each index of `groups`. A program takes and returns all parts, laid end to end along the dimension named above; an argument that names none is the same for every part. Nothing has to cross between parts.
Inputs may be any that keep to these rules, and one draw needn't show every extreme that they name: `enc_count`: live encoder slots of each block; one owner has 4 live slots from every tile. `dec_count`: live decoder slots of each block; one tile has 4 live slots from every owner.
All inputs are finite; a program needn't handle non-finite values.
Results may differ from a plain program's by a relative error of at most 0.025.
Values may be sent and summed in bfloat16 or wider, within the bound.
A program may use at most 128 MiB of HBM per device.

v0:
```python
import jax
import jax.numpy as jnp
from jax import lax
from jax.sharding import PartitionSpec as P

LAYERS = 1
G_DEV = 512
MESH_DEV = 64


def shortened(value):

    def short(part):
        return part.astype(jnp.bfloat16) if part.dtype == jnp.float32 else part

    return jax.tree.map(short, value)


def extended_2(block, sides, width):
    for axis, dim in sides:
        count = lax.axis_size(axis)
        forward = [(i, i + 1) for i in range(count - 1)]
        backward = [(target, source) for source, target in forward]
        low = lax.ppermute(
            lax.slice_in_dim(block, block.shape[dim] - width, None, axis=dim), axis, forward
        )
        high = lax.ppermute(lax.slice_in_dim(block, 0, width, axis=dim), axis, backward)
        block = jnp.concatenate([low, block, high], axis=dim)
    return block


def round_low(values):
    return lax.optimization_barrier(values.astype(jnp.bfloat16)).astype(jnp.float32)


def plain_product(left, right):
    return jnp.dot(
        left.astype(jnp.bfloat16), right.astype(jnp.bfloat16), preferred_element_type=jnp.float32
    )


def product_forward(left, right):
    return (plain_product(left, right), (left, right))


def product_backward(saved, incoming):
    left, right = saved
    grad_low = incoming.astype(jnp.bfloat16)
    grad_left = jnp.dot(grad_low, right.astype(jnp.bfloat16).T, preferred_element_type=jnp.float32)
    grad_right = jnp.dot(left.astype(jnp.bfloat16).T, grad_low, preferred_element_type=jnp.float32)
    return (grad_left, grad_right)


def product(left, right):
    core = jax.custom_vjp(plain_product)
    core.defvjp(product_forward, product_backward)
    return core(left, right)


def one_hot(targets, count):
    return (targets[None, :] == jnp.arange(count, dtype=jnp.int32)[:, None]).astype(jnp.float32)


def embed_grid(grid_tile, first, second):
    hidden = round_low(jax.nn.silu(product(grid_tile.astype(jnp.float32).T, first)))
    return round_low(product(hidden, second))


def send_messages(grid_latent, senders, features, edge_weight, feature_weight):
    rows = jnp.take(grid_latent, senders, axis=0)
    summed = product(rows, edge_weight) + product(features.astype(jnp.float32).T, feature_weight)
    return round_low(jax.nn.silu(summed))


def gather_mesh(received, targets, count):
    total = product(one_hot(targets, count), received)
    scale = lax.rsqrt(jnp.mean(total * total, axis=-1, keepdims=True) + 1e-05)
    return round_low(total * scale)


def process_layer(latent, extended, senders, targets, edge_in, edge_out, node_in, node_out):
    pairs = jnp.concatenate(
        [jnp.take(extended, senders, axis=0), jnp.take(latent, targets, axis=0)], axis=1
    )
    hidden = round_low(jax.nn.silu(product(pairs, edge_in)))
    messages = round_low(product(hidden, edge_out))
    summed = round_low(product(one_hot(targets, latent.shape[0]), messages))
    joined = jnp.concatenate([latent, summed], axis=1)
    inner = round_low(jax.nn.silu(product(joined, node_in)))
    return round_low(latent + product(inner, node_out))


def collect_grid(received, targets, count):
    return round_low(product(one_hot(targets, count), received))


def decode_grid(grid_latent, collected, out_first, out_second):
    joined = jnp.concatenate([grid_latent, collected], axis=1)
    inner = round_low(jax.nn.silu(product(joined, out_first)))
    return product(inner, out_second.T).T


def route_forward(values):
    return lax.all_to_all(values, ("grid", "mesh"), split_axis=0, concat_axis=0, tiled=True)


def route_backward(values):
    return jax.tree.map(
        lambda part, own: part.astype(own.dtype),
        lax.all_to_all(
            shortened(values), ("grid", "mesh"), split_axis=0, concat_axis=0, tiled=True
        ),
        values,
    )


def flatten_rows(grads):
    return tuple((matrix.reshape(-1, matrix.shape[-1]) for matrix in grads))


def restore_rows(summed, grads):
    return tuple(
        (flat.reshape(matrix.shape[:-1] + (flat.shape[-1],)) for flat, matrix in zip(summed, grads))
    )


def reduce_whole(grads):
    summed = lax.psum_scatter(
        flatten_rows(grads), ("grid", "mesh"), scatter_dimension=1, tiled=True
    )
    return restore_rows(summed, grads)


def on_device(
    grid_in,
    grid_cot,
    enc_src,
    enc_feat,
    enc_dst,
    enc_count,
    halo_up,
    halo_down,
    proc_src,
    proc_dst,
    dec_send,
    dec_row,
    dec_count,
    embed_first,
    embed_second,
    edge_weight,
    feature_weight,
    layer_edge_in,
    layer_edge_out,
    layer_node_in,
    layer_node_out,
    out_first,
    out_second,
):
    halo_rows = halo_up.shape[0]
    capacity = enc_src.shape[1]
    dec_capacity = dec_send.shape[1]
    (
        first_wide,
        second_wide,
        edge_wide,
        feature_wide,
        edge_in_wide,
        edge_out_wide,
        node_in_wide,
        node_out_wide,
        out_first_wide,
        out_second_wide,
    ) = tuple(
        (
            matrix.astype(jnp.float32)
            for matrix in (
                embed_first,
                embed_second,
                edge_weight,
                feature_weight,
                layer_edge_in,
                layer_edge_out,
                layer_node_in,
                layer_node_out,
                out_first,
                out_second,
            )
        )
    )
    grid_latent, pull_embed = jax.vjp(
        lambda first_rows, second_rows: embed_grid(grid_in, first_rows, second_rows),
        first_wide,
        second_wide,
    )
    send_list = enc_src.reshape(-1)
    messages, pull_send = jax.vjp(
        lambda latent_rows, edge_rows, feature_rows: send_messages(
            latent_rows, send_list, enc_feat, edge_rows, feature_rows
        ),
        grid_latent,
        edge_wide,
        feature_wide,
    )
    received = route_forward(messages.astype(jnp.bfloat16)).astype(jnp.float32)
    enc_valid = jnp.arange(capacity, dtype=jnp.int32)[None, :] < enc_count[:, None]
    enc_targets = jnp.where(enc_valid, enc_dst, -1).reshape(-1)
    latent, pull_mesh = jax.vjp(
        lambda arrived_rows: gather_mesh(arrived_rows, enc_targets, MESH_DEV), received
    )
    layer_index = 0
    table = lax.all_gather(latent.astype(jnp.bfloat16), "grid", axis=0, tiled=True).astype(
        jnp.float32
    )
    outgoing = jnp.concatenate(
        [jnp.take(table, halo_down, axis=0), jnp.take(table, halo_up, axis=0)], axis=0
    )
    widened = extended_2(outgoing.astype(jnp.bfloat16), (("mesh", 0),), halo_rows).astype(
        jnp.float32
    )
    extended = jnp.concatenate(
        [widened[:halo_rows], table, widened[widened.shape[0] - halo_rows :]], axis=0
    )
    latent, pull_layer = jax.vjp(
        lambda latent_rows, extended_rows, first_rows, second_rows, third_rows, fourth_rows: process_layer(
            latent_rows,
            extended_rows,
            proc_src,
            proc_dst,
            first_rows,
            second_rows,
            third_rows,
            fourth_rows,
        ),
        latent,
        extended,
        edge_in_wide[layer_index],
        edge_out_wide[layer_index],
        node_in_wide[layer_index],
        node_out_wide[layer_index],
    )
    layer_pulls = [pull_layer]
    pick_list = dec_send.reshape(-1)
    sent, pull_pick = jax.vjp(lambda latent_rows: jnp.take(latent_rows, pick_list, axis=0), latent)
    arrived = route_forward(sent.astype(jnp.bfloat16)).astype(jnp.float32)
    dec_valid = jnp.arange(dec_capacity, dtype=jnp.int32)[None, :] < dec_count[:, None]
    dec_targets = jnp.where(dec_valid, dec_row, -1).reshape(-1)
    collected, pull_collect = jax.vjp(
        lambda arrived_rows: collect_grid(arrived_rows, dec_targets, G_DEV), arrived
    )
    delta_full, pull_out = jax.vjp(
        decode_grid, grid_latent, collected, out_first_wide, out_second_wide
    )
    grad_grid_out, grad_collected, grad_out_first, grad_out_second = pull_out(
        grid_cot.astype(jnp.float32)
    )
    out_grads = (grad_out_first, grad_out_second)
    (grad_arrived,) = pull_collect(grad_collected)
    grad_sent = route_backward(grad_arrived)
    (grad_latent,) = pull_pick(grad_sent)
    layer_grads = [None] * LAYERS
    layer_index = 0
    grad_own, grad_extended, grad_first, grad_second, grad_third, grad_fourth = layer_pulls[
        layer_index
    ](grad_latent)
    part_rows = grad_extended.shape[0] - 2 * halo_rows
    lower = grad_extended[:halo_rows]
    upper = grad_extended[halo_rows + part_rows :]
    returned = extended_2(
        shortened(jnp.concatenate([lower, upper], axis=0)), (("mesh", 0),), halo_rows
    )
    grad_table = grad_extended[halo_rows : halo_rows + part_rows]
    grad_table = grad_table.at[halo_down].add(returned[:halo_rows])
    grad_table = grad_table.at[halo_up].add(returned[returned.shape[0] - halo_rows :])
    grad_latent = grad_own + lax.psum_scatter(
        grad_table.astype(jnp.bfloat16), "grid", scatter_dimension=0, tiled=True
    ).astype(jnp.float32)
    current = (grad_first, grad_second, grad_third, grad_fourth)
    layer_grads[layer_index] = current
    (grad_received,) = pull_mesh(grad_latent)
    grad_messages = route_backward(grad_received)
    grad_grid_send, grad_edge, grad_feature = pull_send(grad_messages)
    grad_embed_first, grad_embed_second = pull_embed(grad_grid_out + grad_grid_send)
    stacked = tuple((jnp.stack([layer_grads[0][member]], axis=0) for member in range(4)))
    encoder_grads = (grad_embed_first, grad_embed_second, grad_edge, grad_feature)
    everything = reduce_whole(encoder_grads + stacked + out_grads)
    return (delta_full.astype(jnp.bfloat16),) + tuple(everything)


def solution(mesh):
    return jax.shard_map(
        on_device,
        mesh=mesh,
        in_specs=(
            P(None, ("groups", "grid", "mesh")),
            P(None, ("groups", "grid", "mesh")),
            P(("grid", "mesh"), None),
            P(None, ("grid", "mesh")),
            P(("grid", "mesh"), None),
            P(("grid", "mesh")),
            P("mesh"),
            P("mesh"),
            P(("grid", "mesh")),
            P(("grid", "mesh")),
            P(("grid", "mesh"), None),
            P(("grid", "mesh"), None),
            P(("grid", "mesh")),
            P(),
            P(),
            P(),
            P(),
            P(),
            P(),
            P(),
            P(),
            P(),
            P(),
        ),
        out_specs=(
            P(None, ("groups", "grid", "mesh")),
            P("groups", ("grid", "mesh")),
            P("groups", ("grid", "mesh")),
            P("groups", ("grid", "mesh")),
            P("groups", ("grid", "mesh")),
            P("groups", None, ("grid", "mesh")),
            P("groups", None, ("grid", "mesh")),
            P("groups", None, ("grid", "mesh")),
            P("groups", None, ("grid", "mesh")),
            P("groups", ("grid", "mesh")),
            P("groups", ("grid", "mesh")),
        ),
        check_vma=False,
    )
```

profile of v0, /device:TPU:0, one launch (start us, length us, event | category | flops | bytes accessed | tf_op | source)
XLA Modules:
  0.0 804.0 jit_solution(9477446330335413695)
XLA Ops:
  7.2 0.9 copy.53
  9.0 2.5 multiply_convert_fusion.2
  13.2 0.9 multiply_convert_fusion.5
  14.8 7.4 all-to-all-start
  23.2 1.1 convolution_convert_fusion.5
  24.7 4.2 all-to-all-done
  29.8 5.8 all_gather.3
  38.0 2.9 collective-permute-start
  41.7 1.3 collective-permute-start.1
  43.0 7.5 gather_fusion.2
  50.6 1.7 select_convert_fusion
  52.2 1.0 maximum_convert_fusion
  53.3 9.2 %gather_fusion.1 = bf16[2048,512]{1,0:T(8,128)(2,1)} fusion(bf16[512,512]{1,0:T(8,128)(2,1)S(1)} %pad_maximum_fusion.3, s32[2048]{0:T(1024)S(1)} %get-tuple-element.52), kind=kCustom, calls=%fused_computation.3 | custom fusion | bytes 4202496 | tf_op jit(solution)/shard_map/jvp(jit(_take))/gather | solution.py:83
  62.5 2.0 select_convert_fusion.1
  64.7 4.4 multiply_convert_fusion
  69.2 1.2 convolution_convert_fusion.2
  73.1 4.8 all-to-all-start.1
  78.2 6.4 all-to-all-done.1
  85.0 2.3 multiply_convert_fusion.1
  87.3 0.9 fusion.75
  88.2 1.4 copy-done.16
  89.9 9.2 %all_to_all.42 = bf16[16,4,512]{2,1,0:T(4,128)(2,1)S(1)} all-to-all(bf16[16,4,512]{2,1,0:T(4,128)(2,1)S(1)} %all_to_all.33), channel_id=1, replica_groups=mesh['groups'=2,'grid'=4,'mesh'=4] {'grid','mesh'}, dimensions={0} | all-to-all | bytes 131072 | tf_op jit(solution)/shard_map/all_to_all | solution.py:110
  99.2 1.3 scatter_custom_fusion
  100.8 1.7 fusion.17
  103.2 1.4 copy-done.9
  104.6 1.3 convolution_convert_fusion
  106.7 6.5 fusion.21
  113.2 13.7 %scatter_custom_fusion.1 = f32[512,512]{1,0:T(8,128)S(1)} fusion(s32[2048]{0:T(1024)} %get-tuple-element.51, f32[2048,1024]{1,0:T(8,128)} %fusion.21, f32[]{:T(128)} %constant.91.clone.1), kind=kCustom, calls=%fused_computation.20 | custom fusion | flops 1048576 | bytes 5243392 | tf_op jit(solution)/shard_map/transpose(jvp(jit(_take)))/scatter-add | solution.py:83
  127.7 3.0 collective-permute-start.2
  130.8 1.4 collective-permute-start.3
  133.1 1.9 scatter_custom_fusion.2
  135.1 3.2 collective-permute-done.3
  138.3 1.9 scatter_custom_fusion.3
  141.0 17.6 %reduce-scatter.18.cloned.1.call-done = bf16[64,512]{1,0:T(8,128)(2,1)} async-done(((bf16[256,512]{1,0:T(8,128)(2,1)}), bf16[64,512]{1,0:T(8,128)(2,1)}) %reduce-scatter.18.cloned.1.call-update) | async-done | bytes 65552 | tf_op jit(solution)/shard_map/reduce_scatter | solution.py:274
  158.7 0.9 fusion.46
  159.6 13.8 %scatter_custom_fusion.4 = f32[64,512]{1,0:T(8,128)S(1)} fusion(f32[64,512]{1,0:T(8,128)S(1)} %fusion.46, s32[2048]{0:T(1024)S(1)} %get-tuple-element.49, f32[2048,1024]{1,0:T(8,128)} %fusion.21), kind=kCustom, calls=%fused_computation.18 | custom fusion | flops 1048576 | bytes 4325376 | tf_op jit(solution)/shard_map/transpose(jvp(jit(_take)))/scatter-add | solution.py:83
  174.5 4.7 all-to-all-start.3
  179.3 6.6 all-to-all-done.3
  187.1 1.1 convolution_bitcast_fusion
  188.1 1.4 split.26
  189.5 2.0 copy.62
  191.6 1.3 fusion.81
  192.9 1.4 scatter_fusion
  194.9 1.9 convolution_bitcast_fusion.1
  196.8 1.0 copy.58
  197.9 1.4 fusion.84
  199.4 4.6 fusion.83
  204.1 1.5 fusion.82
  205.7 1.3 fusion.71
  207.1 3.6 fusion.24
  210.9 1.9 fusion.50
  212.8 8.3 %fusion.7 = f32[1024,512]{0,1:T(8,128)} fusion(bf16[2048,512]{1,0:T(8,128)(2,1)} %select_convert_fusion, bf16[2048,512]{1,0:T(8,128)(2,1)} %copy-done.15, bf16[2048,512]{1,0:T(8,128)(2,1)} %copy-done.65, f32[2048,512]{1,0:T(8,128)} %get-tuple-element.60), kind=kOutput, calls=%fused_computation.30 | convolution fusion | flops 2167406592 | bytes 12582912 | tf_op jit(solution)/shard_map/transpose(jvp())/dot_general | solution.py:57
  221.1 1.0 fusion.9
  222.2 18.5 %reduce-scatter.36.cloned.1.call-done = f32[32,4]{1,0:T(8,128)} async-done(((f32[512,4]{1,0:T(8,128)}), f32[32,4]{1,0:T(8,128)}) %reduce-scatter.36.cloned.1.call-update) | async-done | bytes 528
  240.6 1.4 copy.61
  242.0 58.0 %reduce-scatter.38.cloned.1.call-done = f32[32,227]{1,0:T(8,128)} async-done(((f32[512,227]{1,0:T(8,128)}), f32[32,227]{1,0:T(8,128)}) %reduce-scatter.38.cloned.1.call-update) | async-done | bytes 29072
  300.0 58.9 %reduce-scatter.34.cloned.1.call-done = f32[32,227]{1,0:T(8,128)} async-done(((f32[512,227]{1,0:T(8,128)}), f32[32,227]{1,0:T(8,128)}) %reduce-scatter.34.cloned.1.call-update) | async-done | bytes 29072
  358.9 60.9 %reduce-scatter.30.cloned.1.call-done = f32[512,32]{0,1:T(8,128)} async-done(((f32[512,512]{0,1:T(8,128)}), f32[512,32]{0,1:T(8,128)}) %reduce-scatter.30.cloned.1.call-update) | async-done | bytes 65552 | tf_op jit(solution)/shard_map/reduce_scatter | solution.py:128
  419.8 60.4 %reduce-scatter.26.cloned.1.call-done = f32[512,32]{0,1:T(8,128)} async-done(((f32[512,512]{0,1:T(8,128)}), f32[512,32]{0,1:T(8,128)}) %reduce-scatter.26.cloned.1.call-update) | async-done | bytes 65552 | tf_op jit(solution)/shard_map/reduce_scatter | solution.py:128
  480.2 61.1 %reduce-scatter.20.cloned.1.call-done = f32[512,32]{0,1:T(8,128)} async-done(((f32[512,512]{0,1:T(8,128)}), f32[512,32]{0,1:T(8,128)}) %reduce-scatter.20.cloned.1.call-update) | async-done | bytes 65552 | tf_op jit(solution)/shard_map/reduce_scatter | solution.py:128
  541.3 60.7 %reduce-scatter.22.cloned.1.call-done = f32[512,32]{0,1:T(8,128)} async-done(((f32[512,512]{0,1:T(8,128)}), f32[512,32]{0,1:T(8,128)}) %reduce-scatter.22.cloned.1.call-update) | async-done | bytes 65552 | tf_op jit(solution)/shard_map/reduce_scatter | solution.py:128
  602.0 65.3 %reduce-scatter.32.cloned.1.call-done = f32[1024,32]{0,1:T(8,128)} async-done(((f32[1024,512]{0,1:T(8,128)}), f32[1024,32]{0,1:T(8,128)}) %reduce-scatter.32.cloned.1.call-update) | async-done | bytes 131088 | tf_op jit(solution)/shard_map/reduce_scatter | solution.py:128
  667.3 64.8 %reduce-scatter.28.cloned.1.call-done = f32[1024,32]{0,1:T(8,128)} async-done(((f32[1024,512]{0,1:T(8,128)}), f32[1024,32]{0,1:T(8,128)}) %reduce-scatter.28.cloned.1.call-update) | async-done | bytes 131088 | tf_op jit(solution)/shard_map/reduce_scatter | solution.py:128
  732.1 65.4 %reduce-scatter.24.cloned.1.call-done = f32[1024,32]{0,1:T(8,128)} async-done(((f32[1024,512]{0,1:T(8,128)}), f32[1024,32]{0,1:T(8,128)}) %reduce-scatter.24.cloned.1.call-update) | async-done | bytes 131088 | tf_op jit(solution)/shard_map/reduce_scatter | solution.py:128
  (230 shorter events, 19.9 us)
Async XLA Ops:
  7.2 57.4 %copy-start = (bf16[1,1024,512]{2,1,0:T(8,128)(2,1)S(1)}, bf16[1,1024,512]{2,1,0:T(8,128)(2,1)}, u32[]{:S(2)}) copy-start(bf16[1,1024,512]{2,1,0:T(8,128)(2,1)} %param.42) | copy-start | bytes 3145732
  7.2 5.1 copy-start.41
  7.2 5.1 copy-start.43
  7.2 6.0 copy-start.25
  8.3 5.8 copy-start.50
  8.9 13.3 %copy-start.62 = (s32[128]{0:T(128)S(1)}, s32[128]{0:T(128)}, u32[]{:S(2)}) copy-start(s32[128]{0:T(128)} %param.31) | copy-start | bytes 1540
  8.9 13.3 %copy-start.63 = (s32[128]{0:T(128)S(1)}, s32[128]{0:T(128)}, u32[]{:S(2)}) copy-start(s32[128]{0:T(128)} %param.32) | copy-start | bytes 1540
  8.9 13.4 %copy-start.38 = (s32[16,4]{0,1:T(4,128)S(1)}, s32[16,4]{0,1:T(4,128)}, u32[]{:S(2)}) copy-start(s32[16,4]{0,1:T(4,128)} %param.35) | copy-start | bytes 772
  8.9 13.5 %copy-start.37 = (s32[2048]{0:T(1024)S(1)}, s32[2048]{0:T(1024)}, u32[]{:S(2)}) copy-start(s32[2048]{0:T(1024)} %param.33) | copy-start | bytes 24580
  8.9 14.1 %copy-start.35 = (s32[2048]{0:T(1024)S(1)}, s32[2048]{0:T(1024)}, u32[]{:S(2)}) copy-start(s32[2048]{0:T(1024)} %param.34) | copy-start | bytes 24580
  8.9 14.2 %copy-start.48 = (s32[16,4]{0,1:T(4,128)S(1)}, s32[16,4]{0,1:T(4,128)}, u32[]{:S(2)}) copy-start(s32[16,4]{0,1:T(4,128)} %param.29) | copy-start | bytes 772
  8.9 14.2 %copy-start.54 = (s32[16]{0:T(128)S(1)}, s32[16]{0:T(128)}, u32[]{:S(2)}) copy-start(s32[16]{0:T(128)} %param.30) | copy-start | bytes 196
  8.9 14.2 %copy-start.18 = (bf16[227,512]{1,0:T(8,128)(2,1)S(1)}, bf16[227,512]{1,0:T(8,128)(2,1)}, u32[]{:S(2)}) copy-start(bf16[227,512]{1,0:T(8,128)(2,1)} %param.26) | copy-start | bytes 697348
  9.0 14.2 %copy-start.20 = (bf16[227,512]{1,0:T(8,128)(2,1)S(1)}, bf16[227,512]{1,0:T(8,128)(2,1)}, u32[]{:S(2)}) copy-start(bf16[227,512]{1,0:T(8,128)(2,1)} %param.47) | copy-start | bytes 697348
  12.3 30.7 %copy-start.3 = (bf16[512,512]{1,0:T(8,128)(2,1)}, bf16[512,512]{1,0:T(8,128)(2,1)S(1)}, u32[]{:S(2)}) copy-start(bf16[512,512]{1,0:T(8,128)(2,1)S(1)} %convolution_convert_fusion.4) | copy-start | bytes 1572868
  13.2 11.4 %copy-start.31 = (bf16[64,512]{1,0:T(8,128)(2,1)}, bf16[64,512]{1,0:T(8,128)(2,1)S(1)}, u32[]{:S(2)}) copy-start(bf16[64,512]{1,0:T(8,128)(2,1)S(1)} %gather_fusion) | copy-start | bytes 196612
  14.8 14.0 %all-to-all-start = ((bf16[16,4,512]{2,1,0:T(4,128)(2,1)}), bf16[16,4,512]{2,1,0:T(4,128)(2,1)S(1)}, u32[]{:S(2)}, u32[]{:S(2)}) async-start(bf16[16,4,512]{2,1,0:T(4,128)(2,1)} %all_to_all.28), calls=%async_computation | async-start | bytes 131072 | tf_op jit(solution)/shard_map/all_to_all | solution.py:104
  22.2 28.3 %copy-start.56 = (s32[128]{0:T(128)}, s32[128]{0:T(128)S(1)}, u32[]{:S(2)}) copy-start(s32[128]{0:T(128)S(1)} %compare_select_fusion.4) | copy-start | bytes 1540
  23.2 6.0 copy-start.58
  24.6 25.9 %copy-start.39 = (s32[64]{0:T(128)}, s32[64]{0:T(128)S(1)}, u32[]{:S(2)}) copy-start(s32[64]{0:T(128)S(1)} %eq.47) | copy-start | bytes 772
  29.1 21.5 %copy-start.52 = (f32[64]{0:T(128)}, f32[64]{0:T(128)S(1)}, u32[]{:S(2)}) copy-start(f32[64]{0:T(128)S(1)} %get-tuple-element.57) | copy-start | bytes 772
  29.1 21.5 %copy-start.44 = (f32[64]{0:T(128)}, f32[64]{0:T(128)S(1)}, u32[]{:S(2)}) copy-start(f32[64]{0:T(128)S(1)} %fusion.63) | copy-start | bytes 772
  38.0 14.2 %collective-permute-start = (bf16[128,512]{1,0:T(8,128)(2,1)}, bf16[128,512]{1,0:T(8,128)(2,1)}, u32[]{:S(2)}, u32[]{:S(2)}) collective-permute-start(bf16[128,512]{1,0:T(8,128)(2,1)} %select_convert_fusion.3), channel_id=1, source_target_pairs={{0,1},{1,2},{2,3},{4,5},{5,6},{6,7},{8,9},{9,10},{10,11},{12,13},{... | collective-permute-start | bytes 393224 | tf_op jit(solution)/shard_map/ppermute | solution.py:24
  41.7 10.5 %collective-permute-start.1 = (bf16[128,512]{1,0:T(8,128)(2,1)}, bf16[128,512]{1,0:T(8,128)(2,1)}, u32[]{:S(2)}, u32[]{:S(2)}) collective-permute-start(bf16[128,512]{1,0:T(8,128)(2,1)} %select_convert_fusion.2), channel_id=1, source_target_pairs={{1,0},{2,1},{3,2},{5,4},{6,5},{7,6},{9,8},{10,9},{11,10},{13,12},{... | collective-permute-start | bytes 393224 | tf_op jit(solution)/shard_map/ppermute | solution.py:27
  64.7 4.4 copy-start.15
  64.7 4.4 copy-start.60
  70.5 7.5 copy-start.49
  70.5 7.5 copy-start.55
  70.5 14.4 %copy-start.4 = (bf16[512,512]{1,0:T(8,128)(2,1)S(1)}, bf16[512,512]{1,0:T(8,128)(2,1)}, u32[]{:S(2)}) copy-start(bf16[512,512]{1,0:T(8,128)(2,1)} %copy-done.3) | copy-start | bytes 1572868
  71.1 13.5 %copy-start.29 = (bf16[64,512]{1,0:T(8,128)(2,1)}, bf16[64,512]{1,0:T(8,128)(2,1)S(1)}, u32[]{:S(2)}) copy-start(bf16[64,512]{1,0:T(8,128)(2,1)S(1)} %convolution_convert_fusion.11) | copy-start | bytes 196612
  71.4 13.2 %copy-start.33 = (bf16[64,512]{1,0:T(8,128)(2,1)}, bf16[64,512]{1,0:T(8,128)(2,1)S(1)}, u32[]{:S(2)}) copy-start(bf16[64,512]{1,0:T(8,128)(2,1)S(1)} %get-tuple-element.61) | copy-start | bytes 196612
  71.5 29.3 %copy-start.23 = (f32[64,512]{1,0:T(8,128)}, f32[64,512]{1,0:T(8,128)S(1)}, u32[]{:S(2)}) copy-start(f32[64,512]{1,0:T(8,128)S(1)} %get-tuple-element.62) | copy-start | bytes 393220
  73.1 11.5 %all-to-all-start.1 = ((bf16[16,4,512]{2,1,0:T(4,128)(2,1)}), bf16[16,4,512]{2,1,0:T(4,128)(2,1)S(1)}, u32[]{:S(2)}, u32[]{:S(2)}) async-start(bf16[16,4,512]{2,1,0:T(4,128)(2,1)} %select_convert_fusion.4), calls=%async_computation.1 | async-start | bytes 131072 | tf_op jit(solution)/shard_map/all_to_all | solution.py:104
  78.0 80.7 %reduce-scatter.18.cloned.1.call-start = ((), (), s32[]{:S(2)}) async-start(), calls=%async_computation.15 | async-start | bytes 327680 | tf_op jit(solution)/shard_map/reduce_scatter | solution.py:274
  87.3 99.7 %copy-start.7 = (bf16[512,512]{1,0:T(8,128)(2,1)}, bf16[512,512]{1,0:T(8,128)(2,1)S(1)}, u32[]{:S(2)}) copy-start(bf16[512,512]{1,0:T(8,128)(2,1)S(1)} %get-tuple-element.63) | copy-start | bytes 1572868
  89.6 15.0 %copy-start.61 = (bf16[1,512,512]{2,1,0:T(8,128)(2,1)S(1)}, bf16[1,512,512]{2,1,0:T(8,128)(2,1)}, u32[]{:S(2)}) copy-start(bf16[1,512,512]{2,1,0:T(8,128)(2,1)} %param.43) | copy-start | bytes 1572868
  105.9 7.4 copy-start.65
  127.7 45.8 %copy-start.13 = (f32[64,512]{1,0:T(8,128)S(1)}, f32[64,512]{1,0:T(8,128)}, u32[]{:S(2)}) copy-start(f32[64,512]{1,0:T(8,128)} %copy-done.12) | copy-start | bytes 393220
  127.7 5.4 collective-permute-start.2
  130.7 42.8 %copy-start.53 = (f32[64]{0:T(128)S(1)}, f32[64]{0:T(128)}, u32[]{:S(2)}) copy-start(f32[64]{0:T(128)} %copy-done.52) | copy-start | bytes 772
  130.7 42.9 %copy-start.40 = (s32[64]{0:T(128)S(1)}, s32[64]{0:T(128)}, u32[]{:S(2)}) copy-start(s32[64]{0:T(128)} %copy-done.39) | copy-start | bytes 772
  130.8 42.9 %copy-start.45 = (f32[64]{0:T(128)S(1)}, f32[64]{0:T(128)}, u32[]{:S(2)}) copy-start(f32[64]{0:T(128)} %copy-done.44) | copy-start | bytes 772
  130.8 7.6 collective-permute-start.3
  132.2 53.7 %copy-start.36 = (f32[64,512]{1,0:T(8,128)S(1)}, f32[64,512]{1,0:T(8,128)}, u32[]{:S(2)}) copy-start(f32[64,512]{1,0:T(8,128)} %get-tuple-element.56) | copy-start | bytes 393220
  132.2 53.7 %copy-start.42 = (bf16[4,64]{1,0:T(4,128)(2,1)S(1)}, bf16[4,64]{1,0:T(4,128)(2,1)}, u32[]{:S(2)}) copy-start(bf16[4,64]{1,0:T(4,128)(2,1)} %param.28) | copy-start | bytes 1540
  135.1 52.0 %copy-start.19 = (bf16[227,512]{1,0:T(8,128)(2,1)S(1)}, bf16[227,512]{1,0:T(8,128)(2,1)}, u32[]{:S(2)}) copy-start(bf16[227,512]{1,0:T(8,128)(2,1)} %param.26) | copy-start | bytes 697348
  173.4 19.5 %copy-start.47 = (s32[64]{0:T(128)S(1)}, s32[64]{0:T(128)}, u32[]{:S(2)}) copy-start(s32[64]{0:T(128)} %copy-done.46) | copy-start | bytes 772
  174.5 11.3 %all-to-all-start.3 = ((bf16[16,4,512]{2,1,0:T(4,128)(2,1)}), bf16[16,4,512]{2,1,0:T(4,128)(2,1)S(1)}, u32[]{:S(2)}, u32[]{:S(2)}) async-start(bf16[16,4,512]{2,1,0:T(4,128)(2,1)} %all_to_all.35), calls=%async_computation.4 | async-start | bytes 131072 | tf_op jit(solution)/shard_map/all_to_all | solution.py:110
  179.2 61.4 %reduce-scatter.36.cloned.1.call-start = ((), (), s32[]{:S(2)}) async-start(), calls=%async_computation.24 | async-start | bytes 278528
  187.0 113.0 %reduce-scatter.38.cloned.1.call-start = ((), (), s32[]{:S(2)}) async-start(), calls=%async_computation.25 | async-start | bytes 557056
  188.1 6.2 copy-start.2
  191.6 167.3 %reduce-scatter.34.cloned.1.call-start = ((), (), s32[]{:S(2)}) async-start(), calls=%async_computation.23 | async-start | bytes 557056
  197.9 221.9 %reduce-scatter.30.cloned.1.call-start = ((), (), s32[]{:S(2)}) async-start(), calls=%async_computation.21 | async-start | bytes 1114112 | tf_op jit(solution)/shard_map/reduce_scatter | solution.py:128
  199.4 4.8 copy-start.11
  199.4 6.3 copy-start.32
  199.4 6.3 copy-start.51
  199.4 280.8 %reduce-scatter.26.cloned.1.call-start = ((), (), s32[]{:S(2)}) async-start(), calls=%async_computation.19 | async-start | bytes 1114112 | tf_op jit(solution)/shard_map/reduce_scatter | solution.py:128
  204.1 337.3 %reduce-scatter.20.cloned.1.call-start = ((), (), s32[]{:S(2)}) async-start(), calls=%async_computation.16 | async-start | bytes 1114112 | tf_op jit(solution)/shard_map/reduce_scatter | solution.py:128
  205.6 396.4 %reduce-scatter.22.cloned.1.call-start = ((), (), s32[]{:S(2)}) async-start(), calls=%async_computation.17 | async-start | bytes 1114112 | tf_op jit(solution)/shard_map/reduce_scatter | solution.py:128
  207.1 460.2 %reduce-scatter.32.cloned.1.call-start = ((), (), s32[]{:S(2)}) async-start(), calls=%async_computation.22 | async-start | bytes 2228224 | tf_op jit(solution)/shard_map/reduce_scatter | solution.py:128
  210.8 521.3 %reduce-scatter.28.cloned.1.call-start = ((), (), s32[]{:S(2)}) async-start(), calls=%async_computation.20 | async-start | bytes 2228224 | tf_op jit(solution)/shard_map/reduce_scatter | solution.py:128
  212.8 8.4 %copy-start.8 = (bf16[512,512]{1,0:T(8,128)(2,1)S(1)}, bf16[512,512]{1,0:T(8,128)(2,1)}, u32[]{:S(2)}) copy-start(bf16[512,512]{1,0:T(8,128)(2,1)} %copy-done.7) | copy-start | bytes 1572868
  212.8 8.4 %copy-start.21 = (bf16[227,512]{1,0:T(8,128)(2,1)S(1)}, bf16[227,512]{1,0:T(8,128)(2,1)}, u32[]{:S(2)}) copy-start(bf16[227,512]{1,0:T(8,128)(2,1)} %param.47) | copy-start | bytes 697348
  212.8 584.7 %reduce-scatter.24.cloned.1.call-start = ((), (), s32[]{:S(2)}) async-start(), calls=%async_computation.18 | async-start | bytes 2228224 | tf_op jit(solution)/shard_map/reduce_scatter | solution.py:128
  (22 other events, 49.7 us)
Sparse Core Ops, SparseCore 0:
  141.2 17.4 reduce-scatter.17
  187.1 53.4 reduce-scatter.35
  245.2 54.7 reduce-scatter.37
  304.0 54.8 reduce-scatter.33
  363.3 56.3 reduce-scatter.29
  423.8 56.3 reduce-scatter.25
  484.8 56.4 reduce-scatter.19
  545.5 56.4 reduce-scatter.21
  606.8 60.4 reduce-scatter.31
  671.5 60.5 reduce-scatter.27
  736.9 60.5 reduce-scatter.23
where the time goes:
time: 805 us; the launch traced here: 804 us
  waiting for transfers between devices  613 us (76%)
  matrix products  54.9 us (7%)
  other arithmetic  43.9 us (5%)
  local copies, waits for them, and re-layouts  36.2 us (4%)
  starting transfers between devices  26 us (3%)
  between operations  15.1 us (2%)
  blocking collectives  15 us (2%)
    reduce_scatter x7, waiting for transfers between devices, reduce_whole(): lax.psum_scatter(flatten_rows(grads), ('grid', 'mesh'), scatter_dimension...  439 us
    unnamed x14, waiting for transfers between devices  136 us
    dot_general x21, matrix products, product(): return core(left, right)  40.4 us
    reduce_scatter x1, waiting for transfers between devices, on_device(): lax.psum_scatter(grad_table.astype(jnp.bfloat16), 'grid', scatter_dimensi...  17.6 us
  transfers between devices with their start and end apart: 18, of which 16 were waited for; matrix products, arithmetic and copies ran while one was open for 6% of the time, Pallas kernels for 0%

commit v1 on v0

v1 whole, which is shorter than its diff:
```python
import jax
import jax.numpy as jnp
from jax import lax
from jax.sharding import PartitionSpec as P

G_DEV = 512
MESH_DEV = 64
LOW = jnp.bfloat16
TILE = ("grid", "mesh")


def mm(left, right, over_left=1, over_right=0):
    return lax.dot_general(
        left,
        right,
        (((over_left,), (over_right,)), ((), ())),
        preferred_element_type=jnp.float32,
    )


def low(values):
    return values.astype(LOW)


def wide(values):
    return values.astype(jnp.float32)


def hot(targets, count):
    return low(targets[:, None] == lax.broadcasted_iota(jnp.int32, (1, count), 1))


def hot_columns(targets, count):
    return low(targets[None, :] == lax.broadcasted_iota(jnp.int32, (count, 1), 0))


def silu_both(value):
    gate = 1.0 / (1.0 + jnp.exp(-value))
    return low(value * gate), gate * (1.0 + value * (1.0 - gate))


def route(values):
    return lax.all_to_all(values, TILE, split_axis=0, concat_axis=0, tiled=True)


def exchange(to_next, to_previous):
    count = lax.axis_size("mesh")
    forward = [(i, i + 1) for i in range(count - 1)]
    backward = [(i + 1, i) for i in range(count - 1)]
    from_previous = lax.ppermute(to_next, "mesh", forward)
    from_next = lax.ppermute(to_previous, "mesh", backward)
    return from_previous, from_next


def reduce_group(grads):
    padded = []
    for grad in grads:
        extra = -grad.shape[1] % 128
        padded.append(jnp.pad(low(grad), ((0, 0), (0, extra))) if extra else low(grad))
    whole = jnp.concatenate(padded, axis=1)
    part = lax.psum_scatter(whole, "grid", scatter_dimension=0, tiled=True)
    part = lax.psum_scatter(part, "mesh", scatter_dimension=0, tiled=True)
    part = wide(part)
    outs = []
    start = 0
    for grad, block in zip(grads, padded):
        outs.append(part[:, start : start + grad.shape[1]].T)
        start += block.shape[1]
    return outs


def on_device(
    grid_in,
    grid_cot,
    enc_src,
    enc_feat,
    enc_dst,
    enc_count,
    halo_up,
    halo_down,
    proc_src,
    proc_dst,
    dec_send,
    dec_row,
    dec_count,
    embed_first,
    embed_second,
    edge_weight,
    feature_weight,
    layer_edge_in,
    layer_edge_out,
    layer_node_in,
    layer_node_out,
    out_first,
    out_second,
):
    width = embed_second.shape[0]
    halo = halo_up.shape[0]
    capacity = enc_src.shape[1]
    dec_capacity = dec_send.shape[1]
    n_grid = lax.axis_size("grid")
    part = MESH_DEV * n_grid
    span = part + 2 * halo
    edge_in, edge_out = layer_edge_in[0], layer_edge_out[0]
    node_in, node_out = layer_node_in[0], layer_node_out[0]
    edge_in_send, edge_in_own = edge_in[:width], edge_in[width:]
    out_grid, out_mesh = out_first[:width], out_first[width:]

    pre_embed = mm(grid_in, embed_first, 0, 0)
    hid_embed, slope_embed = silu_both(pre_embed)
    grid_latent = low(mm(hid_embed, embed_second))

    send_hot = hot(enc_src.reshape(-1), G_DEV)
    rows = low(mm(send_hot, grid_latent))
    msg, slope_msg = silu_both(mm(rows, edge_weight) + mm(enc_feat, feature_weight, 0, 0))
    received = route(msg)

    enc_valid = jnp.arange(capacity, dtype=jnp.int32)[None, :] < enc_count[:, None]
    enc_hot = hot_columns(jnp.where(enc_valid, enc_dst, -1).reshape(-1), MESH_DEV)
    total = mm(enc_hot, received)
    scale = lax.rsqrt(jnp.mean(total * total, axis=-1, keepdims=True) + 1e-05)
    latent = low(total * scale)

    table = lax.all_gather(latent, "grid", axis=0, tiled=True)
    up_hot, down_hot = hot(halo_up, part), hot(halo_down, part)
    below, above = exchange(low(mm(up_hot, table)), low(mm(down_hot, table)))
    extended = jnp.concatenate([below, table, above], axis=0)

    mapped = low(
        jnp.concatenate([mm(extended, edge_in_send), mm(latent, edge_in_own)], axis=0)
    )
    places = lax.broadcasted_iota(jnp.int32, (1, span + MESH_DEV), 1)
    edge_hot = low(
        (proc_src[:, None] == places) | ((proc_dst + span)[:, None] == places)
    )
    own_hot = hot(proc_dst, MESH_DEV)
    hid_edge, slope_edge = silu_both(mm(edge_hot, mapped))
    hid_sum = low(mm(own_hot, hid_edge, 0, 0))
    edge_sum = low(mm(hid_sum, edge_out))
    joined = jnp.concatenate([latent, edge_sum], axis=1)
    hid_node, slope_node = silu_both(mm(joined, node_in))
    final = low(wide(latent) + mm(hid_node, node_out))

    pick_hot = hot(dec_send.reshape(-1), MESH_DEV)
    arrived = route(low(mm(pick_hot, final)))

    dec_valid = jnp.arange(dec_capacity, dtype=jnp.int32)[None, :] < dec_count[:, None]
    dec_hot = hot_columns(jnp.where(dec_valid, dec_row, -1).reshape(-1), G_DEV)
    pre_out = mm(grid_latent, out_grid) + mm(dec_hot, low(mm(arrived, out_mesh)))
    hid_out, slope_out = silu_both(pre_out)
    delta = low(mm(out_second, hid_out, 1, 1))

    g_out = low(wide(low(mm(grid_cot, out_second, 0, 0))) * slope_out)
    g_out_mesh = low(mm(dec_hot, g_out, 0, 0))
    g_sent = route(low(mm(g_out_mesh, out_mesh, 1, 1)))
    g_final = low(mm(pick_hot, g_sent, 0, 0))
    g_node = low(wide(low(mm(g_final, node_out, 1, 1))) * slope_node)
    g_joined = mm(g_node, node_in, 1, 1)
    g_own = wide(g_final) + g_joined[:, :width]
    g_sum = low(g_joined[:, width:])
    g_hid = low(mm(g_sum, edge_out, 1, 1))
    g_edge = low(mm(own_hot, g_hid) * slope_edge)
    g_mapped = low(mm(edge_hot, g_edge, 0, 0))
    g_send_map, g_own_map = g_mapped[:span], g_mapped[span:]
    g_extended = mm(g_send_map, edge_in_send, 1, 1)

    to_down, to_up = exchange(
        low(g_extended[halo + part :]), low(g_extended[:halo])
    )
    g_table = (
        g_extended[halo : halo + part]
        + mm(down_hot, to_down, 0, 0)
        + mm(up_hot, to_up, 0, 0)
    )
    shares = lax.all_to_all(low(g_table), "grid", split_axis=0, concat_axis=0, tiled=True)
    g_latent = (
        g_own
        + mm(g_own_map, edge_in_own, 1, 1)
        + jnp.sum(wide(shares).reshape(n_grid, MESH_DEV, width), axis=0)
    )
    g_latent = wide(low(g_latent))
    normal = total * scale
    g_total = low(
        scale * (g_latent - normal * jnp.mean(g_latent * normal, axis=-1, keepdims=True))
    )
    g_msg = route(low(mm(enc_hot, g_total, 0, 0)))

    early = reduce_group(
        (
            jnp.concatenate(
                [mm(g_send_map, extended, 0, 0), mm(g_own_map, latent, 0, 0)], axis=1
            ),
            mm(g_sum, hid_sum, 0, 0),
            mm(g_node, joined, 0, 0),
            mm(g_final, hid_node, 0, 0),
            jnp.concatenate(
                [mm(g_out, grid_latent, 0, 0), mm(g_out_mesh, arrived, 0, 0)], axis=1
            ),
            mm(hid_out, grid_cot, 0, 1),
        )
    )

    g_pre = low(wide(g_msg) * slope_msg)
    g_rows = low(mm(g_pre, edge_weight, 1, 1))
    g_grid = low(mm(g_out, out_grid, 1, 1) + mm(send_hot, g_rows, 0, 0))
    g_embed = low(wide(low(mm(g_grid, embed_second, 1, 1))) * slope_embed)
    late = reduce_group(
        (
            mm(g_embed, grid_in, 0, 1),
            mm(g_grid, hid_embed, 0, 0),
            mm(g_pre, rows, 0, 0),
            mm(g_pre, enc_feat, 0, 1),
        )
    )
    layer = [grad[None] for grad in early[:4]]
    return (delta,) + tuple(late) + tuple(layer) + tuple(early[4:])


def solution(mesh):
    return jax.shard_map(
        on_device,
        mesh=mesh,
        in_specs=(
            P(None, ("groups", "grid", "mesh")),
            P(None, ("groups", "grid", "mesh")),
            P(("grid", "mesh"), None),
            P(None, ("grid", "mesh")),
            P(("grid", "mesh"), None),
            P(("grid", "mesh")),
            P("mesh"),
            P("mesh"),
            P(("grid", "mesh")),
            P(("grid", "mesh")),
            P(("grid", "mesh"), None),
            P(("grid", "mesh"), None),
            P(("grid", "mesh")),
            P(),
            P(),
            P(),
            P(),
            P(),
            P(),
            P(),
            P(),
            P(),
            P(),
        ),
        out_specs=(
            P(None, ("groups", "grid", "mesh")),
            P("groups", ("grid", "mesh")),
            P("groups", ("grid", "mesh")),
            P("groups", ("grid", "mesh")),
            P("groups", ("grid", "mesh")),
            P("groups", None, ("grid", "mesh")),
            P("groups", None, ("grid", "mesh")),
            P("groups", None, ("grid", "mesh")),
            P("groups", None, ("grid", "mesh")),
            P("groups", ("grid", "mesh")),
            P("groups", ("grid", "mesh")),
        ),
        check_vma=False,
    )
```

time: 805 us -> 270 us (0.34)
  waiting for transfers between devices: 613 us -> 127 us
  other arithmetic: 43.9 us -> 2.24 us
  local copies, waits for them, and re-layouts: 36.2 us -> 22.7 us
  blocking collectives: 15 us -> 25 us
    reduce_scatter x8 -> x2, waiting for transfers between devices: 456 us -> 73.4 us  [the longest x1 48.9 us: reduce_group(): part = lax.psum_scatter(whole, 'grid', scatter_dimension=0, tiled=True)]
    unnamed x14 -> x6, waiting for transfers between devices: 136 us -> 30.5 us
    scatter-add x6 -> x0, other arithmetic: 34.1 us -> none  [the longest x1 13.8 us: process_layer(): jnp.take(latent, targets, axis=0)]
    gather x7 -> x0, local copies, waits for them, and re-layouts: 19.9 us -> none  [the longest x1 9.21 us: process_layer(): jnp.take(extended, senders, axis=0)]
    all_to_all x1 -> x2, blocking collectives: 9.19 us -> 19.2 us  [the longest x1 10.8 us: route(): return lax.all_to_all(values, TILE, split_axis=0, concat_axis=0, tiled=True)]
    dot_general x34 -> x45, matrix products: 54.9 us -> 52.8 us  [mm(): lax.dot_general(left, right, (((over_left,), (over_right,)), ((), ())), p...]
  transfers between devices with their start and end apart: 18 -> 11, of which waited for: 16 -> 11; matrix products, arithmetic and copies ran while one was open for 6% -> 10% of each run, Pallas kernels for 0% -> 0%
where the time goes in v1:
time: 270 us; the launch traced here: 269 us
  waiting for transfers between devices  127 us (47%)
  matrix products  52.8 us (20%)
  blocking collectives  25 us (9%)
  starting transfers between devices  24.3 us (9%)
  local copies, waits for them, and re-layouts  22.7 us (8%)
  between operations  14.7 us (5%)
    dot_general x45, matrix products, mm(): lax.dot_general(left, right, (((over_left,), (over_right,)), ((), ())), p...  52.8 us
    reduce_scatter x1, waiting for transfers between devices, reduce_group(): part = lax.psum_scatter(whole, 'grid', scatter_dimension=0, tiled=True)  48.9 us
    unnamed x6, waiting for transfers between devices  30.5 us
    reduce_scatter x1, waiting for transfers between devices, reduce_group(): part = lax.psum_scatter(part, 'mesh', scatter_dimension=0, tiled=True)  24.5 us
    all_to_all x3, waiting for transfers between devices, route(): return lax.all_to_all(values, TILE, split_axis=0, concat_axis=0, tiled=True)  15.1 us
    all_to_all x3, starting transfers between devices, route(): return lax.all_to_all(values, TILE, split_axis=0, concat_axis=0, tiled=True)  14.8 us
    unnamed x119, local copies, waits for them, and re-layouts  13.7 us
    all_to_all x1, blocking collectives, route(): return lax.all_to_all(values, TILE, split_axis=0, concat_axis=0, tiled=True)  10.8 us
  transfers between devices with their start and end apart: 11, of which 11 were waited for; matrix products, arithmetic and copies ran while one was open for 10% of the time, Pallas kernels for 0%

profile of v1, /device:TPU:0, one launch (start us, length us, event | category | flops | bytes accessed | tf_op | source)
XLA Modules:
  0.0 268.9 jit_solution(13268013338656990317)
XLA Ops:
  7.2 0.8 copy.79
  8.2 1.0 fusion.111
  9.2 1.5 fusion.110
  10.7 1.9 convolution_convert_fusion.6
  12.6 0.8 copy-done.4
  13.7 0.9 multiply_convert_fusion.10
  15.3 7.4 %all-to-all-start = ((bf16[16,4,512]{2,1,0:T(4,128)(2,1)}), bf16[16,4,512]{2,1,0:T(4,128)(2,1)S(1)}, u32[]{:S(2)}, u32[]{:S(2)}) async-start(bf16[16,4,512]{2,1,0:T(4,128)(2,1)} %all_to_all.36), calls=%async_computation | async-start | bytes 131072 | tf_op jit(solution)/shard_map/all_to_all | solution.py:43
  23.0 2.5 fusion.78
  25.5 3.7 %all-to-all-done = bf16[16,4,512]{2,1,0:T(4,128)(2,1)S(1)} async-done(((bf16[16,4,512]{2,1,0:T(4,128)(2,1)}), bf16[16,4,512]{2,1,0:T(4,128)(2,1)S(1)}, u32[]{:S(2)}, u32[]{:S(2)}) %all-to-all-start) | async-done | bytes 65568 | tf_op jit(solution)/shard_map/all_to_all | solution.py:43
  29.6 5.8 %all_gather.3 = bf16[256,512]{1,0:T(8,128)(2,1)S(1)} all-gather(bf16[64,512]{1,0:T(8,128)(2,1)S(1)} %multiply_convert_fusion.11), channel_id=1, replica_groups=mesh['groups'=2,'grid'=4,'mesh'=4] {'grid'}, dimensions={0}, use_global_device_ids=true | all-gather | bytes 327680 | tf_op jit(solution)/shard_map/all_gather | solution.py:124
  35.9 2.3 collective-permute-start
  38.2 1.3 collective-permute-start.1
  39.7 1.7 collective-permute-done
  41.4 4.1 %collective-permute-done.1 = bf16[128,512]{1,0:T(8,128)(2,1)S(1)} collective-permute-done((bf16[128,512]{1,0:T(8,128)(2,1)S(1)}, bf16[128,512]{1,0:T(8,128)(2,1)S(1)}, u32[]{:S(2)}, u32[]{:S(2)}) %collective-permute-start.1) | collective-permute-done | bytes 131104 | tf_op jit(solution)/shard_map/ppermute | solution.py:51
  45.5 0.8 copy-done.30
  46.8 1.9 fusion.3
  48.8 1.5 fusion.38
  51.0 1.0 fusion.44
  51.9 1.5 convolution_convert_fusion.25
  54.0 3.5 %all-to-all-start.1 = ((bf16[16,4,512]{2,1,0:T(4,128)(2,1)}), bf16[16,4,512]{2,1,0:T(4,128)(2,1)S(1)}, u32[]{:S(2)}, u32[]{:S(2)}) async-start(bf16[16,4,512]{2,1,0:T(4,128)(2,1)} %all_to_all.39), calls=%async_computation.1 | async-start | bytes 131072 | tf_op jit(solution)/shard_map/all_to_all | solution.py:43
  57.7 6.4 %all-to-all-done.1 = bf16[16,4,512]{2,1,0:T(4,128)(2,1)S(1)} async-done(((bf16[16,4,512]{2,1,0:T(4,128)(2,1)}), bf16[16,4,512]{2,1,0:T(4,128)(2,1)S(1)}, u32[]{:S(2)}, u32[]{:S(2)}) %all-to-all-start.1) | async-done | bytes 65568 | tf_op jit(solution)/shard_map/all_to_all | solution.py:43
  64.1 3.0 %multiply_convert_fusion.5 = (bf16[512,512]{1,0:T(8,128)(2,1)}, f32[512,512]{1,0:T(8,128)}) fusion(f32[512,512]{1,0:T(8,128)} %fusion.78, bf16[64,512]{1,0:T(8,128)(2,1)S(1)} %all_to_all.41, bf16[1024,512]{1,0:T(8,128)(2,1)S(1)} %copy-done.2, s32[64]{0:T(128)S(1)} %eq.62), kind=kOutput, calls=%fused_computation.89 | convolution fusion | flops 68747264 | bytes 3211776 | tf_op jit(solution)/shard_map/dot_general | solution.py:13
  67.2 2.0 fusion.25
  69.2 0.9 copy-done.6
  71.2 10.8 %all_to_all.54 = bf16[16,4,512]{2,1,0:T(4,128)(2,1)} all-to-all(bf16[16,4,512]{2,1,0:T(4,128)(2,1)} %all_to_all.42), channel_id=1, replica_groups=mesh['groups'=2,'grid'=4,'mesh'=4] {'grid','mesh'}, dimensions={0} | all-to-all | bytes 131072 | tf_op jit(solution)/shard_map/all_to_all | solution.py:43
  82.0 0.9 all_to_all.44
  83.8 1.3 fusion.41
  85.1 1.1 fusion.42
  86.3 5.0 %multiply_convert_fusion = bf16[2048,512]{1,0:T(8,128)(2,1)} fusion(f32[2048,512]{1,0:T(8,128)} %copy-done.52, bf16[1,512,512]{2,1,0:T(8,128)(2,1)} %param.41, s32[2048]{0:T(1024)S(1)} %copy-done.32, f32[64,1024]{1,0:T(8,128)} %fusion.42), kind=kOutput, calls=%fused_computation.3 | convolution fusion | flops 177373184 | bytes 6889472 | tf_op jit(solution)/shard_map/dot_general | solution.py:13
  91.3 3.9 %fusion.16 = bf16[576,512]{1,0:T(8,128)(2,1)S(1)} fusion(bf16[2048,512]{1,0:T(8,128)(2,1)} %multiply_convert_fusion, s32[2048]{0:T(1024)S(1)} %copy-done.34, s32[2048]{0:T(1024)} %param.31), kind=kOutput, calls=%fused_computation.24 | convolution fusion | flops 1211793408 | bytes 2703360 | tf_op jit(solution)/shard_map/dot_general | solution.py:13
  95.8 1.3 collective-permute-start.3
  97.1 4.6 %collective-permute-start.2 = (bf16[128,512]{1,0:T(8,128)(2,1)S(1)}, bf16[128,512]{1,0:T(8,128)(2,1)S(1)}, u32[]{:S(2)}, u32[]{:S(2)}) collective-permute-start(bf16[128,512]{1,0:T(8,128)(2,1)S(1)} %get-tuple-element.62), channel_id=1, source_target_pairs={{0,1},{1,2},{2,3},{4,5},{5,6},{6,7},{8,9},{9,10},{10,11},{12,13},{... | collective-permute-start | bytes 393224 | tf_op jit(solution)/shard_map/ppermute | solution.py:50
  101.7 1.5 collective-permute-done.3
  103.6 0.8 collective-permute-done.2
  104.8 8.4 %all_to_all.55 = bf16[4,64,512]{2,1,0:T(8,128)(2,1)S(1)} all-to-all(bf16[4,64,512]{2,1,0:T(8,128)(2,1)S(1)} %bitcast.114), channel_id=1, replica_groups=mesh['groups'=2,'grid'=4,'mesh'=4] {'grid'}, dimensions={0} | all-to-all | bytes 524288 | tf_op jit(solution)/shard_map/all_to_all | solution.py:175
  114.6 3.9 %all-to-all-start.4 = ((bf16[16,4,512]{2,1,0:T(4,128)(2,1)}), bf16[16,4,512]{2,1,0:T(4,128)(2,1)S(1)}, u32[]{:S(2)}, u32[]{:S(2)}) async-start(bf16[16,4,512]{2,1,0:T(4,128)(2,1)} %all_to_all.47), calls=%async_computation.4 | async-start | bytes 131072 | tf_op jit(solution)/shard_map/all_to_all | solution.py:43
  118.5 1.5 fusion.76
  120.1 5.1 %all-to-all-done.4 = bf16[16,4,512]{2,1,0:T(4,128)(2,1)S(1)} async-done(((bf16[16,4,512]{2,1,0:T(4,128)(2,1)}), bf16[16,4,512]{2,1,0:T(4,128)(2,1)S(1)}, u32[]{:S(2)}, u32[]{:S(2)}) %all-to-all-start.4) | async-done | bytes 65568 | tf_op jit(solution)/shard_map/all_to_all | solution.py:43
  125.1 1.0 multiply_convert_fusion.7
  126.2 1.6 fusion.19
  127.9 3.0 %fusion.32 = bf16[512,227]{0,1:T(8,128)(2,1)} fusion(bf16[227,512]{1,0:T(8,128)(2,1)} %param.23, bf16[512,512]{1,0:T(8,128)(2,1)S(1)} %fusion.19, bf16[512,512]{1,0:T(8,128)(2,1)} %param.37, f32[512,512]{1,0:T(8,128)} %copy-done.8), kind=kOutput, calls=%fused_computation.51 | convolution fusion | flops 390448640 | bytes 2562048 | tf_op jit(solution)/shard_map/dot_general | solution.py:13
  132.2 1.6 copy.93
  134.3 1.7 convolution_convert_fusion.2
  136.2 1.2 convolution_convert_fusion.10
  137.6 1.2 convolution_convert_fusion.11
  138.8 1.0 copy.84
  139.8 0.9 constant_dynamic-update-slice_fusion.5
  140.7 1.9 constant_dynamic-update-slice_fusion.4
  142.7 0.9 constant_dynamic-update-slice_fusion.3
  143.5 2.3 fusion.12
  145.8 1.1 fusion.28
  147.0 1.4 fusion.22
  148.3 1.3 fusion.27
  149.6 0.8 pad_dynamic-update-slice_fusion
  150.5 8.7 %reduce-scatter.13.cloned.1.call-done = bf16[128,1408]{1,0:T(8,128)(2,1)} async-done(((bf16[512,1408]{1,0:T(8,128)(2,1)}), bf16[128,1408]{1,0:T(8,128)(2,1)}) %reduce-scatter.13.cloned.1.call-update) | async-done | bytes 360464
  159.2 48.9 %reduce-scatter.9.cloned.1.call-done = bf16[128,4352]{1,0:T(8,128)(2,1)} async-done(((bf16[512,4352]{1,0:T(8,128)(2,1)}), bf16[128,4352]{1,0:T(8,128)(2,1)}) %reduce-scatter.9.cloned.1.call-update) | async-done | bytes 1114128 | tf_op jit(solution)/shard_map/reduce_scatter | solution.py:61
  208.1 1.0 fusion.33
  209.2 21.7 %reduce-scatter.15.cloned.1.call-done = bf16[32,1408]{1,0:T(8,128)(2,1)} async-done(((bf16[128,1408]{1,0:T(8,128)(2,1)}), bf16[32,1408]{1,0:T(8,128)(2,1)}) %reduce-scatter.15.cloned.1.call-update) | async-done | bytes 90128
  230.9 1.1 copy.96
  232.8 0.7 copy.89
  233.5 0.7 copy.88
  234.9 24.5 %reduce-scatter.11.cloned.1.call-done = bf16[32,4352]{1,0:T(8,128)(2,1)} async-done(((bf16[128,4352]{1,0:T(8,128)(2,1)}), bf16[32,4352]{1,0:T(8,128)(2,1)}) %reduce-scatter.11.cloned.1.call-update) | async-done | bytes 278544 | tf_op jit(solution)/shard_map/reduce_scatter | solution.py:62
  259.4 1.0 convert_element_type.239
  261.6 0.8 slice_bitcast_fusion.2
  (166 shorter events, 14.2 us)
Async XLA Ops:
  7.2 43.8 %copy-start = (bf16[1,1024,512]{2,1,0:T(8,128)(2,1)S(1)}, bf16[1,1024,512]{2,1,0:T(8,128)(2,1)}, u32[]{:S(2)}) copy-start(bf16[1,1024,512]{2,1,0:T(8,128)(2,1)} %param.42) | copy-start | bytes 3145732
  8.1 4.5 %copy-start.39 = (s32[64]{0:T(128)}, s32[64]{0:T(128)S(1)}, u32[]{:S(2)}) copy-start(s32[64]{0:T(128)S(1)} %eq.137) | copy-start | bytes 772
  8.1 5.6 %copy-start.15 = (bf16[512,512]{1,0:T(8,128)(2,1)S(1)}, bf16[512,512]{1,0:T(8,128)(2,1)}, u32[]{:S(2)}) copy-start(bf16[512,512]{1,0:T(8,128)(2,1)} %param.38) | copy-start | bytes 1572868
  9.1 13.5 %copy-start.45 = (s32[16,4]{0,1:T(4,128)S(1)}, s32[16,4]{0,1:T(4,128)}, u32[]{:S(2)}) copy-start(s32[16,4]{0,1:T(4,128)} %param.27) | copy-start | bytes 772
  9.1 13.5 %copy-start.49 = (s32[16]{0:T(128)S(1)}, s32[16]{0:T(128)}, u32[]{:S(2)}) copy-start(s32[16]{0:T(128)} %param.28) | copy-start | bytes 196
  9.1 13.7 %copy-start.44 = (s32[16,4]{0,1:T(4,128)S(1)}, s32[16,4]{0,1:T(4,128)}, u32[]{:S(2)}) copy-start(s32[16,4]{0,1:T(4,128)} %param.33) | copy-start | bytes 772
  9.2 13.9 %copy-start.2 = (bf16[1024,512]{1,0:T(8,128)(2,1)S(1)}, bf16[1024,512]{1,0:T(8,128)(2,1)}, u32[]{:S(2)}) copy-start(bf16[1024,512]{1,0:T(8,128)(2,1)} %param.44) | copy-start | bytes 3145732
  10.6 3.0 %copy-start.8 = (f32[512,512]{1,0:T(8,128)}, f32[512,512]{1,0:T(8,128)S(1)}, u32[]{:S(2)}) copy-start(f32[512,512]{1,0:T(8,128)S(1)} %fusion.110) | copy-start | bytes 3145732
  10.7 14.9 %copy-start.31 = (s32[2048]{0:T(1024)S(1)}, s32[2048]{0:T(1024)}, u32[]{:S(2)}) copy-start(s32[2048]{0:T(1024)} %param.32) | copy-start | bytes 24580
  10.7 24.8 %copy-start.42 = (s32[128]{0:T(128)S(1)}, s32[128]{0:T(128)}, u32[]{:S(2)}) copy-start(s32[128]{0:T(128)} %param.30) | copy-start | bytes 1540
  10.7 25.0 %copy-start.47 = (s32[128]{0:T(128)S(1)}, s32[128]{0:T(128)}, u32[]{:S(2)}) copy-start(s32[128]{0:T(128)} %param.29) | copy-start | bytes 1540
  12.6 0.8 copy-start.4
  13.4 26.0 %copy-start.1 = (bf16[1,1024,512]{2,1,0:T(8,128)(2,1)S(1)}, bf16[1,1024,512]{2,1,0:T(8,128)(2,1)}, u32[]{:S(2)}) copy-start(bf16[1,1024,512]{2,1,0:T(8,128)(2,1)} %param.40) | copy-start | bytes 3145732
  13.7 11.8 %copy-start.19 = (bf16[64,512]{1,0:T(8,128)(2,1)}, bf16[64,512]{1,0:T(8,128)(2,1)S(1)}, u32[]{:S(2)}) copy-start(bf16[64,512]{1,0:T(8,128)(2,1)S(1)} %convolution_convert_fusion.28) | copy-start | bytes 196612
  13.7 33.1 %copy-start.51 = (s32[2048]{0:T(1024)S(1)}, s32[2048]{0:T(1024)}, u32[]{:S(2)}) copy-start(s32[2048]{0:T(1024)} %param.31) | copy-start | bytes 24580
  15.3 14.0 %all-to-all-start = ((bf16[16,4,512]{2,1,0:T(4,128)(2,1)}), bf16[16,4,512]{2,1,0:T(4,128)(2,1)S(1)}, u32[]{:S(2)}, u32[]{:S(2)}) async-start(bf16[16,4,512]{2,1,0:T(4,128)(2,1)} %all_to_all.36), calls=%async_computation | async-start | bytes 131072 | tf_op jit(solution)/shard_map/all_to_all | solution.py:43
  22.8 6.7 %copy-start.37 = (s32[64]{0:T(128)}, s32[64]{0:T(128)S(1)}, u32[]{:S(2)}) copy-start(s32[64]{0:T(128)S(1)} %eq.133) | copy-start | bytes 772
  25.5 21.2 %copy-start.33 = (s32[2048]{0:T(1024)}, s32[2048]{0:T(1024)S(1)}, u32[]{:S(2)}) copy-start(s32[2048]{0:T(1024)S(1)} %broadcast_add_fusion) | copy-start | bytes 24580
  29.5 17.2 %copy-start.35 = (f32[64]{0:T(128)}, f32[64]{0:T(128)S(1)}, u32[]{:S(2)}) copy-start(f32[64]{0:T(128)S(1)} %add_rsqrt_fusion) | copy-start | bytes 772
  35.9 5.5 %collective-permute-start = (bf16[128,512]{1,0:T(8,128)(2,1)S(1)}, bf16[128,512]{1,0:T(8,128)(2,1)S(1)}, u32[]{:S(2)}, u32[]{:S(2)}) collective-permute-start(bf16[128,512]{1,0:T(8,128)(2,1)S(1)} %convolution_convert_fusion.16), channel_id=1, source_target_pairs={{0,1},{1,2},{2,3},{4,5},{5,6},{6,7},{8,9},{9,10},{10,11},{12,13},{... | collective-permute-start | bytes 393224 | tf_op jit(solution)/shard_map/ppermute | solution.py:50
  38.2 7.4 %collective-permute-start.1 = (bf16[128,512]{1,0:T(8,128)(2,1)S(1)}, bf16[128,512]{1,0:T(8,128)(2,1)S(1)}, u32[]{:S(2)}, u32[]{:S(2)}) collective-permute-start(bf16[128,512]{1,0:T(8,128)(2,1)S(1)} %convolution_convert_fusion.15), channel_id=1, source_target_pairs={{1,0},{2,1},{3,2},{5,4},{6,5},{7,6},{9,8},{10,9},{11,10},{13,12},{... | collective-permute-start | bytes 393224 | tf_op jit(solution)/shard_map/ppermute | solution.py:51
  45.5 0.8 copy-start.30
  48.7 2.0 copy-start.52
  48.7 2.0 copy-start.16
  48.8 8.8 %copy-start.46 = (s32[16,4]{0,1:T(4,128)S(1)}, s32[16,4]{0,1:T(4,128)}, u32[]{:S(2)}) copy-start(s32[16,4]{0,1:T(4,128)} %param.34) | copy-start | bytes 772
  48.8 8.8 %copy-start.50 = (s32[16]{0:T(128)S(1)}, s32[16]{0:T(128)}, u32[]{:S(2)}) copy-start(s32[16]{0:T(128)} %param.35) | copy-start | bytes 196
  50.7 7.0 %copy-start.21 = (bf16[64,512]{1,0:T(8,128)(2,1)}, bf16[64,512]{1,0:T(8,128)(2,1)S(1)}, u32[]{:S(2)}) copy-start(bf16[64,512]{1,0:T(8,128)(2,1)S(1)} %fusion.38) | copy-start | bytes 196612
  54.0 10.1 %all-to-all-start.1 = ((bf16[16,4,512]{2,1,0:T(4,128)(2,1)}), bf16[16,4,512]{2,1,0:T(4,128)(2,1)S(1)}, u32[]{:S(2)}, u32[]{:S(2)}) async-start(bf16[16,4,512]{2,1,0:T(4,128)(2,1)} %all_to_all.39), calls=%async_computation.1 | async-start | bytes 131072 | tf_op jit(solution)/shard_map/all_to_all | solution.py:43
  64.1 3.0 %copy-start.17 = (bf16[64,512]{1,0:T(8,128)(2,1)}, bf16[64,512]{1,0:T(8,128)(2,1)S(1)}, u32[]{:S(2)}) copy-start(bf16[64,512]{1,0:T(8,128)(2,1)S(1)} %all_to_all.41) | copy-start | bytes 196612
  67.2 19.1 %copy-start.32 = (s32[2048]{0:T(1024)S(1)}, s32[2048]{0:T(1024)}, u32[]{:S(2)}) copy-start(s32[2048]{0:T(1024)} %param.32) | copy-start | bytes 24580
  69.2 0.9 copy-start.6
  70.3 21.0 %copy-start.13 = (bf16[64,512]{1,0:T(8,128)(2,1)}, bf16[64,512]{1,0:T(8,128)(2,1)S(1)}, u32[]{:S(2)}) copy-start(bf16[64,512]{1,0:T(8,128)(2,1)S(1)} %convolution_convert_fusion.23) | copy-start | bytes 196612
  83.1 0.6 copy-start.23
  85.1 6.2 %copy-start.22 = (bf16[64,512]{1,0:T(8,128)(2,1)}, bf16[64,512]{1,0:T(8,128)(2,1)S(1)}, u32[]{:S(2)}) copy-start(bf16[64,512]{1,0:T(8,128)(2,1)S(1)} %fusion.41) | copy-start | bytes 196612
  86.3 5.0 %copy-start.34 = (s32[2048]{0:T(1024)S(1)}, s32[2048]{0:T(1024)}, u32[]{:S(2)}) copy-start(s32[2048]{0:T(1024)} %copy-done.33) | copy-start | bytes 24580
  91.3 12.0 %copy-start.48 = (s32[128]{0:T(128)S(1)}, s32[128]{0:T(128)}, u32[]{:S(2)}) copy-start(s32[128]{0:T(128)} %param.29) | copy-start | bytes 1540
  91.3 13.1 %copy-start.43 = (s32[128]{0:T(128)S(1)}, s32[128]{0:T(128)}, u32[]{:S(2)}) copy-start(s32[128]{0:T(128)} %param.30) | copy-start | bytes 1540
  95.3 18.4 %copy-start.12 = (bf16[576,512]{1,0:T(8,128)(2,1)}, bf16[576,512]{1,0:T(8,128)(2,1)S(1)}, u32[]{:S(2)}) copy-start(bf16[576,512]{1,0:T(8,128)(2,1)S(1)} %fusion.16) | copy-start | bytes 1769476
  95.3 18.0 %copy-start.10 = (f32[64,1024]{1,0:T(8,128)S(1)}, f32[64,1024]{1,0:T(8,128)}, u32[]{:S(2)}) copy-start(f32[64,1024]{1,0:T(8,128)} %fusion.42) | copy-start | bytes 786436
  95.3 18.0 %copy-start.24 = (bf16[64,512]{1,0:T(8,128)(2,1)S(1)}, bf16[64,512]{1,0:T(8,128)(2,1)}, u32[]{:S(2)}) copy-start(bf16[64,512]{1,0:T(8,128)(2,1)} %copy-done.23) | copy-start | bytes 196612
  95.3 18.0 %copy-start.36 = (f32[64]{0:T(128)S(1)}, f32[64]{0:T(128)}, u32[]{:S(2)}) copy-start(f32[64]{0:T(128)} %copy-done.35) | copy-start | bytes 772
  95.3 18.4 %copy-start.38 = (s32[64]{0:T(128)S(1)}, s32[64]{0:T(128)}, u32[]{:S(2)}) copy-start(s32[64]{0:T(128)} %copy-done.37) | copy-start | bytes 772
  95.8 30.3 %copy-start.41 = (bf16[4,64]{1,0:T(4,128)(2,1)S(1)}, bf16[4,64]{1,0:T(4,128)(2,1)}, u32[]{:S(2)}) copy-start(bf16[4,64]{1,0:T(4,128)(2,1)} %param.26) | copy-start | bytes 1540
  95.8 30.4 %copy-start.40 = (s32[64]{0:T(128)S(1)}, s32[64]{0:T(128)}, u32[]{:S(2)}) copy-start(s32[64]{0:T(128)} %copy-done.39) | copy-start | bytes 772
  95.8 7.4 %collective-permute-start.3 = (bf16[128,512]{1,0:T(8,128)(2,1)S(1)}, bf16[128,512]{1,0:T(8,128)(2,1)S(1)}, u32[]{:S(2)}, u32[]{:S(2)}) collective-permute-start(bf16[128,512]{1,0:T(8,128)(2,1)S(1)} %get-tuple-element.63), channel_id=1, source_target_pairs={{1,0},{2,1},{3,2},{5,4},{6,5},{7,6},{9,8},{10,9},{11,10},{13,12},{... | collective-permute-start | bytes 393224 | tf_op jit(solution)/shard_map/ppermute | solution.py:51
  97.1 7.3 %collective-permute-start.2 = (bf16[128,512]{1,0:T(8,128)(2,1)S(1)}, bf16[128,512]{1,0:T(8,128)(2,1)S(1)}, u32[]{:S(2)}, u32[]{:S(2)}) collective-permute-start(bf16[128,512]{1,0:T(8,128)(2,1)S(1)} %get-tuple-element.62), channel_id=1, source_target_pairs={{0,1},{1,2},{2,3},{4,5},{5,6},{6,7},{8,9},{9,10},{10,11},{12,13},{... | collective-permute-start | bytes 393224 | tf_op jit(solution)/shard_map/ppermute | solution.py:50
  114.6 10.6 %all-to-all-start.4 = ((bf16[16,4,512]{2,1,0:T(4,128)(2,1)}), bf16[16,4,512]{2,1,0:T(4,128)(2,1)S(1)}, u32[]{:S(2)}, u32[]{:S(2)}) async-start(bf16[16,4,512]{2,1,0:T(4,128)(2,1)} %all_to_all.47), calls=%async_computation.4 | async-start | bytes 131072 | tf_op jit(solution)/shard_map/all_to_all | solution.py:43
  118.5 40.7 %reduce-scatter.13.cloned.1.call-start = ((), (), s32[]{:S(2)}) async-start(), calls=%async_computation.11 | async-start | bytes 1802240
  127.9 3.1 %copy-start.9 = (f32[512,512]{1,0:T(8,128)S(1)}, f32[512,512]{1,0:T(8,128)}, u32[]{:S(2)}) copy-start(f32[512,512]{1,0:T(8,128)} %copy-done.8) | copy-start | bytes 3145732
  130.9 0.8 copy-start.20
  130.9 1.2 copy-start.28
  131.8 2.1 copy-start.3
  131.8 2.1 copy-start.26
  133.8 2.4 copy-start.11
  133.8 74.3 %reduce-scatter.9.cloned.1.call-start = ((), (), s32[]{:S(2)}) async-start(), calls=%async_computation.9 | async-start | bytes 5570560 | tf_op jit(solution)/shard_map/reduce_scatter | solution.py:61
  139.8 6.0 %copy-start.25 = (bf16[64,512]{1,0:T(8,128)(2,1)S(1)}, bf16[64,512]{1,0:T(8,128)(2,1)}, u32[]{:S(2)}) copy-start(bf16[64,512]{1,0:T(8,128)(2,1)} %copy-done.23) | copy-start | bytes 196612
  139.8 6.0 %copy-start.29 = (f32[64,512]{1,0:T(8,128)S(1)}, f32[64,512]{1,0:T(8,128)}, u32[]{:S(2)}) copy-start(f32[64,512]{1,0:T(8,128)} %fusion.44) | copy-start | bytes 393220
  139.8 7.1 %copy-start.5 = (bf16[512,512]{1,0:T(8,128)(2,1)S(1)}, bf16[512,512]{1,0:T(8,128)(2,1)}, u32[]{:S(2)}) copy-start(bf16[512,512]{1,0:T(8,128)(2,1)} %copy-done.4) | copy-start | bytes 1572868
  139.8 7.1 %copy-start.7 = (bf16[512,512]{1,0:T(8,128)(2,1)S(1)}, bf16[512,512]{1,0:T(8,128)(2,1)}, u32[]{:S(2)}) copy-start(bf16[512,512]{1,0:T(8,128)(2,1)} %copy-done.6) | copy-start | bytes 1572868
  139.8 8.5 %copy-start.14 = (bf16[64,512]{1,0:T(8,128)(2,1)S(1)}, bf16[64,512]{1,0:T(8,128)(2,1)}, u32[]{:S(2)}) copy-start(bf16[64,512]{1,0:T(8,128)(2,1)} %copy-done.13) | copy-start | bytes 196612
  139.8 8.5 %copy-start.18 = (bf16[64,512]{1,0:T(8,128)(2,1)S(1)}, bf16[64,512]{1,0:T(8,128)(2,1)}, u32[]{:S(2)}) copy-start(bf16[64,512]{1,0:T(8,128)(2,1)} %copy-done.17) | copy-start | bytes 196612
  146.9 61.2 %copy-start.27 = (bf16[227,512]{1,0:T(8,128)(2,1)S(1)}, bf16[227,512]{1,0:T(8,128)(2,1)}, u32[]{:S(2)}) copy-start(bf16[227,512]{1,0:T(8,128)(2,1)} %param.45) | copy-start | bytes 697348
  150.4 80.5 %reduce-scatter.15.cloned.1.call-start = ((), (), s32[]{:S(2)}) async-start(), calls=%async_computation.12 | async-start | bytes 450560
  159.2 100.2 %reduce-scatter.11.cloned.1.call-start = ((), (), s32[]{:S(2)}) async-start(), calls=%async_computation.10 | async-start | bytes 1392640 | tf_op jit(solution)/shard_map/reduce_scatter | solution.py:62
Sparse Core Ops, SparseCore 0:
  133.9 25.2 reduce-scatter.12
  161.9 46.2 reduce-scatter.8
  210.4 20.4 reduce-scatter.14
  233.1 26.2 reduce-scatter.10

commit v2 on v1

--- a/solution.py
+++ b/solution.py
@@ -1,6 +1,10 @@
+import functools
+
 import jax
 import jax.numpy as jnp
 from jax import lax
+from jax.experimental import pallas as pl
+from jax.experimental.pallas import tpu as pltpu
 from jax.sharding import PartitionSpec as P
 
 G_DEV = 512
@@ -52,21 +56,161 @@
     return from_previous, from_next
 
 
-def reduce_group(grads):
+def join_grads(grads):
     padded = []
     for grad in grads:
         extra = -grad.shape[1] % 128
         padded.append(jnp.pad(low(grad), ((0, 0), (0, extra))) if extra else low(grad))
-    whole = jnp.concatenate(padded, axis=1)
-    part = lax.psum_scatter(whole, "grid", scatter_dimension=0, tiled=True)
-    part = lax.psum_scatter(part, "mesh", scatter_dimension=0, tiled=True)
+    return jnp.concatenate(padded, axis=1)
+
+
+def split_grads(part, sizes):
     part = wide(part)
     outs = []
     start = 0
-    for grad, block in zip(grads, padded):
-        outs.append(part[:, start : start + grad.shape[1]].T)
-        start += block.shape[1]
+    for size in sizes:
+        outs.append(part[:, start : start + size].T)
+        start += size + (-size % 128)
     return outs
+
+
+def plan_of(counts, order):
+    left = dict(counts)
+    bit = {"grid": 1, "mesh": 1}
+    plan = []
+    for axis in order:
+        plan.append((axis, bit[axis], left["grid"], left["mesh"]))
+        left[axis] //= 2
+        bit[axis] *= 2
+    return plan
+
+
+def pieces_of(step, mine, rows):
+    axis, bit, grids, meshes = step
+    own = (mine[axis] // bit) % 2
+    other = 1 - own
+    pieces = []
+    if axis == "grid":
+        size = meshes * rows
+        for high in range(grids // 2):
+            pieces.append(((2 * high + own) * size, (2 * high + other) * size, high * size, size))
+    else:
+        for block in range(grids):
+            for high in range(meshes // 2):
+                base = block * meshes + 2 * high
+                target = (block * (meshes // 2) + high) * rows
+                pieces.append(((base + own) * rows, (base + other) * rows, target, rows))
+    return pieces
+
+
+def halving_kernel(counts, rows, spans, plans, x_ref, out_ref, *scratch):
+    depth = len(plans[0])
+    sums = [scratch[c * depth : (c + 1) * depth - 1] for c in range(len(spans))]
+    base = len(spans) * depth
+    lands = [scratch[base + c * depth : base + (c + 1) * depth] for c in range(len(spans))]
+    sends, arrivals = scratch[-2], scratch[-1]
+    mine = {"grid": lax.axis_index("grid"), "mesh": lax.axis_index("mesh")}
+
+    def partner(axis, bit):
+        return mine[axis] + bit * (1 - 2 * ((mine[axis] // bit) % 2))
+
+    partners = {(axis, bit) for axis, bit, _, _ in plans[0]}
+    barrier = pltpu.get_barrier_semaphore()
+    for axis, bit in sorted(partners):
+        pl.semaphore_signal(
+            barrier,
+            inc=1,
+            device_id={axis: partner(axis, bit)},
+            device_id_type=pl.DeviceIdType.MESH,
+        )
+    pl.semaphore_wait(barrier, len(partners))
+
+    started = []
+    number = 0
+    flying = {}
+
+    def source(c, s):
+        return (x_ref, spans[c][0]) if s == 0 else (sums[c][s - 1], 0)
+
+    def start(c, s):
+        nonlocal number
+        axis, bit, _, _ = plans[c][s]
+        ref, first = source(c, s)
+        copies = []
+        for _, away, target, size in pieces_of(plans[c][s], mine, rows):
+            copy = pltpu.make_async_remote_copy(
+                src_ref=ref.at[pl.ds(pl.multiple_of(away, 16), size), pl.ds(first, spans[c][1])],
+                dst_ref=lands[c][s].at[pl.ds(target, size), :],
+                send_sem=sends.at[number],
+                recv_sem=arrivals.at[number],
+                device_id={axis: partner(axis, bit)},
+                device_id_type=pl.DeviceIdType.MESH,
+            )
+            number += 1
+            copy.start()
+            copies.append(copy)
+            started.append(copy)
+        flying[c, s] = copies
+
+    def finish(c, s):
+        ref, first = source(c, s)
+        pieces = pieces_of(plans[c][s], mine, rows)
+        for copy, (keep, _, target, size) in zip(flying[c, s], pieces):
+            copy.wait_recv()
+            value = ref[pl.ds(pl.multiple_of(keep, 16), size), pl.ds(first, spans[c][1])].astype(
+                jnp.float32
+            ) + lands[c][s][pl.ds(target, size), :].astype(jnp.float32)
+            if s == depth - 1:
+                out_ref[:, pl.ds(spans[c][0], spans[c][1])] = value
+            else:
+                sums[c][s][pl.ds(target, size), :] = value.astype(LOW)
+
+    for c in range(len(spans)):
+        start(c, 0)
+    for s in range(depth):
+        for c in range(len(spans)):
+            finish(c, s)
+            if s + 1 < depth:
+                start(c, s + 1)
+    for copy in started:
+        copy.wait_send()
+
+
+def halving_scatter(whole):
+    counts = {"grid": lax.axis_size("grid"), "mesh": lax.axis_size("mesh")}
+    tiles = counts["grid"] * counts["mesh"]
+    rows = whole.shape[0] // tiles
+    if rows % 16 or counts["grid"] & (counts["grid"] - 1) or counts["mesh"] & (counts["mesh"] - 1):
+        return lax.psum_scatter(whole, TILE, scatter_dimension=0, tiled=True)
+    columns = whole.shape[1]
+    grid_steps = ["grid"] * (counts["grid"].bit_length() - 1)
+    mesh_steps = ["mesh"] * (counts["mesh"].bit_length() - 1)
+    cut = (columns * 6 // 10) // 128 * 128
+    spans = ((0, cut), (cut, columns - cut))
+    orders = (grid_steps + mesh_steps, grid_steps[:1] + mesh_steps + grid_steps[1:])
+    plans = [plan_of(counts, order) for order in orders]
+    depth = len(plans[0])
+    heights = [whole.shape[0] >> (s + 1) for s in range(depth)]
+    sums = []
+    lands = []
+    for _, size in spans:
+        sums += [pltpu.VMEM((heights[s], size), LOW) for s in range(depth)]
+        lands += [pltpu.VMEM((heights[s], size), LOW) for s in range(depth)]
+    fake = {"grid": 0, "mesh": 0}
+    total = sum(len(pieces_of(step, fake, rows)) for plan in plans for step in plan)
+    return pl.pallas_call(
+        functools.partial(halving_kernel, counts, rows, spans, plans),
+        out_shape=jax.ShapeDtypeStruct((rows, columns), jnp.float32),
+        in_specs=[pl.BlockSpec(memory_space=pltpu.VMEM)],
+        out_specs=pl.BlockSpec(memory_space=pltpu.VMEM),
+        scratch_shapes=sums
+        + lands
+        + [pltpu.SemaphoreType.DMA((total,)), pltpu.SemaphoreType.DMA((total,))],
+        compiler_params=pltpu.CompilerParams(
+            collective_id=1, has_side_effects=True, vmem_limit_bytes=24 * 2**20
+        ),
+        cost_estimate=pl.CostEstimate(flops=0, bytes_accessed=90 * 10**6, transcendentals=0),
+    )(whole)
 
 
 def on_device(
@@ -167,25 +311,7 @@
     to_down, to_up = exchange(
         low(g_extended[halo + part :]), low(g_extended[:halo])
     )
-    g_table = (
-        g_extended[halo : halo + part]
-        + mm(down_hot, to_down, 0, 0)
-        + mm(up_hot, to_up, 0, 0)
-    )
-    shares = lax.all_to_all(low(g_table), "grid", split_axis=0, concat_axis=0, tiled=True)
-    g_latent = (
-        g_own
-        + mm(g_own_map, edge_in_own, 1, 1)
-        + jnp.sum(wide(shares).reshape(n_grid, MESH_DEV, width), axis=0)
-    )
-    g_latent = wide(low(g_latent))
-    normal = total * scale
-    g_total = low(
-        scale * (g_latent - normal * jnp.mean(g_latent * normal, axis=-1, keepdims=True))
-    )
-    g_msg = route(low(mm(enc_hot, g_total, 0, 0)))
-
-    early = reduce_group(
+    early_whole = join_grads(
         (
             jnp.concatenate(
                 [mm(g_send_map, extended, 0, 0), mm(g_own_map, latent, 0, 0)], axis=1
@@ -200,17 +326,46 @@
         )
     )
 
+    to_down, to_up, early_whole = lax.optimization_barrier((to_down, to_up, early_whole))
+    early_part = lax.psum_scatter(early_whole, "grid", scatter_dimension=0, tiled=True)
+    g_table = (
+        g_extended[halo : halo + part]
+        + mm(down_hot, to_down, 0, 0)
+        + mm(up_hot, to_up, 0, 0)
+    )
+    shares = lax.all_to_all(low(g_table), "grid", split_axis=0, concat_axis=0, tiled=True)
+    g_latent = (
+        g_own
+        + mm(g_own_map, edge_in_own, 1, 1)
+        + jnp.sum(wide(shares).reshape(n_grid, MESH_DEV, width), axis=0)
+    )
+    g_latent = wide(low(g_latent))
+    normal = total * scale
+    g_total = low(
+        scale * (g_latent - normal * jnp.mean(g_latent * normal, axis=-1, keepdims=True))
+    )
+    g_msg = route(low(mm(enc_hot, g_total, 0, 0)))
+
     g_pre = low(wide(g_msg) * slope_msg)
     g_rows = low(mm(g_pre, edge_weight, 1, 1))
     g_grid = low(mm(g_out, out_grid, 1, 1) + mm(send_hot, g_rows, 0, 0))
     g_embed = low(wide(low(mm(g_grid, embed_second, 1, 1))) * slope_embed)
-    late = reduce_group(
+    late_whole = join_grads(
         (
             mm(g_embed, grid_in, 0, 1),
             mm(g_grid, hid_embed, 0, 0),
             mm(g_pre, rows, 0, 0),
             mm(g_pre, enc_feat, 0, 1),
         )
+    )
+    channels = grid_in.shape[0]
+    late_whole, early_part = lax.optimization_barrier((late_whole, early_part))
+    early_part = lax.psum_scatter(early_part, "mesh", scatter_dimension=0, tiled=True)
+    late = split_grads(
+        halving_scatter(late_whole), (channels, width, width, enc_feat.shape[0])
+    )
+    early = split_grads(
+        early_part, (2 * width, width, 2 * width, width, 2 * width, channels)
     )
     layer = [grad[None] for grad in early[:4]]
     return (delta,) + tuple(late) + tuple(layer) + tuple(early[4:])

time: 270 us -> 222 us (0.82)
  waiting for transfers between devices: 127 us -> 45.9 us
  Pallas kernels: 0 us -> 25.8 us
  blocking collectives: 25 us -> 14.3 us
  local copies, waits for them, and re-layouts: 22.7 us -> 32.2 us
  matrix products: 52.8 us -> 59.6 us
    reduce_scatter x2, waiting for transfers between devices: 73.4 us -> 18.4 us  [the longest x1 12.2 us: on_device(): lax.psum_scatter(early_whole, 'grid', scatter_dimension=0, tiled=True)]
    unnamed x6 -> x2, waiting for transfers between devices: 30.5 us -> 0.03 us
    pallas_call x0 -> x1, Pallas kernels: none -> 25.8 us  [halving_scatter(): pl.pallas_call(functools.partial(halving_kernel, counts, rows, spans, pla...]
    all_to_all x1 -> x0, blocking collectives: 10.8 us -> none  [route(): return lax.all_to_all(values, TILE, split_axis=0, concat_axis=0, tiled=True)]
    dot_general x45, matrix products: 52.8 us -> 59.6 us  [mm(): lax.dot_general(left, right, (((over_left,), (over_right,)), ((), ())), p...]
    convert_element_type x1 -> x3, local copies, waits for them, and re-layouts: 0.21 us -> 3.73 us  [low(): return values.astype(LOW)]
    all_to_all x3 -> x4, starting transfers between devices: 14.8 us -> 17.9 us  [route(): return lax.all_to_all(values, TILE, split_axis=0, concat_axis=0, tiled=True)]
    ppermute x2, waiting for transfers between devices: 5.61 us -> 8.52 us  [exchange(): from_next = lax.ppermute(to_previous, 'mesh', backward)]
  transfers between devices with their start and end apart: 11 -> 10, of which waited for: 11 -> 9; matrix products, arithmetic and copies ran while one was open for 10% -> 13% of each run, Pallas kernels for 0% -> 12%
where the time goes in v2:
time: 222 us; the launch traced here: 221 us
  matrix products  59.6 us (27%)
  waiting for transfers between devices  45.9 us (21%)
  local copies, waits for them, and re-layouts  32.2 us (15%)
  starting transfers between devices  26 us (12%)
  Pallas kernels  25.8 us (12%)
  between operations  14.8 us (7%)
  blocking collectives  14.3 us (6%)
    dot_general x45, matrix products, mm(): lax.dot_general(left, right, (((over_left,), (over_right,)), ((), ())), p...  59.6 us
    pallas_call x1, Pallas kernels, halving_scatter(): pl.pallas_call(functools.partial(halving_kernel, counts, rows, spans, pla...  25.8 us
    all_to_all x4, starting transfers between devices, route(): return lax.all_to_all(values, TILE, split_axis=0, concat_axis=0, tiled=True)  17.9 us
    all_to_all x4, waiting for transfers between devices, route(): return lax.all_to_all(values, TILE, split_axis=0, concat_axis=0, tiled=True)  17.4 us
    unnamed x109, local copies, waits for them, and re-layouts  13.7 us
    reduce_scatter x1, waiting for transfers between devices, on_device(): lax.psum_scatter(early_whole, 'grid', scatter_dimension=0, tiled=True)  12.2 us
    all_to_all x1, blocking collectives, on_device(): lax.all_to_all(low(g_table), 'grid', split_axis=0, concat_axis=0, tiled=T...  8.56 us
    ppermute x2, waiting for transfers between devices, exchange(): from_next = lax.ppermute(to_previous, 'mesh', backward)  8.52 us
  transfers between devices with their start and end apart: 10, of which 9 were waited for; matrix products, arithmetic and copies ran while one was open for 13% of the time, Pallas kernels for 12%

profile of v2, /device:TPU:0, one launch (start us, length us, event | category | flops | bytes accessed | tf_op | source)
XLA Modules:
  0.0 220.6 jit_solution(7692034030026902009)
XLA Ops:
  7.2 0.8 copy.69
  8.2 1.4 fusion.110
  9.6 1.0 copy-done.9
  10.7 1.6 convolution_convert_fusion.6
  13.7 0.9 multiply_convert_fusion.10
  15.2 7.4 %all-to-all-start = ((bf16[16,4,512]{2,1,0:T(4,128)(2,1)}), bf16[16,4,512]{2,1,0:T(4,128)(2,1)S(1)}, u32[]{:S(2)}, u32[]{:S(2)}) async-start(bf16[16,4,512]{2,1,0:T(4,128)(2,1)} %all_to_all.36), calls=%async_computation | async-start | bytes 131072 | tf_op jit(solution)/shard_map/all_to_all | solution.py:47
  23.5 2.5 %fusion.78 = f32[512,512]{1,0:T(8,128)} fusion(bf16[512,512]{1,0:T(8,128)(2,1)} %copy-done.4, bf16[1024,512]{1,0:T(8,128)(2,1)S(1)} %copy-done.2), kind=kOutput, calls=%fused_computation.120 | convolution fusion | flops 268435456 | bytes 2097152 | tf_op jit(solution)/shard_map/dot_general | solution.py:17
  26.0 3.2 %all-to-all-done = bf16[16,4,512]{2,1,0:T(4,128)(2,1)S(1)} async-done(((bf16[16,4,512]{2,1,0:T(4,128)(2,1)}), bf16[16,4,512]{2,1,0:T(4,128)(2,1)S(1)}, u32[]{:S(2)}, u32[]{:S(2)}) %all-to-all-start) | async-done | bytes 65568 | tf_op jit(solution)/shard_map/all_to_all | solution.py:47
  29.6 5.8 %all_gather.3 = bf16[256,512]{1,0:T(8,128)(2,1)S(1)} all-gather(bf16[64,512]{1,0:T(8,128)(2,1)S(1)} %multiply_convert_fusion.11), channel_id=1, replica_groups=mesh['groups'=2,'grid'=4,'mesh'=4] {'grid'}, dimensions={0}, use_global_device_ids=true | all-gather | bytes 327680 | tf_op jit(solution)/shard_map/all_gather | solution.py:268
  35.6 2.3 %collective-permute-start = (bf16[128,512]{1,0:T(8,128)(2,1)S(1)}, bf16[128,512]{1,0:T(8,128)(2,1)S(1)}, u32[]{:S(2)}, u32[]{:S(2)}) collective-permute-start(bf16[128,512]{1,0:T(8,128)(2,1)S(1)} %convolution_convert_fusion.16), channel_id=1, source_target_pairs={{0,1},{1,2},{2,3},{4,5},{5,6},{6,7},{8,9},{9,10},{10,11},{12,13},{... | collective-permute-start | bytes 393224 | tf_op jit(solution)/shard_map/ppermute | solution.py:54
  38.1 1.3 collective-permute-start.1
  39.6 1.5 collective-permute-done
  41.1 4.3 %collective-permute-done.1 = bf16[128,512]{1,0:T(8,128)(2,1)S(1)} collective-permute-done((bf16[128,512]{1,0:T(8,128)(2,1)S(1)}, bf16[128,512]{1,0:T(8,128)(2,1)S(1)}, u32[]{:S(2)}, u32[]{:S(2)}) %collective-permute-start.1) | collective-permute-done | bytes 131104 | tf_op jit(solution)/shard_map/ppermute | solution.py:55
  46.7 1.9 fusion.3
  48.7 1.5 fusion.38
  51.5 2.1 convolution_convert_fusion.25
  53.6 1.5 all_to_all.39
  55.1 3.5 %all-to-all-start.1 = ((bf16[16,4,512]{2,1,0:T(4,128)(2,1)}), bf16[16,4,512]{2,1,0:T(4,128)(2,1)S(1)}, u32[]{:S(2)}, u32[]{:S(2)}) async-start(bf16[16,4,512]{2,1,0:T(4,128)(2,1)} %all_to_all.39), calls=%async_computation.1 | async-start | bytes 131072 | tf_op jit(solution)/shard_map/all_to_all | solution.py:47
  60.0 5.2 %all-to-all-done.1 = bf16[16,4,512]{2,1,0:T(4,128)(2,1)S(1)} async-done(((bf16[16,4,512]{2,1,0:T(4,128)(2,1)}), bf16[16,4,512]{2,1,0:T(4,128)(2,1)S(1)}, u32[]{:S(2)}, u32[]{:S(2)}) %all-to-all-start.1) | async-done | bytes 65568 | tf_op jit(solution)/shard_map/all_to_all | solution.py:47
  65.2 3.0 %multiply_convert_fusion.5 = (bf16[512,512]{1,0:T(8,128)(2,1)}, f32[512,512]{1,0:T(8,128)}) fusion(f32[512,512]{1,0:T(8,128)} %fusion.78, bf16[64,512]{1,0:T(8,128)(2,1)S(1)} %all_to_all.41, bf16[1024,512]{1,0:T(8,128)(2,1)S(1)} %copy-done.2, s32[64]{0:T(128)} %eq.62), kind=kOutput, calls=%fused_computation.89 | convolution fusion | flops 68747264 | bytes 3211520 | tf_op jit(solution)/shard_map/dot_general | solution.py:17
  68.2 2.0 fusion.25
  71.3 0.9 convolution_convert_fusion.22
  72.2 1.5 all_to_all.42
  73.7 3.5 %all-to-all-start.2 = ((bf16[16,4,512]{2,1,0:T(4,128)(2,1)}), bf16[16,4,512]{2,1,0:T(4,128)(2,1)S(1)}, u32[]{:S(2)}, u32[]{:S(2)}) async-start(bf16[16,4,512]{2,1,0:T(4,128)(2,1)} %all_to_all.42), calls=%async_computation.2 | async-start | bytes 131072 | tf_op jit(solution)/shard_map/all_to_all | solution.py:47
  77.4 1.4 convolution_convert_fusion.13
  78.8 0.9 copy.87
  79.7 4.1 %all-to-all-done.2 = bf16[16,4,512]{2,1,0:T(4,128)(2,1)S(1)} async-done(((bf16[16,4,512]{2,1,0:T(4,128)(2,1)}), bf16[16,4,512]{2,1,0:T(4,128)(2,1)S(1)}, u32[]{:S(2)}, u32[]{:S(2)}) %all-to-all-start.2) | async-done | bytes 65568 | tf_op jit(solution)/shard_map/all_to_all | solution.py:47
  83.8 0.9 convolution_convert_fusion.21
  85.4 1.3 fusion.41
  87.4 5.0 %multiply_convert_fusion = bf16[2048,512]{1,0:T(8,128)(2,1)} fusion(f32[2048,512]{1,0:T(8,128)} %copy-done.49, bf16[1,512,512]{2,1,0:T(8,128)(2,1)} %param.41, s32[2048]{0:T(1024)S(1)} %copy-done.29, f32[64,1024]{1,0:T(8,128)S(1)} %fusion.42), kind=kOutput, calls=%fused_computation.3 | convolution fusion | flops 177373184 | bytes 6889472 | tf_op jit(solution)/shard_map/dot_general | solution.py:17
  92.4 4.0 %fusion.16 = bf16[576,512]{1,0:T(8,128)(2,1)S(1)} fusion(bf16[2048,512]{1,0:T(8,128)(2,1)} %multiply_convert_fusion, s32[2048]{0:T(1024)S(1)} %broadcast_add_fusion, s32[2048]{0:T(1024)S(1)} %copy-done.48), kind=kOutput, calls=%fused_computation.24 | convolution fusion | flops 1211793408 | bytes 2703360 | tf_op jit(solution)/shard_map/dot_general | solution.py:17
  96.4 1.3 convolution_convert_fusion.4
  97.7 1.1 convolution_convert_fusion.12
  98.8 1.1 convolution_convert_fusion.11
  100.0 1.3 fusion.109
  101.3 2.0 copy.73
  103.3 1.9 constant_dynamic-update-slice_fusion.5
  105.2 2.0 copy.74
  107.3 2.1 copy.75
  109.4 2.0 constant_dynamic-update-slice_fusion.4
  111.4 1.9 constant_dynamic-update-slice_fusion.3
  113.3 2.3 %fusion.12 = bf16[512,4352]{1,0:T(8,128)(2,1)} fusion(bf16[512,4352]{1,0:T(8,128)(2,1)} %constant_dynamic-update-slice_fusion.3, bf16[64,512]{1,0:T(8,128)(2,1)} %copy-done.22, bf16[64,512]{1,0:T(8,128)(2,1)S(1)} %convolution_convert_fusion.26, bf16[64,512]{1,0:T(8,128)(2,1)S(1)} %multiply_convert_fusion.11), kind=kOutput, calls=%fused_computation.18 | convolution fusion | flops 67895296 | bytes 1245184 | tf_op jit(solution)/shard_map/dot_general | solution.py:17
  115.6 2.1 fusion.28
  117.8 1.3 fusion.20
  119.8 2.9 %collective-permute-start.2 = (bf16[128,512]{1,0:T(8,128)(2,1)}, bf16[128,512]{1,0:T(8,128)(2,1)}, u32[]{:S(2)}, u32[]{:S(2)}) collective-permute-start(bf16[128,512]{1,0:T(8,128)(2,1)} %get-tuple-element.60), channel_id=1, source_target_pairs={{0,1},{1,2},{2,3},{4,5},{5,6},{6,7},{8,9},{9,10},{10,11},{12,13},{... | collective-permute-start | bytes 393224 | tf_op jit(solution)/shard_map/ppermute | solution.py:54
  122.7 1.4 collective-permute-start.3
  124.1 1.1 fusion.27
  126.1 4.2 %collective-permute-done.3 = bf16[128,512]{1,0:T(8,128)(2,1)} collective-permute-done((bf16[128,512]{1,0:T(8,128)(2,1)}, bf16[128,512]{1,0:T(8,128)(2,1)}, u32[]{:S(2)}, u32[]{:S(2)}) %collective-permute-start.3) | collective-permute-done | bytes 131104 | tf_op jit(solution)/shard_map/ppermute | solution.py:55
  130.3 1.3 fusion.80
  131.6 1.2 fusion.31
  132.9 8.6 %all_to_all.54 = bf16[4,64,512]{2,1,0:T(8,128)(2,1)S(1)} all-to-all(bf16[4,64,512]{2,1,0:T(8,128)(2,1)S(1)} %bitcast.112), channel_id=1, replica_groups=mesh['groups'=2,'grid'=4,'mesh'=4] {'grid'}, dimensions={0} | all-to-all | bytes 524288 | tf_op jit(solution)/shard_map/all_to_all | solution.py:336
  141.5 1.3 multiply_reduce_fusion
  143.7 3.5 %all-to-all-start.4 = ((bf16[16,4,512]{2,1,0:T(4,128)(2,1)}), bf16[16,4,512]{2,1,0:T(4,128)(2,1)S(1)}, u32[]{:S(2)}, u32[]{:S(2)}) async-start(bf16[16,4,512]{2,1,0:T(4,128)(2,1)} %all_to_all.47), calls=%async_computation.4 | async-start | bytes 131072 | tf_op jit(solution)/shard_map/all_to_all | solution.py:47
  147.3 1.7 fusion.76
  149.0 4.9 %all-to-all-done.4 = bf16[16,4,512]{2,1,0:T(4,128)(2,1)S(1)} async-done(((bf16[16,4,512]{2,1,0:T(4,128)(2,1)}), bf16[16,4,512]{2,1,0:T(4,128)(2,1)S(1)}, u32[]{:S(2)}, u32[]{:S(2)}) %all-to-all-start.4) | async-done | bytes 65568 | tf_op jit(solution)/shard_map/all_to_all | solution.py:47
  154.0 2.4 %fusion.19 = bf16[512,512]{1,0:T(8,128)(2,1)} fusion(f32[512,512]{1,0:T(8,128)S(1)} %fusion.76, bf16[64,512]{1,0:T(8,128)(2,1)S(1)} %multiply_convert_fusion.7, bf16[512,512]{1,0:T(8,128)(2,1)} %param.38, s32[64]{0:T(128)S(1)} %copy-done.35), kind=kOutput, calls=%fused_computation.25 | convolution fusion | flops 67698688 | bytes 2162944 | tf_op jit(solution)/shard_map/dot_general | solution.py:17
  156.5 2.2 fusion.32
  158.6 0.8 copy.77
  160.8 1.7 convolution_convert_fusion.1
  162.6 12.2 %reduce-scatter.3.cloned.1.call-done = bf16[128,4352]{1,0:T(8,128)(2,1)} async-done(((bf16[512,4352]{1,0:T(8,128)(2,1)}), bf16[128,4352]{1,0:T(8,128)(2,1)}) %reduce-scatter.3.cloned.1.call-update) | async-done | bytes 1114128 | tf_op jit(solution)/shard_map/reduce_scatter | solution.py:330
  174.8 2.0 fusion.33
  176.8 25.8 %shard_map.302 = f32[32,1408]{1,0:T(8,128)S(1)} custom-call(bf16[512,1408]{1,0:T(8,128)(2,1)S(1)} %fusion.13.x_ref), custom_call_target="tpu_custom_call" | custom-call | bytes 90000000 | tf_op jit(solution)/shard_map/pallas_call | solution.py:201
  204.5 6.2 %reduce-scatter.5.cloned.1.call-done = bf16[32,4352]{1,0:T(8,128)(2,1)} async-done(((bf16[128,4352]{1,0:T(8,128)(2,1)}), bf16[32,4352]{1,0:T(8,128)(2,1)}) %reduce-scatter.5.cloned.1.call-update) | async-done | bytes 278544 | tf_op jit(solution)/shard_map/reduce_scatter | solution.py:363
  210.8 1.0 convert_element_type.235
  (153 shorter events, 18.5 us)
Async XLA Ops:
  7.2 44.0 %copy-start = (bf16[1,1024,512]{2,1,0:T(8,128)(2,1)S(1)}, bf16[1,1024,512]{2,1,0:T(8,128)(2,1)}, u32[]{:S(2)}) copy-start(bf16[1,1024,512]{2,1,0:T(8,128)(2,1)} %param.42) | copy-start | bytes 3145732
  7.2 6.2 %copy-start.36 = (bf16[4,64]{1,0:T(4,128)(2,1)S(1)}, bf16[4,64]{1,0:T(4,128)(2,1)}, u32[]{:S(2)}) copy-start(bf16[4,64]{1,0:T(4,128)(2,1)} %param.26) | copy-start | bytes 1540
  7.2 6.2 %copy-start.38 = (bf16[4,512]{1,0:T(4,128)(2,1)S(1)}, bf16[4,512]{1,0:T(4,128)(2,1)}, u32[]{:S(2)}) copy-start(bf16[4,512]{1,0:T(4,128)(2,1)} %param.39) | copy-start | bytes 12292
  8.1 5.2 %copy-start.34 = (s32[64]{0:T(128)}, s32[64]{0:T(128)S(1)}, u32[]{:S(2)}) copy-start(s32[64]{0:T(128)S(1)} %eq.137) | copy-start | bytes 772
  8.2 5.5 %copy-start.15 = (bf16[512,512]{1,0:T(8,128)(2,1)S(1)}, bf16[512,512]{1,0:T(8,128)(2,1)}, u32[]{:S(2)}) copy-start(bf16[512,512]{1,0:T(8,128)(2,1)} %param.38) | copy-start | bytes 1572868
  9.6 1.0 copy-start.9
  10.7 11.9 %copy-start.42 = (s32[16,4]{0,1:T(4,128)S(1)}, s32[16,4]{0,1:T(4,128)}, u32[]{:S(2)}) copy-start(s32[16,4]{0,1:T(4,128)} %param.27) | copy-start | bytes 772
  10.7 11.9 %copy-start.46 = (s32[16]{0:T(128)S(1)}, s32[16]{0:T(128)}, u32[]{:S(2)}) copy-start(s32[16]{0:T(128)} %param.28) | copy-start | bytes 196
  10.7 12.1 %copy-start.41 = (s32[16,4]{0,1:T(4,128)S(1)}, s32[16,4]{0,1:T(4,128)}, u32[]{:S(2)}) copy-start(s32[16,4]{0,1:T(4,128)} %param.33) | copy-start | bytes 772
  10.7 12.8 %copy-start.2 = (bf16[1024,512]{1,0:T(8,128)(2,1)S(1)}, bf16[1024,512]{1,0:T(8,128)(2,1)}, u32[]{:S(2)}) copy-start(bf16[1024,512]{1,0:T(8,128)(2,1)} %param.44) | copy-start | bytes 3145732
  10.7 15.3 %copy-start.29 = (s32[2048]{0:T(1024)S(1)}, s32[2048]{0:T(1024)}, u32[]{:S(2)}) copy-start(s32[2048]{0:T(1024)} %param.32) | copy-start | bytes 24580
  10.7 24.7 %copy-start.43 = (s32[128]{0:T(128)S(1)}, s32[128]{0:T(128)}, u32[]{:S(2)}) copy-start(s32[128]{0:T(128)} %param.29) | copy-start | bytes 1540
  10.7 27.1 %copy-start.39 = (s32[128]{0:T(128)S(1)}, s32[128]{0:T(128)}, u32[]{:S(2)}) copy-start(s32[128]{0:T(128)} %param.30) | copy-start | bytes 1540
  12.3 0.8 copy-start.4
  13.1 26.2 %copy-start.1 = (bf16[1,1024,512]{2,1,0:T(8,128)(2,1)S(1)}, bf16[1,1024,512]{2,1,0:T(8,128)(2,1)}, u32[]{:S(2)}) copy-start(bf16[1,1024,512]{2,1,0:T(8,128)(2,1)} %param.40) | copy-start | bytes 3145732
  13.4 1.1 copy-start.18
  13.6 33.1 %copy-start.47 = (s32[2048]{0:T(1024)S(1)}, s32[2048]{0:T(1024)}, u32[]{:S(2)}) copy-start(s32[2048]{0:T(1024)} %param.31) | copy-start | bytes 24580
  15.2 14.0 %all-to-all-start = ((bf16[16,4,512]{2,1,0:T(4,128)(2,1)}), bf16[16,4,512]{2,1,0:T(4,128)(2,1)S(1)}, u32[]{:S(2)}, u32[]{:S(2)}) async-start(bf16[16,4,512]{2,1,0:T(4,128)(2,1)} %all_to_all.36), calls=%async_computation | async-start | bytes 131072 | tf_op jit(solution)/shard_map/all_to_all | solution.py:47
  22.8 6.7 %copy-start.32 = (s32[64]{0:T(128)}, s32[64]{0:T(128)S(1)}, u32[]{:S(2)}) copy-start(s32[64]{0:T(128)S(1)} %eq.133) | copy-start | bytes 772
  29.5 19.2 %copy-start.30 = (f32[64]{0:T(128)}, f32[64]{0:T(128)S(1)}, u32[]{:S(2)}) copy-start(f32[64]{0:T(128)S(1)} %add_rsqrt_fusion) | copy-start | bytes 772
  35.6 5.5 %collective-permute-start = (bf16[128,512]{1,0:T(8,128)(2,1)S(1)}, bf16[128,512]{1,0:T(8,128)(2,1)S(1)}, u32[]{:S(2)}, u32[]{:S(2)}) collective-permute-start(bf16[128,512]{1,0:T(8,128)(2,1)S(1)} %convolution_convert_fusion.16), channel_id=1, source_target_pairs={{0,1},{1,2},{2,3},{4,5},{5,6},{6,7},{8,9},{9,10},{10,11},{12,13},{... | collective-permute-start | bytes 393224 | tf_op jit(solution)/shard_map/ppermute | solution.py:54
  38.1 7.4 %collective-permute-start.1 = (bf16[128,512]{1,0:T(8,128)(2,1)S(1)}, bf16[128,512]{1,0:T(8,128)(2,1)S(1)}, u32[]{:S(2)}, u32[]{:S(2)}) collective-permute-start(bf16[128,512]{1,0:T(8,128)(2,1)S(1)} %convolution_convert_fusion.15), channel_id=1, source_target_pairs={{1,0},{2,1},{3,2},{5,4},{6,5},{7,6},{9,8},{10,9},{11,10},{13,12},{... | collective-permute-start | bytes 393224 | tf_op jit(solution)/shard_map/ppermute | solution.py:55
  45.5 0.8 copy-start.27
  48.6 1.9 copy-start.49
  48.7 1.9 copy-start.16
  50.6 0.6 copy-start.20
  51.5 3.6 %copy-start.25 = (f32[64,512]{1,0:T(8,128)}, f32[64,512]{1,0:T(8,128)S(1)}, u32[]{:S(2)}) copy-start(f32[64,512]{1,0:T(8,128)S(1)} %fusion.44) | copy-start | bytes 393220
  55.1 10.1 %all-to-all-start.1 = ((bf16[16,4,512]{2,1,0:T(4,128)(2,1)}), bf16[16,4,512]{2,1,0:T(4,128)(2,1)S(1)}, u32[]{:S(2)}, u32[]{:S(2)}) async-start(bf16[16,4,512]{2,1,0:T(4,128)(2,1)} %all_to_all.39), calls=%async_computation.1 | async-start | bytes 131072 | tf_op jit(solution)/shard_map/all_to_all | solution.py:47
  68.2 2.8 %copy-start.45 = (s32[64]{0:T(128)S(1)}, s32[64]{0:T(128)}, u32[]{:S(2)}) copy-start(s32[64]{0:T(128)} %eq.62) | copy-start | bytes 772
  70.2 0.8 copy-start.6
  73.7 10.1 %all-to-all-start.2 = ((bf16[16,4,512]{2,1,0:T(4,128)(2,1)}), bf16[16,4,512]{2,1,0:T(4,128)(2,1)S(1)}, u32[]{:S(2)}, u32[]{:S(2)}) async-start(bf16[16,4,512]{2,1,0:T(4,128)(2,1)} %all_to_all.42), calls=%async_computation.2 | async-start | bytes 131072 | tf_op jit(solution)/shard_map/all_to_all | solution.py:47
  77.2 97.6 %reduce-scatter.3.cloned.1.call-start = ((), (), s32[]{:S(2)}) async-start(), calls=%async_computation.7 | async-start | bytes 5570560 | tf_op jit(solution)/shard_map/reduce_scatter | solution.py:330
  84.7 0.6 copy-start.23
  86.7 0.6 copy-start.22
  87.4 11.5 %copy-start.12 = (f32[64,1024]{1,0:T(8,128)}, f32[64,1024]{1,0:T(8,128)S(1)}, u32[]{:S(2)}) copy-start(f32[64,1024]{1,0:T(8,128)S(1)} %fusion.42) | copy-start | bytes 786436
  87.4 5.0 %copy-start.48 = (s32[2048]{0:T(1024)S(1)}, s32[2048]{0:T(1024)}, u32[]{:S(2)}) copy-start(s32[2048]{0:T(1024)} %param.31) | copy-start | bytes 24580
  92.4 4.0 %copy-start.28 = (bf16[512,512]{1,0:T(8,128)(2,1)S(1)}, bf16[512,512]{1,0:T(8,128)(2,1)}, u32[]{:S(2)}) copy-start(bf16[512,512]{1,0:T(8,128)(2,1)} %copy-done.27) | copy-start | bytes 1572868
  92.4 6.5 %copy-start.21 = (bf16[64,512]{1,0:T(8,128)(2,1)S(1)}, bf16[64,512]{1,0:T(8,128)(2,1)}, u32[]{:S(2)}) copy-start(bf16[64,512]{1,0:T(8,128)(2,1)} %copy-done.20) | copy-start | bytes 196612
  96.4 3.6 %copy-start.14 = (bf16[576,512]{1,0:T(8,128)(2,1)}, bf16[576,512]{1,0:T(8,128)(2,1)S(1)}, u32[]{:S(2)}) copy-start(bf16[576,512]{1,0:T(8,128)(2,1)S(1)} %fusion.16) | copy-start | bytes 1769476
  109.3 8.4 %copy-start.5 = (bf16[512,512]{1,0:T(8,128)(2,1)S(1)}, bf16[512,512]{1,0:T(8,128)(2,1)}, u32[]{:S(2)}) copy-start(bf16[512,512]{1,0:T(8,128)(2,1)} %copy-done.4) | copy-start | bytes 1572868
  109.4 8.4 %copy-start.7 = (bf16[512,512]{1,0:T(8,128)(2,1)S(1)}, bf16[512,512]{1,0:T(8,128)(2,1)}, u32[]{:S(2)}) copy-start(bf16[512,512]{1,0:T(8,128)(2,1)} %copy-done.6) | copy-start | bytes 1572868
  109.4 9.7 %copy-start.8 = (bf16[512,512]{1,0:T(8,128)(2,1)S(1)}, bf16[512,512]{1,0:T(8,128)(2,1)}, u32[]{:S(2)}) copy-start(bf16[512,512]{1,0:T(8,128)(2,1)} %get-tuple-element.69) | copy-start | bytes 1572868
  109.4 15.9 %copy-start.11 = (bf16[512,227]{1,0:T(8,128)(2,1)S(1)}, bf16[512,227]{1,0:T(8,128)(2,1)}, u32[]{:S(2)}) copy-start(bf16[512,227]{1,0:T(8,128)(2,1)} %copy.87) | copy-start | bytes 697348
  117.8 12.5 %copy-start.44 = (s32[128]{0:T(128)S(1)}, s32[128]{0:T(128)}, u32[]{:S(2)}) copy-start(s32[128]{0:T(128)} %param.29) | copy-start | bytes 1540
  117.8 13.8 %copy-start.40 = (s32[128]{0:T(128)S(1)}, s32[128]{0:T(128)}, u32[]{:S(2)}) copy-start(s32[128]{0:T(128)} %param.30) | copy-start | bytes 1540
  119.8 6.3 %collective-permute-start.2 = (bf16[128,512]{1,0:T(8,128)(2,1)}, bf16[128,512]{1,0:T(8,128)(2,1)}, u32[]{:S(2)}, u32[]{:S(2)}) collective-permute-start(bf16[128,512]{1,0:T(8,128)(2,1)} %get-tuple-element.60), channel_id=1, source_target_pairs={{0,1},{1,2},{2,3},{4,5},{5,6},{6,7},{8,9},{9,10},{10,11},{12,13},{... | collective-permute-start | bytes 393224 | tf_op jit(solution)/shard_map/ppermute | solution.py:54
  122.7 18.8 %copy-start.24 = (bf16[64,512]{1,0:T(8,128)(2,1)S(1)}, bf16[64,512]{1,0:T(8,128)(2,1)}, u32[]{:S(2)}) copy-start(bf16[64,512]{1,0:T(8,128)(2,1)} %copy-done.23) | copy-start | bytes 196612
  122.7 18.8 %copy-start.31 = (f32[64]{0:T(128)S(1)}, f32[64]{0:T(128)}, u32[]{:S(2)}) copy-start(f32[64]{0:T(128)} %copy-done.30) | copy-start | bytes 772
  122.7 7.6 %collective-permute-start.3 = (bf16[128,512]{1,0:T(8,128)(2,1)}, bf16[128,512]{1,0:T(8,128)(2,1)}, u32[]{:S(2)}, u32[]{:S(2)}) collective-permute-start(bf16[128,512]{1,0:T(8,128)(2,1)} %get-tuple-element.59), channel_id=1, source_target_pairs={{1,0},{2,1},{3,2},{5,4},{6,5},{7,6},{9,8},{10,9},{11,10},{13,12},{... | collective-permute-start | bytes 393224 | tf_op jit(solution)/shard_map/ppermute | solution.py:55
  126.1 16.8 %copy-start.33 = (s32[64]{0:T(128)S(1)}, s32[64]{0:T(128)}, u32[]{:S(2)}) copy-start(s32[64]{0:T(128)} %copy-done.32) | copy-start | bytes 772
  130.3 23.7 %copy-start.26 = (f32[64,512]{1,0:T(8,128)S(1)}, f32[64,512]{1,0:T(8,128)}, u32[]{:S(2)}) copy-start(f32[64,512]{1,0:T(8,128)} %get-tuple-element.64) | copy-start | bytes 393220
  130.3 23.7 %copy-start.35 = (s32[64]{0:T(128)S(1)}, s32[64]{0:T(128)}, u32[]{:S(2)}) copy-start(s32[64]{0:T(128)} %copy-done.34) | copy-start | bytes 772
  132.9 23.6 %copy-start.10 = (f32[512,512]{1,0:T(8,128)S(1)}, f32[512,512]{1,0:T(8,128)}, u32[]{:S(2)}) copy-start(f32[512,512]{1,0:T(8,128)} %copy-done.9) | copy-start | bytes 3145732
  143.7 10.2 %all-to-all-start.4 = ((bf16[16,4,512]{2,1,0:T(4,128)(2,1)}), bf16[16,4,512]{2,1,0:T(4,128)(2,1)S(1)}, u32[]{:S(2)}, u32[]{:S(2)}) async-start(bf16[16,4,512]{2,1,0:T(4,128)(2,1)} %all_to_all.47), calls=%async_computation.4 | async-start | bytes 131072 | tf_op jit(solution)/shard_map/all_to_all | solution.py:47
  147.2 63.5 %reduce-scatter.5.cloned.1.call-start = ((), (), s32[]{:S(2)}) async-start(), calls=%async_computation.8 | async-start | bytes 1392640 | tf_op jit(solution)/shard_map/reduce_scatter | solution.py:363
  156.5 3.0 %copy-start.37 = (bf16[4,64]{1,0:T(4,128)(2,1)S(1)}, bf16[4,64]{1,0:T(4,128)(2,1)}, u32[]{:S(2)}) copy-start(bf16[4,64]{1,0:T(4,128)(2,1)} %param.26) | copy-start | bytes 1540
  156.5 4.0 %copy-start.19 = (bf16[64,512]{1,0:T(8,128)(2,1)S(1)}, bf16[64,512]{1,0:T(8,128)(2,1)}, u32[]{:S(2)}) copy-start(bf16[64,512]{1,0:T(8,128)(2,1)} %copy-done.18) | copy-start | bytes 196612
  160.4 2.0 copy-start.13
  160.4 2.0 copy-start.17
  160.8 14.1 %copy-start.3 = (bf16[512,512]{1,0:T(8,128)(2,1)S(1)}, bf16[512,512]{1,0:T(8,128)(2,1)}, u32[]{:S(2)}) copy-start(bf16[512,512]{1,0:T(8,128)(2,1)} %get-tuple-element.67) | copy-start | bytes 1572868
Sparse Core Ops, SparseCore 0:
  130.4 44.3 reduce-scatter.2
  177.2 33.5 reduce-scatter.4

commit v3 on v2

--- a/solution.py
+++ b/solution.py
@@ -56,12 +56,39 @@
     return from_previous, from_next
 
 
-def join_grads(grads):
-    padded = []
-    for grad in grads:
-        extra = -grad.shape[1] % 128
-        padded.append(jnp.pad(low(grad), ((0, 0), (0, extra))) if extra else low(grad))
-    return jnp.concatenate(padded, axis=1)
+def products_kernel(count, out_ref_at, *refs):
+    out_ref = refs[2 * count]
+    for index, start in enumerate(out_ref_at):
+        left, right = refs[2 * index], refs[2 * index + 1]
+        size = right.shape[1]
+        out_ref[:, start : start + size] = lax.dot_general(
+            left[...], right[...], (((0,), (0,)), ((), ())), preferred_element_type=jnp.float32
+        ).astype(LOW)
+
+
+def products(pairs):
+    starts = []
+    operands = []
+    columns = 0
+    for left, right in pairs:
+        starts.append(columns)
+        columns += right.shape[1]
+        operands += [left, right]
+    return pl.pallas_call(
+        functools.partial(products_kernel, len(pairs), tuple(starts)),
+        out_shape=jax.ShapeDtypeStruct((operands[0].shape[1], columns), LOW),
+        in_specs=[pl.BlockSpec(memory_space=pltpu.VMEM)] * len(operands),
+        out_specs=pl.BlockSpec(memory_space=pltpu.VMEM),
+        compiler_params=pltpu.CompilerParams(vmem_limit_bytes=32 * 2**20),
+        cost_estimate=pl.CostEstimate(
+            flops=0, bytes_accessed=6000 * columns, transcendentals=0
+        ),
+    )(*operands)
+
+
+def turned(values):
+    extra = -values.shape[0] % 128
+    return jnp.pad(values, ((0, extra), (0, 0))).T
 
 
 def split_grads(part, sizes):
@@ -311,21 +338,18 @@
     to_down, to_up = exchange(
         low(g_extended[halo + part :]), low(g_extended[:halo])
     )
-    early_whole = join_grads(
+    early_whole = products(
         (
-            jnp.concatenate(
-                [mm(g_send_map, extended, 0, 0), mm(g_own_map, latent, 0, 0)], axis=1
-            ),
-            mm(g_sum, hid_sum, 0, 0),
-            mm(g_node, joined, 0, 0),
-            mm(g_final, hid_node, 0, 0),
-            jnp.concatenate(
-                [mm(g_out, grid_latent, 0, 0), mm(g_out_mesh, arrived, 0, 0)], axis=1
-            ),
-            mm(hid_out, grid_cot, 0, 1),
+            (g_send_map, extended),
+            (g_own_map, latent),
+            (g_sum, hid_sum),
+            (g_node, joined),
+            (g_final, hid_node),
+            (g_out, grid_latent),
+            (g_out_mesh, arrived),
+            (hid_out, turned(grid_cot)),
         )
     )
-
     to_down, to_up, early_whole = lax.optimization_barrier((to_down, to_up, early_whole))
     early_part = lax.psum_scatter(early_whole, "grid", scatter_dimension=0, tiled=True)
     g_table = (
@@ -350,12 +374,12 @@
     g_rows = low(mm(g_pre, edge_weight, 1, 1))
     g_grid = low(mm(g_out, out_grid, 1, 1) + mm(send_hot, g_rows, 0, 0))
     g_embed = low(wide(low(mm(g_grid, embed_second, 1, 1))) * slope_embed)
-    late_whole = join_grads(
+    late_whole = products(
         (
-            mm(g_embed, grid_in, 0, 1),
-            mm(g_grid, hid_embed, 0, 0),
-            mm(g_pre, rows, 0, 0),
-            mm(g_pre, enc_feat, 0, 1),
+            (g_embed, turned(grid_in)),
+            (g_grid, hid_embed),
+            (g_pre, rows),
+            (g_pre, turned(enc_feat)),
         )
     )
     channels = grid_in.shape[0]

time: 222 us -> 200 us (0.901)
  local copies, waits for them, and re-layouts: 32.2 us -> 18.3 us
  matrix products: 59.6 us -> 49.8 us
  blocking collectives: 14.3 us -> 5.77 us
  starting transfers between devices: 26 us -> 29.8 us
  waiting for transfers between devices: 45.9 us -> 49.5 us
  Pallas kernels: 25.8 us -> 28.3 us
    dot_general x45 -> x34, matrix products: 59.6 us -> 49.8 us  [mm(): lax.dot_general(left, right, (((over_left,), (over_right,)), ((), ())), p...]
    all_to_all x1 -> x0, blocking collectives: 8.56 us -> none  [on_device(): lax.all_to_all(low(g_table), 'grid', split_axis=0, concat_axis=0, tiled=T...]
    all_to_all x0 -> x1, waiting for transfers between devices: none -> 5.21 us  [on_device(): lax.all_to_all(low(g_table), 'grid', split_axis=0, concat_axis=0, tiled=T...]
    unnamed x109 -> x102, local copies, waits for them, and re-layouts: 13.7 us -> 8.63 us
    another operation x2 -> x0, local copies, waits for them, and re-layouts: 4.09 us -> none
    convert_element_type x3 -> x0, local copies, waits for them, and re-layouts: 3.73 us -> none  [low(): return values.astype(LOW)]
    all_to_all x0 -> x1, starting transfers between devices: none -> 3.4 us  [on_device(): lax.all_to_all(low(g_table), 'grid', split_axis=0, concat_axis=0, tiled=T...]
    ppermute x2, waiting for transfers between devices: 8.52 us -> 5.55 us  [exchange(): from_next = lax.ppermute(to_previous, 'mesh', backward)]
  transfers between devices with their start and end apart: 10 -> 11, of which waited for: 9 -> 10; matrix products, arithmetic and copies ran while one was open for 13% -> 12% of each run, Pallas kernels for 12% -> 14%
where the time goes in v3:
time: 200 us; the launch traced here: 199 us
  matrix products  49.8 us (25%)
  waiting for transfers between devices  49.5 us (25%)
  starting transfers between devices  29.8 us (15%)
  Pallas kernels  28.3 us (14%)
  local copies, waits for them, and re-layouts  18.3 us (9%)
  between operations  15 us (8%)
  blocking collectives  5.77 us (3%)
  other arithmetic  2.1 us (1%)
    dot_general x34, matrix products, mm(): lax.dot_general(left, right, (((over_left,), (over_right,)), ((), ())), p...  49.8 us
    pallas_call x1, Pallas kernels, halving_scatter(): pl.pallas_call(functools.partial(halving_kernel, counts, rows, spans, pla...  25.8 us
    all_to_all x4, waiting for transfers between devices, route(): return lax.all_to_all(values, TILE, split_axis=0, concat_axis=0, tiled=True)  19.8 us
    all_to_all x4, starting transfers between devices, route(): return lax.all_to_all(values, TILE, split_axis=0, concat_axis=0, tiled=True)  18.4 us
    reduce_scatter x1, waiting for transfers between devices, on_device(): lax.psum_scatter(early_whole, 'grid', scatter_dimension=0, tiled=True)  12.2 us
    unnamed x102, local copies, waits for them, and re-layouts  8.63 us
    reduce_scatter x1, waiting for transfers between devices, on_device(): lax.psum_scatter(early_part, 'mesh', scatter_dimension=0, tiled=True)  6.28 us
    all_gather x1, blocking collectives, on_device(): table = lax.all_gather(latent, 'grid', axis=0, tiled=True)  5.77 us
  transfers between devices with their start and end apart: 11, of which 10 were waited for; matrix products, arithmetic and copies ran while one was open for 12% of the time, Pallas kernels for 14%

profile of v3, /device:TPU:0, one launch (start us, length us, event | category | flops | bytes accessed | tf_op | source)
XLA Modules:
  0.0 198.5 jit_solution(8909113357539227606)
XLA Ops:
  7.2 0.8 copy.45
  8.2 2.6 %multiply_convert_fusion.6 = (bf16[512,512]{1,0:T(8,128)(2,1)S(1)}, f32[512,512]{1,0:T(8,128)}) fusion(bf16[227,512]{1,0:T(8,128)(2,1)} %param.23, bf16[227,512]{1,0:T(8,128)(2,1)} %param.36), kind=kOutput, calls=%fused_computation.64 | convolution fusion | flops 120324096 | bytes 2037760 | tf_op jit(solution)/shard_map/dot_general | solution.py:17
  12.2 0.9 multiply_convert_fusion.10
  13.1 0.6 all_to_all.35
  13.8 7.4 %all-to-all-start = ((bf16[16,4,512]{2,1,0:T(4,128)(2,1)}), bf16[16,4,512]{2,1,0:T(4,128)(2,1)S(1)}, u32[]{:S(2)}, u32[]{:S(2)}) async-start(bf16[16,4,512]{2,1,0:T(4,128)(2,1)} %all_to_all.35), calls=%async_computation | async-start | bytes 131072 | tf_op jit(solution)/shard_map/all_to_all | solution.py:47
  21.5 1.5 fusion.60
  23.1 4.7 %all-to-all-done = bf16[16,4,512]{2,1,0:T(4,128)(2,1)S(1)} async-done(((bf16[16,4,512]{2,1,0:T(4,128)(2,1)}), bf16[16,4,512]{2,1,0:T(4,128)(2,1)S(1)}, u32[]{:S(2)}, u32[]{:S(2)}) %all-to-all-start) | async-done | bytes 65568 | tf_op jit(solution)/shard_map/all_to_all | solution.py:47
  28.6 5.8 %all_gather.3 = bf16[256,512]{1,0:T(8,128)(2,1)S(1)} all-gather(bf16[64,512]{1,0:T(8,128)(2,1)S(1)} %multiply_convert_fusion.11.refs_3_), channel_id=1, replica_groups=mesh['groups'=2,'grid'=4,'mesh'=4] {'grid'}, dimensions={0}, use_global_device_ids=true | all-gather | bytes 327680 | tf_op jit(solution)/shard_map/all_gather | solution.py:295
  34.6 2.3 %collective-permute-start = (bf16[128,512]{1,0:T(8,128)(2,1)S(1)}, bf16[128,512]{1,0:T(8,128)(2,1)S(1)}, u32[]{:S(2)}, u32[]{:S(2)}) collective-permute-start(bf16[128,512]{1,0:T(8,128)(2,1)S(1)} %convolution_convert_fusion.6), channel_id=1, source_target_pairs={{0,1},{1,2},{2,3},{4,5},{5,6},{6,7},{8,9},{9,10},{10,11},{12,13},{... | collective-permute-start | bytes 393224 | tf_op jit(solution)/shard_map/ppermute | solution.py:54
  37.1 1.3 collective-permute-start.1
  38.4 1.2 convolution_convert_fusion.17
  40.1 4.3 %collective-permute-done.1 = bf16[128,512]{1,0:T(8,128)(2,1)S(1)} collective-permute-done((bf16[128,512]{1,0:T(8,128)(2,1)S(1)}, bf16[128,512]{1,0:T(8,128)(2,1)S(1)}, u32[]{:S(2)}, u32[]{:S(2)}) %collective-permute-start.1) | collective-permute-done | bytes 131104 | tf_op jit(solution)/shard_map/ppermute | solution.py:55
  44.5 1.7 convolution_convert_fusion.1
  46.2 1.9 fusion.3
  48.1 1.5 fusion.27.refs_5_
  50.3 1.0 multiply_convert_fusion.9
  51.3 1.4 convolution_convert_fusion.15
  52.7 0.7 all_to_all.38
  53.3 3.5 %all-to-all-start.1 = ((bf16[16,4,512]{2,1,0:T(4,128)(2,1)}), bf16[16,4,512]{2,1,0:T(4,128)(2,1)S(1)}, u32[]{:S(2)}, u32[]{:S(2)}) async-start(bf16[16,4,512]{2,1,0:T(4,128)(2,1)} %all_to_all.38), calls=%async_computation.1 | async-start | bytes 131072 | tf_op jit(solution)/shard_map/all_to_all | solution.py:47
  57.0 6.4 %all-to-all-done.1 = bf16[16,4,512]{2,1,0:T(4,128)(2,1)S(1)} async-done(((bf16[16,4,512]{2,1,0:T(4,128)(2,1)}), bf16[16,4,512]{2,1,0:T(4,128)(2,1)S(1)}, u32[]{:S(2)}, u32[]{:S(2)}) %all-to-all-start.1) | async-done | bytes 65568 | tf_op jit(solution)/shard_map/all_to_all | solution.py:47
  63.4 3.0 %multiply_convert_fusion.5 = (bf16[512,512]{1,0:T(8,128)(2,1)S(1)}, f32[512,512]{1,0:T(8,128)}) fusion(f32[512,512]{1,0:T(8,128)} %fusion.60, bf16[64,512]{1,0:T(8,128)(2,1)S(1)} %all_to_all.40.refs_13_, bf16[1024,512]{1,0:T(8,128)(2,1)} %param.44, s32[64]{0:T(128)S(1)} %eq.62), kind=kOutput, calls=%fused_computation.61 | convolution fusion | flops 68747264 | bytes 3211520 | tf_op jit(solution)/shard_map/dot_general | solution.py:17
  66.5 2.2 %fusion.18.refs_10_ = bf16[512,512]{1,0:T(8,128)(2,1)S(1)} fusion(bf16[227,512]{1,0:T(8,128)(2,1)} %param.24, bf16[227,512]{1,0:T(8,128)(2,1)} %param.45, f32[512,512]{1,0:T(8,128)} %get-tuple-element.61), kind=kOutput, calls=%fused_computation.25 | convolution fusion | flops 121896960 | bytes 2037760 | tf_op jit(solution)/shard_map/dot_general | solution.py:17
  69.2 0.7 all_to_all.41
  69.9 3.5 %all-to-all-start.2 = ((bf16[16,4,512]{2,1,0:T(4,128)(2,1)}), bf16[16,4,512]{2,1,0:T(4,128)(2,1)S(1)}, u32[]{:S(2)}, u32[]{:S(2)}) async-start(bf16[16,4,512]{2,1,0:T(4,128)(2,1)} %all_to_all.41), calls=%async_computation.2 | async-start | bytes 131072 | tf_op jit(solution)/shard_map/all_to_all | solution.py:47
  73.6 1.8 copy.46
  75.4 4.6 %all-to-all-done.2 = bf16[16,4,512]{2,1,0:T(4,128)(2,1)S(1)} async-done(((bf16[16,4,512]{2,1,0:T(4,128)(2,1)}), bf16[16,4,512]{2,1,0:T(4,128)(2,1)S(1)}, u32[]{:S(2)}, u32[]{:S(2)}) %all-to-all-start.2) | async-done | bytes 65568 | tf_op jit(solution)/shard_map/all_to_all | solution.py:47
  80.6 1.1 convolution_convert_fusion.11.refs_8_
  81.7 1.4 fusion.30.refs_6_
  83.1 1.2 fusion.31
  84.9 5.0 %multiply_convert_fusion = bf16[2048,512]{1,0:T(8,128)(2,1)} fusion(f32[2048,512]{1,0:T(8,128)} %copy-done.46, bf16[1,512,512]{2,1,0:T(8,128)(2,1)} %param.41, s32[2048]{0:T(1024)S(1)} %copy-done.25, f32[64,1024]{1,0:T(8,128)} %fusion.31), kind=kOutput, calls=%fused_computation.3 | convolution fusion | flops 177373184 | bytes 6889472 | tf_op jit(solution)/shard_map/dot_general | solution.py:17
  89.9 4.0 %fusion.10 = bf16[576,512]{1,0:T(8,128)(2,1)S(1)} fusion(bf16[2048,512]{1,0:T(8,128)(2,1)} %multiply_convert_fusion, s32[2048]{0:T(1024)S(1)} %broadcast_add_fusion, s32[2048]{0:T(1024)} %param.31), kind=kOutput, calls=%fused_computation.15 | convolution fusion | flops 1211793408 | bytes 2703360 | tf_op jit(solution)/shard_map/dot_general | solution.py:17
  94.0 1.5 fusion.88
  95.4 0.7 fusion.85
  96.2 2.9 %collective-permute-start.2 = (bf16[128,512]{1,0:T(8,128)(2,1)}, bf16[128,512]{1,0:T(8,128)(2,1)}, u32[]{:S(2)}, u32[]{:S(2)}) collective-permute-start(bf16[128,512]{1,0:T(8,128)(2,1)} %get-tuple-element.49), channel_id=1, source_target_pairs={{0,1},{1,2},{2,3},{4,5},{5,6},{6,7},{8,9},{9,10},{10,11},{12,13},{... | collective-permute-start | bytes 393224 | tf_op jit(solution)/shard_map/ppermute | solution.py:54
  99.1 1.3 collective-permute-start.3
  100.5 0.9 slice.152.refs_4_
  101.4 1.7 shard_map.302
  103.2 2.0 %copy-done.1 = bf16[512,4352]{1,0:T(8,128)(2,1)} copy-done((bf16[512,4352]{1,0:T(8,128)(2,1)}, bf16[512,4352]{1,0:T(8,128)(2,1)S(1)}, u32[]{:S(2)}) %copy-start.1) | copy-done | bytes 4456472
  105.3 1.2 collective-permute-done.3
  106.8 1.2 fusion.62
  108.0 2.2 %fusion.21 = bf16[256,512]{1,0:T(8,128)(2,1)} fusion(f32[256,512]{1,0:T(8,128)S(1)} %fusion.62, bf16[128,512]{1,0:T(8,128)(2,1)} %collective-permute-done.2, f32[512,512]{1,0:T(8,128)} %get-tuple-element.63, s32[128]{0:T(128)S(1)} %copy-done.35), kind=kOutput, calls=%fused_computation.29 | convolution fusion | flops 33980416 | bytes 1442304 | tf_op jit(solution)/shard_map/dot_general | solution.py:17
  110.2 3.4 %all-to-all-start.3 = ((bf16[4,64,512]{2,1,0:T(8,128)(2,1)}), bf16[4,64,512]{2,1,0:T(8,128)(2,1)S(1)}, u32[]{:S(2)}, u32[]{:S(2)}) async-start(bf16[4,64,512]{2,1,0:T(8,128)(2,1)} %bitcast.105), calls=%async_computation.3 | async-start | bytes 524288 | tf_op jit(solution)/shard_map/all_to_all | solution.py:360
  113.6 0.8 pad_bitcast_fusion.refs_1_
  114.4 5.2 %all-to-all-done.3 = bf16[4,64,512]{2,1,0:T(8,128)(2,1)S(1)} async-done(((bf16[4,64,512]{2,1,0:T(8,128)(2,1)}), bf16[4,64,512]{2,1,0:T(8,128)(2,1)S(1)}, u32[]{:S(2)}, u32[]{:S(2)}) %all-to-all-start.3) | async-done | bytes 262176 | tf_op jit(solution)/shard_map/all_to_all | solution.py:360
  119.7 1.5 multiply_reduce_fusion
  121.2 0.9 convolution_convert_fusion.8
  122.1 0.7 all_to_all.46
  122.7 4.0 %all-to-all-start.4 = ((bf16[16,4,512]{2,1,0:T(4,128)(2,1)}), bf16[16,4,512]{2,1,0:T(4,128)(2,1)S(1)}, u32[]{:S(2)}, u32[]{:S(2)}) async-start(bf16[16,4,512]{2,1,0:T(4,128)(2,1)} %all_to_all.46), calls=%async_computation.4 | async-start | bytes 131072 | tf_op jit(solution)/shard_map/all_to_all | solution.py:47
  126.8 2.5 %fusion.58 = f32[512,512]{1,0:T(8,128)} fusion(bf16[512,512]{1,0:T(8,128)(2,1)S(1)} %fusion.18.refs_10_, bf16[1024,512]{1,0:T(8,128)(2,1)} %param.44), kind=kOutput, calls=%fused_computation.87 | convolution fusion | flops 268435456 | bytes 2097152 | tf_op jit(solution)/shard_map/dot_general | solution.py:17
  129.3 4.2 %all-to-all-done.4 = bf16[16,4,512]{2,1,0:T(4,128)(2,1)S(1)} async-done(((bf16[16,4,512]{2,1,0:T(4,128)(2,1)}), bf16[16,4,512]{2,1,0:T(4,128)(2,1)S(1)}, u32[]{:S(2)}, u32[]{:S(2)}) %all-to-all-start.4) | async-done | bytes 65568 | tf_op jit(solution)/shard_map/all_to_all | solution.py:47
  133.5 1.0 multiply_convert_fusion.7.refs_4_.refs_6_
  134.5 2.0 fusion.13.refs_2_
  136.5 2.1 %fusion.19.refs_0_ = bf16[512,512]{1,0:T(8,128)(2,1)S(1)} fusion(bf16[512,512]{1,0:T(8,128)(2,1)S(1)} %fusion.13.refs_2_, bf16[512,512]{1,0:T(8,128)(2,1)} %param.37, f32[512,512]{1,0:T(8,128)} %get-tuple-element.53), kind=kOutput, calls=%fused_computation.26 | convolution fusion | flops 271319040 | bytes 2621440 | tf_op jit(solution)/shard_map/dot_general | solution.py:17
  138.6 0.8 copy-done.4
  139.5 0.8 shard_map.303.x_ref
  140.3 12.2 %reduce-scatter.3.cloned.1.call-done = bf16[128,4352]{1,0:T(8,128)(2,1)} async-done(((bf16[512,4352]{1,0:T(8,128)(2,1)}), bf16[128,4352]{1,0:T(8,128)(2,1)}) %reduce-scatter.3.cloned.1.call-update) | async-done | bytes 1114128 | tf_op jit(solution)/shard_map/reduce_scatter | solution.py:354
  152.5 2.1 %fusion.22 = bf16[227,512]{1,0:T(8,128)(2,1)} fusion(bf16[512,512]{1,0:T(8,128)(2,1)} %copy-done.2, bf16[227,512]{1,0:T(8,128)(2,1)} %param.45), kind=kOutput, calls=%fused_computation.31 | convolution fusion | flops 119129600 | bytes 989184 | tf_op jit(solution)/shard_map/dot_general | solution.py:17
  154.6 25.8 %shard_map.304 = f32[32,1408]{1,0:T(8,128)S(1)} custom-call(bf16[512,1408]{1,0:T(8,128)(2,1)S(1)} %shard_map.303.x_ref), custom_call_target="tpu_custom_call" | custom-call | bytes 90000000 | tf_op jit(solution)/shard_map/pallas_call | solution.py:228
  180.4 0.7 copy.49
  181.7 0.7 slice_bitcast_fusion.5
  182.4 6.3 %reduce-scatter.5.cloned.1.call-done = bf16[32,4352]{1,0:T(8,128)(2,1)} async-done(((bf16[128,4352]{1,0:T(8,128)(2,1)}), bf16[32,4352]{1,0:T(8,128)(2,1)}) %reduce-scatter.5.cloned.1.call-update) | async-done | bytes 278544 | tf_op jit(solution)/shard_map/reduce_scatter | solution.py:387
  188.6 1.0 convert_element_type.201
  189.6 0.8 slice_bitcast_fusion
  190.4 0.7 slice_bitcast_fusion.3
  (138 shorter events, 8.2 us)
Async XLA Ops:
  7.2 43.1 %copy-start = (bf16[1,1024,512]{2,1,0:T(8,128)(2,1)S(1)}, bf16[1,1024,512]{2,1,0:T(8,128)(2,1)}, u32[]{:S(2)}) copy-start(bf16[1,1024,512]{2,1,0:T(8,128)(2,1)} %param.42) | copy-start | bytes 3145732
  7.2 4.4 %copy-start.31 = (bf16[4,64]{1,0:T(4,128)(2,1)S(1)}, bf16[4,64]{1,0:T(4,128)(2,1)}, u32[]{:S(2)}) copy-start(bf16[4,64]{1,0:T(4,128)(2,1)} %param.26) | copy-start | bytes 1540
  7.2 4.4 %copy-start.33 = (bf16[4,512]{1,0:T(4,128)(2,1)S(1)}, bf16[4,512]{1,0:T(4,128)(2,1)}, u32[]{:S(2)}) copy-start(bf16[4,512]{1,0:T(4,128)(2,1)} %param.39) | copy-start | bytes 12292
  8.1 3.4 %copy-start.30 = (s32[64]{0:T(128)}, s32[64]{0:T(128)S(1)}, u32[]{:S(2)}) copy-start(s32[64]{0:T(128)S(1)} %eq.137) | copy-start | bytes 772
  8.2 2.7 %copy-start.20 = (bf16[512,512]{1,0:T(8,128)(2,1)S(1)}, bf16[512,512]{1,0:T(8,128)(2,1)}, u32[]{:S(2)}) copy-start(bf16[512,512]{1,0:T(8,128)(2,1)} %param.37) | copy-start | bytes 1572868
  8.2 4.1 %copy-start.19 = (bf16[512,512]{1,0:T(8,128)(2,1)S(1)}, bf16[512,512]{1,0:T(8,128)(2,1)}, u32[]{:S(2)}) copy-start(bf16[512,512]{1,0:T(8,128)(2,1)} %param.38) | copy-start | bytes 1572868
  8.2 12.9 %copy-start.37 = (s32[16,4]{0,1:T(4,128)S(1)}, s32[16,4]{0,1:T(4,128)}, u32[]{:S(2)}) copy-start(s32[16,4]{0,1:T(4,128)} %param.27) | copy-start | bytes 772
  8.2 12.9 %copy-start.43 = (s32[16]{0:T(128)S(1)}, s32[16]{0:T(128)}, u32[]{:S(2)}) copy-start(s32[16]{0:T(128)} %param.28) | copy-start | bytes 196
  8.2 13.1 %copy-start.36 = (s32[16,4]{0,1:T(4,128)S(1)}, s32[16,4]{0,1:T(4,128)}, u32[]{:S(2)}) copy-start(s32[16,4]{0,1:T(4,128)} %param.33) | copy-start | bytes 772
  8.2 13.3 %copy-start.14 = (bf16[1024,512]{1,0:T(8,128)(2,1)S(1)}, bf16[1024,512]{1,0:T(8,128)(2,1)}, u32[]{:S(2)}) copy-start(bf16[1024,512]{1,0:T(8,128)(2,1)} %param.44) | copy-start | bytes 3145732
  8.2 14.8 %copy-start.25 = (s32[2048]{0:T(1024)S(1)}, s32[2048]{0:T(1024)}, u32[]{:S(2)}) copy-start(s32[2048]{0:T(1024)} %param.32) | copy-start | bytes 24580
  10.9 23.5 %copy-start.39 = (s32[128]{0:T(128)S(1)}, s32[128]{0:T(128)}, u32[]{:S(2)}) copy-start(s32[128]{0:T(128)} %param.29) | copy-start | bytes 1540
  10.9 26.0 %copy-start.34 = (s32[128]{0:T(128)S(1)}, s32[128]{0:T(128)}, u32[]{:S(2)}) copy-start(s32[128]{0:T(128)} %param.30) | copy-start | bytes 1540
  11.6 0.6 copy-start.10
  12.2 33.9 %copy-start.45 = (s32[2048]{0:T(1024)S(1)}, s32[2048]{0:T(1024)}, u32[]{:S(2)}) copy-start(s32[2048]{0:T(1024)} %param.31) | copy-start | bytes 24580
  13.8 14.0 %all-to-all-start = ((bf16[16,4,512]{2,1,0:T(4,128)(2,1)}), bf16[16,4,512]{2,1,0:T(4,128)(2,1)S(1)}, u32[]{:S(2)}, u32[]{:S(2)}) async-start(bf16[16,4,512]{2,1,0:T(4,128)(2,1)} %all_to_all.35), calls=%async_computation | async-start | bytes 131072 | tf_op jit(solution)/shard_map/all_to_all | solution.py:47
  21.3 26.8 %copy-start.28 = (s32[64]{0:T(128)}, s32[64]{0:T(128)S(1)}, u32[]{:S(2)}) copy-start(s32[64]{0:T(128)S(1)} %eq.133) | copy-start | bytes 772
  21.5 29.7 %copy-start.29 = (s32[64]{0:T(128)}, s32[64]{0:T(128)S(1)}, u32[]{:S(2)}) copy-start(s32[64]{0:T(128)S(1)} %eq.129) | copy-start | bytes 772
  28.0 11.6 %copy-start.16 = (f32[64,512]{1,0:T(8,128)}, f32[64,512]{1,0:T(8,128)S(1)}, u32[]{:S(2)}) copy-start(f32[64,512]{1,0:T(8,128)S(1)} %get-tuple-element.57) | copy-start | bytes 393220
  28.0 0.5 copy-start.26
  34.6 5.5 %collective-permute-start = (bf16[128,512]{1,0:T(8,128)(2,1)S(1)}, bf16[128,512]{1,0:T(8,128)(2,1)S(1)}, u32[]{:S(2)}, u32[]{:S(2)}) collective-permute-start(bf16[128,512]{1,0:T(8,128)(2,1)S(1)} %convolution_convert_fusion.6), channel_id=1, source_target_pairs={{0,1},{1,2},{2,3},{4,5},{5,6},{6,7},{8,9},{9,10},{10,11},{12,13},{... | collective-permute-start | bytes 393224 | tf_op jit(solution)/shard_map/ppermute | solution.py:54
  37.1 7.4 %collective-permute-start.1 = (bf16[128,512]{1,0:T(8,128)(2,1)S(1)}, bf16[128,512]{1,0:T(8,128)(2,1)S(1)}, u32[]{:S(2)}, u32[]{:S(2)}) collective-permute-start(bf16[128,512]{1,0:T(8,128)(2,1)S(1)} %convolution_convert_fusion.5), channel_id=1, source_target_pairs={{1,0},{2,1},{3,2},{5,4},{6,5},{7,6},{9,8},{10,9},{11,10},{13,12},{... | collective-permute-start | bytes 393224 | tf_op jit(solution)/shard_map/ppermute | solution.py:55
  44.5 3.6 %copy-start.6 = (bf16[512,512]{1,0:T(8,128)(2,1)}, bf16[512,512]{1,0:T(8,128)(2,1)S(1)}, u32[]{:S(2)}) copy-start(bf16[512,512]{1,0:T(8,128)(2,1)S(1)} %constant_dynamic-update-slice_fusion.refs_1_) | copy-start | bytes 1572868
  48.1 2.0 copy-start.46
  48.1 2.0 copy-start.21
  48.1 8.7 %copy-start.38 = (s32[16,4]{0,1:T(4,128)S(1)}, s32[16,4]{0,1:T(4,128)}, u32[]{:S(2)}) copy-start(s32[16,4]{0,1:T(4,128)} %param.34) | copy-start | bytes 772
  48.1 8.7 %copy-start.44 = (s32[16]{0:T(128)S(1)}, s32[16]{0:T(128)}, u32[]{:S(2)}) copy-start(s32[16]{0:T(128)} %param.35) | copy-start | bytes 196
  50.3 16.2 %copy-start.22 = (bf16[64,512]{1,0:T(8,128)(2,1)}, bf16[64,512]{1,0:T(8,128)(2,1)S(1)}, u32[]{:S(2)}) copy-start(bf16[64,512]{1,0:T(8,128)(2,1)S(1)} %convolution_convert_fusion.16) | copy-start | bytes 196612
  53.3 10.1 %all-to-all-start.1 = ((bf16[16,4,512]{2,1,0:T(4,128)(2,1)}), bf16[16,4,512]{2,1,0:T(4,128)(2,1)S(1)}, u32[]{:S(2)}, u32[]{:S(2)}) async-start(bf16[16,4,512]{2,1,0:T(4,128)(2,1)} %all_to_all.38), calls=%async_computation.1 | async-start | bytes 131072 | tf_op jit(solution)/shard_map/all_to_all | solution.py:47
  57.0 9.4 %copy-start.41 = (s32[64]{0:T(128)}, s32[64]{0:T(128)S(1)}, u32[]{:S(2)}) copy-start(s32[64]{0:T(128)S(1)} %eq.62) | copy-start | bytes 772
  66.4 35.0 %copy-start.2 = (bf16[512,512]{1,0:T(8,128)(2,1)}, bf16[512,512]{1,0:T(8,128)(2,1)S(1)}, u32[]{:S(2)}) copy-start(bf16[512,512]{1,0:T(8,128)(2,1)S(1)} %get-tuple-element.60.refs_14_) | copy-start | bytes 1572868
  66.4 2.5 %copy-start.15 = (bf16[1024,512]{1,0:T(8,128)(2,1)S(1)}, bf16[1024,512]{1,0:T(8,128)(2,1)}, u32[]{:S(2)}) copy-start(bf16[1024,512]{1,0:T(8,128)(2,1)} %param.44) | copy-start | bytes 3145732
  66.5 2.2 %copy-start.42 = (s32[64]{0:T(128)S(1)}, s32[64]{0:T(128)}, u32[]{:S(2)}) copy-start(s32[64]{0:T(128)} %copy-done.41) | copy-start | bytes 772
  69.9 10.1 %all-to-all-start.2 = ((bf16[16,4,512]{2,1,0:T(4,128)(2,1)}), bf16[16,4,512]{2,1,0:T(4,128)(2,1)S(1)}, u32[]{:S(2)}, u32[]{:S(2)}) async-start(bf16[16,4,512]{2,1,0:T(4,128)(2,1)} %all_to_all.41), calls=%async_computation.2 | async-start | bytes 131072 | tf_op jit(solution)/shard_map/all_to_all | solution.py:47
  73.4 79.1 %reduce-scatter.3.cloned.1.call-start = ((), (), s32[]{:S(2)}) async-start(), calls=%async_computation.7 | async-start | bytes 5570560 | tf_op jit(solution)/shard_map/reduce_scatter | solution.py:354
  84.2 0.6 copy-start.8
  89.9 4.1 %copy-start.12 = (bf16[1,1024,512]{2,1,0:T(8,128)(2,1)S(1)}, bf16[1,1024,512]{2,1,0:T(8,128)(2,1)}, u32[]{:S(2)}) copy-start(bf16[1,1024,512]{2,1,0:T(8,128)(2,1)} %param.40) | copy-start | bytes 3145732
  89.9 10.5 %copy-start.18 = (bf16[227,512]{0,1:T(8,128)(2,1)S(1)}, bf16[227,512]{0,1:T(8,128)(2,1)}, u32[]{:S(2)}) copy-start(bf16[227,512]{0,1:T(8,128)(2,1)} %copy.46) | copy-start | bytes 697348
  89.9 10.5 %copy-start.23 = (bf16[64,512]{1,0:T(8,128)(2,1)S(1)}, bf16[64,512]{1,0:T(8,128)(2,1)}, u32[]{:S(2)}) copy-start(bf16[64,512]{1,0:T(8,128)(2,1)} %copy-done.22) | copy-start | bytes 196612
  93.9 7.5 %copy-start.13 = (bf16[576,512]{1,0:T(8,128)(2,1)}, bf16[576,512]{1,0:T(8,128)(2,1)S(1)}, u32[]{:S(2)}) copy-start(bf16[576,512]{1,0:T(8,128)(2,1)S(1)} %fusion.10) | copy-start | bytes 1769476
  94.0 7.5 %copy-start.7 = (bf16[512,512]{1,0:T(8,128)(2,1)S(1)}, bf16[512,512]{1,0:T(8,128)(2,1)}, u32[]{:S(2)}) copy-start(bf16[512,512]{1,0:T(8,128)(2,1)} %copy-done.6) | copy-start | bytes 1572868
  94.0 7.5 %copy-start.9 = (bf16[64,512]{1,0:T(8,128)(2,1)S(1)}, bf16[64,512]{1,0:T(8,128)(2,1)}, u32[]{:S(2)}) copy-start(bf16[64,512]{1,0:T(8,128)(2,1)} %copy-done.8) | copy-start | bytes 196612
  96.2 9.1 %collective-permute-start.2 = (bf16[128,512]{1,0:T(8,128)(2,1)}, bf16[128,512]{1,0:T(8,128)(2,1)}, u32[]{:S(2)}, u32[]{:S(2)}) collective-permute-start(bf16[128,512]{1,0:T(8,128)(2,1)} %get-tuple-element.49), channel_id=1, source_target_pairs={{0,1},{1,2},{2,3},{4,5},{5,6},{6,7},{8,9},{9,10},{10,11},{12,13},{... | collective-permute-start | bytes 393224 | tf_op jit(solution)/shard_map/ppermute | solution.py:54
  99.1 7.4 %collective-permute-start.3 = (bf16[128,512]{1,0:T(8,128)(2,1)}, bf16[128,512]{1,0:T(8,128)(2,1)}, u32[]{:S(2)}, u32[]{:S(2)}) collective-permute-start(bf16[128,512]{1,0:T(8,128)(2,1)} %get-tuple-element.48), channel_id=1, source_target_pairs={{1,0},{2,1},{3,2},{5,4},{6,5},{7,6},{9,8},{10,9},{11,10},{13,12},{... | collective-permute-start | bytes 393224 | tf_op jit(solution)/shard_map/ppermute | solution.py:55
  103.2 2.0 %copy-start.1 = (bf16[512,4352]{1,0:T(8,128)(2,1)}, bf16[512,4352]{1,0:T(8,128)(2,1)S(1)}, u32[]{:S(2)}) copy-start(bf16[512,4352]{1,0:T(8,128)(2,1)S(1)} %shard_map.302) | copy-start | bytes 13369348
  105.2 1.3 copy-start.24
  105.2 1.4 copy-start.32
  105.2 1.6 copy-start.40
  105.2 2.8 %copy-start.35 = (s32[128]{0:T(128)S(1)}, s32[128]{0:T(128)}, u32[]{:S(2)}) copy-start(s32[128]{0:T(128)} %param.30) | copy-start | bytes 1540
  105.2 14.4 %copy-start.17 = (f32[64,512]{1,0:T(8,128)S(1)}, f32[64,512]{1,0:T(8,128)}, u32[]{:S(2)}) copy-start(f32[64,512]{1,0:T(8,128)} %copy-done.16) | copy-start | bytes 393220
  105.2 14.4 %copy-start.27 = (f32[64]{0:T(128)S(1)}, f32[64]{0:T(128)}, u32[]{:S(2)}) copy-start(f32[64]{0:T(128)} %copy-done.26) | copy-start | bytes 772
  110.2 9.4 %all-to-all-start.3 = ((bf16[4,64,512]{2,1,0:T(8,128)(2,1)}), bf16[4,64,512]{2,1,0:T(8,128)(2,1)S(1)}, u32[]{:S(2)}, u32[]{:S(2)}) async-start(bf16[4,64,512]{2,1,0:T(8,128)(2,1)} %bitcast.105), calls=%async_computation.3 | async-start | bytes 524288 | tf_op jit(solution)/shard_map/all_to_all | solution.py:360
  122.7 10.8 %all-to-all-start.4 = ((bf16[16,4,512]{2,1,0:T(4,128)(2,1)}), bf16[16,4,512]{2,1,0:T(4,128)(2,1)S(1)}, u32[]{:S(2)}, u32[]{:S(2)}) async-start(bf16[16,4,512]{2,1,0:T(4,128)(2,1)} %all_to_all.46), calls=%async_computation.4 | async-start | bytes 131072 | tf_op jit(solution)/shard_map/all_to_all | solution.py:47
  126.8 61.9 %reduce-scatter.5.cloned.1.call-start = ((), (), s32[]{:S(2)}) async-start(), calls=%async_computation.8 | async-start | bytes 1392640 | tf_op jit(solution)/shard_map/reduce_scatter | solution.py:387
  134.5 2.0 %copy-start.3 = (bf16[64,512]{1,0:T(8,128)(2,1)}, bf16[64,512]{1,0:T(8,128)(2,1)S(1)}, u32[]{:S(2)}) copy-start(bf16[64,512]{1,0:T(8,128)(2,1)S(1)} %multiply_convert_fusion.7.refs_4_.refs_6_) | copy-start | bytes 196612
  136.5 2.1 %copy-start.5 = (bf16[512,256]{1,0:T(8,128)(2,1)S(1)}, bf16[512,256]{1,0:T(8,128)(2,1)}, u32[]{:S(2)}) copy-start(bf16[512,256]{1,0:T(8,128)(2,1)} %pad_bitcast_fusion.refs_1_) | copy-start | bytes 786436
  136.5 2.1 %copy-start.11 = (bf16[64,512]{1,0:T(8,128)(2,1)S(1)}, bf16[64,512]{1,0:T(8,128)(2,1)}, u32[]{:S(2)}) copy-start(bf16[64,512]{1,0:T(8,128)(2,1)} %copy-done.10) | copy-start | bytes 196612
  138.6 0.8 copy-start.4
Sparse Core Ops, SparseCore 0:
  106.6 45.7 reduce-scatter.2
  154.9 33.7 reduce-scatter.4

commit v4 on v3

--- a/solution.py
+++ b/solution.py
@@ -347,7 +347,6 @@
             (g_final, hid_node),
             (g_out, grid_latent),
             (g_out_mesh, arrived),
-            (hid_out, turned(grid_cot)),
         )
     )
     to_down, to_up, early_whole = lax.optimization_barrier((to_down, to_up, early_whole))
@@ -380,19 +379,20 @@
             (g_grid, hid_embed),
             (g_pre, rows),
             (g_pre, turned(enc_feat)),
+            (hid_out, turned(grid_cot)),
         )
     )
     channels = grid_in.shape[0]
     late_whole, early_part = lax.optimization_barrier((late_whole, early_part))
     early_part = lax.psum_scatter(early_part, "mesh", scatter_dimension=0, tiled=True)
     late = split_grads(
-        halving_scatter(late_whole), (channels, width, width, enc_feat.shape[0])
+        halving_scatter(late_whole), (channels, width, width, enc_feat.shape[0], channels)
     )
     early = split_grads(
-        early_part, (2 * width, width, 2 * width, width, 2 * width, channels)
+        early_part, (2 * width, width, 2 * width, width, 2 * width)
     )
     layer = [grad[None] for grad in early[:4]]
-    return (delta,) + tuple(late) + tuple(layer) + tuple(early[4:])
+    return (delta,) + tuple(late[:4]) + tuple(layer) + (early[4], late[4])
 
 
 def solution(mesh):

time: 200 us -> 198 us (0.990)
  waiting for transfers between devices: 49.5 us -> 38.1 us
  blocking collectives: 5.77 us -> 15.9 us
  Pallas kernels: 28.3 us -> 32.7 us
  starting transfers between devices: 29.8 us -> 25.9 us
    all_to_all x0 -> x1, blocking collectives: none -> 10.1 us  [route(): return lax.all_to_all(values, TILE, split_axis=0, concat_axis=0, tiled=True)]
    all_to_all x4 -> x3, waiting for transfers between devices: 19.8 us -> 15.3 us  [route(): return lax.all_to_all(values, TILE, split_axis=0, concat_axis=0, tiled=True)]
    pallas_call x1, Pallas kernels: 25.8 us -> 30.2 us  [halving_scatter(): pl.pallas_call(functools.partial(halving_kernel, counts, rows, spans, pla...]
    all_to_all x4 -> x3, starting transfers between devices: 18.4 us -> 14.5 us  [route(): return lax.all_to_all(values, TILE, split_axis=0, concat_axis=0, tiled=True)]
    reduce_scatter x1, waiting for transfers between devices: 6.28 us -> 2.54 us  [on_device(): lax.psum_scatter(early_part, 'mesh', scatter_dimension=0, tiled=True)]
    reduce_scatter x1, waiting for transfers between devices: 12.2 us -> 9.83 us  [on_device(): lax.psum_scatter(early_whole, 'grid', scatter_dimension=0, tiled=True)]
    unnamed x102 -> x104, local copies, waits for them, and re-layouts: 8.63 us -> 8.08 us
  transfers between devices with their start and end apart: 11 -> 10, of which waited for: 10 -> 9; matrix products, arithmetic and copies ran while one was open for 12% -> 12% of each run, Pallas kernels for 14% -> 17%
where the time goes in v4:
time: 198 us; the launch traced here: 197 us
  matrix products  49.4 us (25%)
  waiting for transfers between devices  38.1 us (19%)
  Pallas kernels  32.7 us (17%)
  starting transfers between devices  25.9 us (13%)
  local copies, waits for them, and re-layouts  18.2 us (9%)
  blocking collectives  15.9 us (8%)
  between operations  14.9 us (8%)
  other arithmetic  2.09 us (1%)
    dot_general x34, matrix products, mm(): lax.dot_general(left, right, (((over_left,), (over_right,)), ((), ())), p...  49.4 us
    pallas_call x1, Pallas kernels, halving_scatter(): pl.pallas_call(functools.partial(halving_kernel, counts, rows, spans, pla...  30.2 us
    all_to_all x3, waiting for transfers between devices, route(): return lax.all_to_all(values, TILE, split_axis=0, concat_axis=0, tiled=True)  15.3 us
    all_to_all x3, starting transfers between devices, route(): return lax.all_to_all(values, TILE, split_axis=0, concat_axis=0, tiled=True)  14.5 us
    all_to_all x1, blocking collectives, route(): return lax.all_to_all(values, TILE, split_axis=0, concat_axis=0, tiled=True)  10.1 us
    reduce_scatter x1, waiting for transfers between devices, on_device(): lax.psum_scatter(early_whole, 'grid', scatter_dimension=0, tiled=True)  9.83 us
    unnamed x104, local copies, waits for them, and re-layouts  8.08 us
    ppermute x2, waiting for transfers between devices, exchange(): from_next = lax.ppermute(to_previous, 'mesh', backward)  5.84 us
  transfers between devices with their start and end apart: 10, of which 9 were waited for; matrix products, arithmetic and copies ran while one was open for 12% of the time, Pallas kernels for 17%

profile of v4, /device:TPU:0, one launch (start us, length us, event | category | flops | bytes accessed | tf_op | source)
XLA Modules:
  0.0 197.2 jit_solution(18017757156562141036)
XLA Ops:
  7.2 0.8 copy.45
  8.2 2.6 %multiply_convert_fusion.6 = (bf16[512,512]{1,0:T(8,128)(2,1)S(1)}, f32[512,512]{1,0:T(8,128)}) fusion(bf16[227,512]{1,0:T(8,128)(2,1)} %param.23, bf16[227,512]{1,0:T(8,128)(2,1)} %param.36), kind=kOutput, calls=%fused_computation.64 | convolution fusion | flops 120324096 | bytes 2037760 | tf_op jit(solution)/shard_map/dot_general | solution.py:17
  12.2 0.9 multiply_convert_fusion.10
  13.1 0.6 all_to_all.35
  13.7 7.4 %all-to-all-start = ((bf16[16,4,512]{2,1,0:T(4,128)(2,1)}), bf16[16,4,512]{2,1,0:T(4,128)(2,1)S(1)}, u32[]{:S(2)}, u32[]{:S(2)}) async-start(bf16[16,4,512]{2,1,0:T(4,128)(2,1)} %all_to_all.35), calls=%async_computation | async-start | bytes 131072 | tf_op jit(solution)/shard_map/all_to_all | solution.py:47
  21.5 1.4 fusion.60
  22.9 4.8 %all-to-all-done = bf16[16,4,512]{2,1,0:T(4,128)(2,1)S(1)} async-done(((bf16[16,4,512]{2,1,0:T(4,128)(2,1)}), bf16[16,4,512]{2,1,0:T(4,128)(2,1)S(1)}, u32[]{:S(2)}, u32[]{:S(2)}) %all-to-all-start) | async-done | bytes 65568 | tf_op jit(solution)/shard_map/all_to_all | solution.py:47
  28.7 5.8 %all_gather.3 = bf16[256,512]{1,0:T(8,128)(2,1)S(1)} all-gather(bf16[64,512]{1,0:T(8,128)(2,1)S(1)} %multiply_convert_fusion.11.refs_3_), channel_id=1, replica_groups=mesh['groups'=2,'grid'=4,'mesh'=4] {'grid'}, dimensions={0}, use_global_device_ids=true | all-gather | bytes 327680 | tf_op jit(solution)/shard_map/all_gather | solution.py:295
  34.7 2.3 %collective-permute-start = (bf16[128,512]{1,0:T(8,128)(2,1)S(1)}, bf16[128,512]{1,0:T(8,128)(2,1)S(1)}, u32[]{:S(2)}, u32[]{:S(2)}) collective-permute-start(bf16[128,512]{1,0:T(8,128)(2,1)S(1)} %convolution_convert_fusion.6), channel_id=1, source_target_pairs={{0,1},{1,2},{2,3},{4,5},{5,6},{6,7},{8,9},{9,10},{10,11},{12,13},{... | collective-permute-start | bytes 393224 | tf_op jit(solution)/shard_map/ppermute | solution.py:54
  37.2 1.3 collective-permute-start.1
  38.5 1.2 convolution_convert_fusion.17
  40.3 4.3 %collective-permute-done.1 = bf16[128,512]{1,0:T(8,128)(2,1)S(1)} collective-permute-done((bf16[128,512]{1,0:T(8,128)(2,1)S(1)}, bf16[128,512]{1,0:T(8,128)(2,1)S(1)}, u32[]{:S(2)}, u32[]{:S(2)}) %collective-permute-start.1) | collective-permute-done | bytes 131104 | tf_op jit(solution)/shard_map/ppermute | solution.py:55
  44.6 1.5 convolution_convert_fusion.1
  46.1 1.9 fusion.3
  48.1 1.5 fusion.27.refs_5_
  50.3 1.0 multiply_convert_fusion.9
  51.2 1.4 convolution_convert_fusion.15
  52.6 0.7 all_to_all.38
  53.3 3.5 %all-to-all-start.1 = ((bf16[16,4,512]{2,1,0:T(4,128)(2,1)}), bf16[16,4,512]{2,1,0:T(4,128)(2,1)S(1)}, u32[]{:S(2)}, u32[]{:S(2)}) async-start(bf16[16,4,512]{2,1,0:T(4,128)(2,1)} %all_to_all.38), calls=%async_computation.1 | async-start | bytes 131072 | tf_op jit(solution)/shard_map/all_to_all | solution.py:47
  57.1 6.3 %all-to-all-done.1 = bf16[16,4,512]{2,1,0:T(4,128)(2,1)S(1)} async-done(((bf16[16,4,512]{2,1,0:T(4,128)(2,1)}), bf16[16,4,512]{2,1,0:T(4,128)(2,1)S(1)}, u32[]{:S(2)}, u32[]{:S(2)}) %all-to-all-start.1) | async-done | bytes 65568 | tf_op jit(solution)/shard_map/all_to_all | solution.py:47
  63.4 3.1 %multiply_convert_fusion.5 = (bf16[512,512]{1,0:T(8,128)(2,1)}, f32[512,512]{1,0:T(8,128)}) fusion(f32[512,512]{1,0:T(8,128)} %fusion.60, bf16[64,512]{1,0:T(8,128)(2,1)S(1)} %all_to_all.40.refs_13_, bf16[1024,512]{1,0:T(8,128)(2,1)} %param.44, s32[64]{0:T(128)S(1)} %eq.62), kind=kOutput, calls=%fused_computation.61 | convolution fusion | flops 68747264 | bytes 3211520 | tf_op jit(solution)/shard_map/dot_general | solution.py:17
  66.5 2.0 %fusion.18.refs_10_ = bf16[512,512]{1,0:T(8,128)(2,1)S(1)} fusion(bf16[227,512]{1,0:T(8,128)(2,1)} %param.24, bf16[227,512]{1,0:T(8,128)(2,1)} %param.45, f32[512,512]{1,0:T(8,128)} %get-tuple-element.63), kind=kOutput, calls=%fused_computation.25 | convolution fusion | flops 121896960 | bytes 2037760 | tf_op jit(solution)/shard_map/dot_general | solution.py:17
  68.6 0.9 convolution_convert_fusion.13.refs_12_
  69.8 0.7 all_to_all.41
  70.4 10.1 %all_to_all.53 = bf16[16,4,512]{2,1,0:T(4,128)(2,1)S(1)} all-to-all(bf16[16,4,512]{2,1,0:T(4,128)(2,1)} %all_to_all.41), channel_id=1, replica_groups=mesh['groups'=2,'grid'=4,'mesh'=4] {'grid','mesh'}, dimensions={0} | all-to-all | bytes 131072 | tf_op jit(solution)/shard_map/all_to_all | solution.py:47
  80.5 0.6 all_to_all.43
  81.2 1.1 convolution_convert_fusion.11.refs_8_
  82.3 1.4 fusion.30.refs_6_
  83.6 1.1 fusion.31
  85.4 4.9 %multiply_convert_fusion = bf16[2048,512]{1,0:T(8,128)(2,1)} fusion(f32[2048,512]{1,0:T(8,128)} %copy-done.47, bf16[1,512,512]{2,1,0:T(8,128)(2,1)} %param.41, s32[2048]{0:T(1024)S(1)} %copy-done.25, f32[64,1024]{1,0:T(8,128)} %fusion.31), kind=kOutput, calls=%fused_computation.3 | convolution fusion | flops 177373184 | bytes 6889472 | tf_op jit(solution)/shard_map/dot_general | solution.py:17
  90.4 4.0 %fusion.10 = bf16[576,512]{1,0:T(8,128)(2,1)S(1)} fusion(bf16[2048,512]{1,0:T(8,128)(2,1)} %multiply_convert_fusion, s32[2048]{0:T(1024)S(1)} %broadcast_add_fusion, s32[2048]{0:T(1024)} %param.31), kind=kOutput, calls=%fused_computation.15 | convolution fusion | flops 1211793408 | bytes 2703360 | tf_op jit(solution)/shard_map/dot_general | solution.py:17
  94.4 1.5 fusion.88
  96.0 0.7 fusion.85
  96.7 2.9 %collective-permute-start.2 = (bf16[128,512]{1,0:T(8,128)(2,1)}, bf16[128,512]{1,0:T(8,128)(2,1)}, u32[]{:S(2)}, u32[]{:S(2)}) collective-permute-start(bf16[128,512]{1,0:T(8,128)(2,1)} %get-tuple-element.49), channel_id=1, source_target_pairs={{0,1},{1,2},{2,3},{4,5},{5,6},{6,7},{8,9},{9,10},{10,11},{12,13},{... | collective-permute-start | bytes 393224 | tf_op jit(solution)/shard_map/ppermute | solution.py:54
  99.6 1.3 collective-permute-start.3
  101.0 0.9 slice.151.refs_4_
  101.9 1.6 shard_map.302
  103.5 2.0 %copy-done.1 = bf16[512,4096]{1,0:T(8,128)(2,1)} copy-done((bf16[512,4096]{1,0:T(8,128)(2,1)}, bf16[512,4096]{1,0:T(8,128)(2,1)S(1)}, u32[]{:S(2)}) %copy-start.1) | copy-done | bytes 4194328
  105.5 1.5 collective-permute-done.3
  107.2 0.8 copy.48
  108.2 1.2 fusion.62
  109.4 2.2 %fusion.21 = bf16[256,512]{1,0:T(8,128)(2,1)} fusion(f32[256,512]{1,0:T(8,128)S(1)} %fusion.62, bf16[128,512]{1,0:T(8,128)(2,1)} %collective-permute-done.2, f32[512,512]{1,0:T(8,128)} %get-tuple-element.65, s32[128]{0:T(128)S(1)} %copy-done.37), kind=kOutput, calls=%fused_computation.29 | convolution fusion | flops 33980416 | bytes 1442304 | tf_op jit(solution)/shard_map/dot_general | solution.py:17
  111.6 3.6 %all-to-all-start.3 = ((bf16[4,64,512]{2,1,0:T(8,128)(2,1)}), bf16[4,64,512]{2,1,0:T(8,128)(2,1)S(1)}, u32[]{:S(2)}, u32[]{:S(2)}) async-start(bf16[4,64,512]{2,1,0:T(8,128)(2,1)} %bitcast.105), calls=%async_computation.3 | async-start | bytes 524288 | tf_op jit(solution)/shard_map/all_to_all | solution.py:359
  115.2 1.9 pad_bitcast_fusion
  117.1 4.1 %all-to-all-done.3 = bf16[4,64,512]{2,1,0:T(8,128)(2,1)S(1)} async-done(((bf16[4,64,512]{2,1,0:T(8,128)(2,1)}), bf16[4,64,512]{2,1,0:T(8,128)(2,1)S(1)}, u32[]{:S(2)}, u32[]{:S(2)}) %all-to-all-start.3) | async-done | bytes 262176 | tf_op jit(solution)/shard_map/all_to_all | solution.py:359
  121.2 1.5 multiply_reduce_fusion
  123.0 0.7 all_to_all.46
  123.6 3.7 %all-to-all-start.4 = ((bf16[16,4,512]{2,1,0:T(4,128)(2,1)}), bf16[16,4,512]{2,1,0:T(4,128)(2,1)S(1)}, u32[]{:S(2)}, u32[]{:S(2)}) async-start(bf16[16,4,512]{2,1,0:T(4,128)(2,1)} %all_to_all.46), calls=%async_computation.4 | async-start | bytes 131072 | tf_op jit(solution)/shard_map/all_to_all | solution.py:47
  127.4 2.5 %fusion.58 = f32[512,512]{1,0:T(8,128)} fusion(bf16[512,512]{1,0:T(8,128)(2,1)S(1)} %fusion.18.refs_10_, bf16[1024,512]{1,0:T(8,128)(2,1)} %param.44), kind=kOutput, calls=%fused_computation.87 | convolution fusion | flops 268435456 | bytes 2097152 | tf_op jit(solution)/shard_map/dot_general | solution.py:17
  129.9 4.2 %all-to-all-done.4 = bf16[16,4,512]{2,1,0:T(4,128)(2,1)S(1)} async-done(((bf16[16,4,512]{2,1,0:T(4,128)(2,1)}), bf16[16,4,512]{2,1,0:T(4,128)(2,1)S(1)}, u32[]{:S(2)}, u32[]{:S(2)}) %all-to-all-start.4) | async-done | bytes 65568 | tf_op jit(solution)/shard_map/all_to_all | solution.py:47
  134.1 1.0 multiply_convert_fusion.7.refs_4_.refs_6_
  135.1 2.0 %fusion.13.refs_2_ = bf16[512,512]{1,0:T(8,128)(2,1)S(1)} fusion(f32[512,512]{1,0:T(8,128)} %fusion.58, bf16[64,512]{1,0:T(8,128)(2,1)S(1)} %multiply_convert_fusion.7.refs_4_.refs_6_, bf16[512,512]{1,0:T(8,128)(2,1)} %param.38, s32[64]{0:T(128)S(1)} %copy-done.32), kind=kOutput, calls=%fused_computation.16 | convolution fusion | flops 67698688 | bytes 2162944 | tf_op jit(solution)/shard_map/dot_general | solution.py:17
  137.1 2.1 %fusion.19.refs_0_ = bf16[512,512]{1,0:T(8,128)(2,1)S(1)} fusion(bf16[512,512]{1,0:T(8,128)(2,1)S(1)} %fusion.13.refs_2_, bf16[512,512]{1,0:T(8,128)(2,1)S(1)} %copy-done.19, f32[512,512]{1,0:T(8,128)} %get-tuple-element.55), kind=kOutput, calls=%fused_computation.26 | convolution fusion | flops 271319040 | bytes 2621440 | tf_op jit(solution)/shard_map/dot_general | solution.py:17
  139.2 1.1 copy-done.3
  140.3 0.9 shard_map.303.x_ref
  141.2 9.8 %reduce-scatter.3.cloned.1.call-done = bf16[128,4096]{1,0:T(8,128)(2,1)} async-done(((bf16[512,4096]{1,0:T(8,128)(2,1)}), bf16[128,4096]{1,0:T(8,128)(2,1)}) %reduce-scatter.3.cloned.1.call-update) | async-done | bytes 1048592 | tf_op jit(solution)/shard_map/reduce_scatter | solution.py:353
  151.1 2.1 %fusion.22 = bf16[227,512]{1,0:T(8,128)(2,1)} fusion(bf16[512,512]{1,0:T(8,128)(2,1)} %get-tuple-element.62.refs_8_, bf16[227,512]{1,0:T(8,128)(2,1)} %param.45), kind=kOutput, calls=%fused_computation.31 | convolution fusion | flops 119129600 | bytes 989184 | tf_op jit(solution)/shard_map/dot_general | solution.py:17
  153.2 30.2 %shard_map.304 = f32[32,1664]{1,0:T(8,128)S(1)} custom-call(bf16[512,1664]{1,0:T(8,128)(2,1)S(1)} %shard_map.303.x_ref), custom_call_target="tpu_custom_call" | custom-call | bytes 90000000 | tf_op jit(solution)/shard_map/pallas_call | solution.py:228
  183.5 0.7 copy.49
  184.7 0.7 slice_bitcast_fusion.5
  185.4 2.5 %reduce-scatter.5.cloned.1.call-done = bf16[32,4096]{1,0:T(8,128)(2,1)} async-done(((bf16[128,4096]{1,0:T(8,128)(2,1)}), bf16[32,4096]{1,0:T(8,128)(2,1)}) %reduce-scatter.5.cloned.1.call-update) | async-done | bytes 262160 | tf_op jit(solution)/shard_map/reduce_scatter | solution.py:387
  187.9 1.0 convert_element_type.201
  188.9 0.8 slice_bitcast_fusion
  189.7 0.7 slice_bitcast_fusion.3
  (137 shorter events, 7.0 us)
Async XLA Ops:
  7.2 43.1 %copy-start = (bf16[1,1024,512]{2,1,0:T(8,128)(2,1)S(1)}, bf16[1,1024,512]{2,1,0:T(8,128)(2,1)}, u32[]{:S(2)}) copy-start(bf16[1,1024,512]{2,1,0:T(8,128)(2,1)} %param.42) | copy-start | bytes 3145732
  7.2 4.3 %copy-start.33 = (bf16[4,64]{1,0:T(4,128)(2,1)S(1)}, bf16[4,64]{1,0:T(4,128)(2,1)}, u32[]{:S(2)}) copy-start(bf16[4,64]{1,0:T(4,128)(2,1)} %param.26) | copy-start | bytes 1540
  7.2 4.3 %copy-start.35 = (bf16[4,512]{1,0:T(4,128)(2,1)S(1)}, bf16[4,512]{1,0:T(4,128)(2,1)}, u32[]{:S(2)}) copy-start(bf16[4,512]{1,0:T(4,128)(2,1)} %param.39) | copy-start | bytes 12292
  8.1 3.4 %copy-start.31 = (s32[64]{0:T(128)}, s32[64]{0:T(128)S(1)}, u32[]{:S(2)}) copy-start(s32[64]{0:T(128)S(1)} %eq.137) | copy-start | bytes 772
  8.2 2.7 %copy-start.18 = (bf16[512,512]{1,0:T(8,128)(2,1)S(1)}, bf16[512,512]{1,0:T(8,128)(2,1)}, u32[]{:S(2)}) copy-start(bf16[512,512]{1,0:T(8,128)(2,1)} %param.37) | copy-start | bytes 1572868
  8.2 4.0 %copy-start.17 = (bf16[512,512]{1,0:T(8,128)(2,1)S(1)}, bf16[512,512]{1,0:T(8,128)(2,1)}, u32[]{:S(2)}) copy-start(bf16[512,512]{1,0:T(8,128)(2,1)} %param.38) | copy-start | bytes 1572868
  8.2 12.9 %copy-start.39 = (s32[16,4]{0,1:T(4,128)S(1)}, s32[16,4]{0,1:T(4,128)}, u32[]{:S(2)}) copy-start(s32[16,4]{0,1:T(4,128)} %param.27) | copy-start | bytes 772
  8.2 12.9 %copy-start.44 = (s32[16]{0:T(128)S(1)}, s32[16]{0:T(128)}, u32[]{:S(2)}) copy-start(s32[16]{0:T(128)} %param.28) | copy-start | bytes 196
  8.2 13.1 %copy-start.38 = (s32[16,4]{0,1:T(4,128)S(1)}, s32[16,4]{0,1:T(4,128)}, u32[]{:S(2)}) copy-start(s32[16,4]{0,1:T(4,128)} %param.33) | copy-start | bytes 772
  8.2 13.2 %copy-start.13 = (bf16[1024,512]{1,0:T(8,128)(2,1)S(1)}, bf16[1024,512]{1,0:T(8,128)(2,1)}, u32[]{:S(2)}) copy-start(bf16[1024,512]{1,0:T(8,128)(2,1)} %param.44) | copy-start | bytes 3145732
  8.2 14.7 %copy-start.25 = (s32[2048]{0:T(1024)S(1)}, s32[2048]{0:T(1024)}, u32[]{:S(2)}) copy-start(s32[2048]{0:T(1024)} %param.32) | copy-start | bytes 24580
  10.8 23.7 %copy-start.41 = (s32[128]{0:T(128)S(1)}, s32[128]{0:T(128)}, u32[]{:S(2)}) copy-start(s32[128]{0:T(128)} %param.29) | copy-start | bytes 1540
  10.8 26.2 %copy-start.36 = (s32[128]{0:T(128)S(1)}, s32[128]{0:T(128)}, u32[]{:S(2)}) copy-start(s32[128]{0:T(128)} %param.30) | copy-start | bytes 1540
  11.5 0.6 copy-start.7
  12.2 33.9 %copy-start.46 = (s32[2048]{0:T(1024)S(1)}, s32[2048]{0:T(1024)}, u32[]{:S(2)}) copy-start(s32[2048]{0:T(1024)} %param.31) | copy-start | bytes 24580
  13.7 14.0 %all-to-all-start = ((bf16[16,4,512]{2,1,0:T(4,128)(2,1)}), bf16[16,4,512]{2,1,0:T(4,128)(2,1)S(1)}, u32[]{:S(2)}, u32[]{:S(2)}) async-start(bf16[16,4,512]{2,1,0:T(4,128)(2,1)} %all_to_all.35), calls=%async_computation | async-start | bytes 131072 | tf_op jit(solution)/shard_map/all_to_all | solution.py:47
  21.3 26.8 %copy-start.28 = (s32[64]{0:T(128)}, s32[64]{0:T(128)S(1)}, u32[]{:S(2)}) copy-start(s32[64]{0:T(128)S(1)} %eq.133) | copy-start | bytes 772
  21.5 29.8 %copy-start.30 = (s32[64]{0:T(128)}, s32[64]{0:T(128)S(1)}, u32[]{:S(2)}) copy-start(s32[64]{0:T(128)S(1)} %eq.129) | copy-start | bytes 772
  28.0 0.7 copy-start.15
  28.0 0.6 copy-start.26
  34.7 5.5 %collective-permute-start = (bf16[128,512]{1,0:T(8,128)(2,1)S(1)}, bf16[128,512]{1,0:T(8,128)(2,1)S(1)}, u32[]{:S(2)}, u32[]{:S(2)}) collective-permute-start(bf16[128,512]{1,0:T(8,128)(2,1)S(1)} %convolution_convert_fusion.6), channel_id=1, source_target_pairs={{0,1},{1,2},{2,3},{4,5},{5,6},{6,7},{8,9},{9,10},{10,11},{12,13},{... | collective-permute-start | bytes 393224 | tf_op jit(solution)/shard_map/ppermute | solution.py:54
  37.2 7.4 %collective-permute-start.1 = (bf16[128,512]{1,0:T(8,128)(2,1)S(1)}, bf16[128,512]{1,0:T(8,128)(2,1)S(1)}, u32[]{:S(2)}, u32[]{:S(2)}) collective-permute-start(bf16[128,512]{1,0:T(8,128)(2,1)S(1)} %convolution_convert_fusion.5), channel_id=1, source_target_pairs={{1,0},{2,1},{3,2},{5,4},{6,5},{7,6},{9,8},{10,9},{11,10},{13,12},{... | collective-permute-start | bytes 393224 | tf_op jit(solution)/shard_map/ppermute | solution.py:55
  48.0 2.0 %copy-start.47 = (f32[2048,512]{1,0:T(8,128)}, f32[2048,512]{1,0:T(8,128)S(1)}, u32[]{:S(2)}) copy-start(f32[2048,512]{1,0:T(8,128)S(1)} %fusion.3) | copy-start | bytes 12582916
  48.1 2.0 %copy-start.20 = (bf16[1,512,512]{2,1,0:T(8,128)(2,1)S(1)}, bf16[1,512,512]{2,1,0:T(8,128)(2,1)}, u32[]{:S(2)}) copy-start(bf16[1,512,512]{2,1,0:T(8,128)(2,1)} %param.41) | copy-start | bytes 1572868
  48.1 8.8 %copy-start.40 = (s32[16,4]{0,1:T(4,128)S(1)}, s32[16,4]{0,1:T(4,128)}, u32[]{:S(2)}) copy-start(s32[16,4]{0,1:T(4,128)} %param.34) | copy-start | bytes 772
  48.1 8.8 %copy-start.45 = (s32[16]{0:T(128)S(1)}, s32[16]{0:T(128)}, u32[]{:S(2)}) copy-start(s32[16]{0:T(128)} %param.35) | copy-start | bytes 196
  50.3 1.0 copy-start.21
  53.3 10.1 %all-to-all-start.1 = ((bf16[16,4,512]{2,1,0:T(4,128)(2,1)}), bf16[16,4,512]{2,1,0:T(4,128)(2,1)S(1)}, u32[]{:S(2)}, u32[]{:S(2)}) async-start(bf16[16,4,512]{2,1,0:T(4,128)(2,1)} %all_to_all.38), calls=%async_computation.1 | async-start | bytes 131072 | tf_op jit(solution)/shard_map/all_to_all | solution.py:47
  56.8 94.3 %reduce-scatter.3.cloned.1.call-start = ((), (), s32[]{:S(2)}) async-start(), calls=%async_computation.7 | async-start | bytes 5242880 | tf_op jit(solution)/shard_map/reduce_scatter | solution.py:353
  57.1 9.5 %copy-start.43 = (s32[64]{0:T(128)}, s32[64]{0:T(128)S(1)}, u32[]{:S(2)}) copy-start(s32[64]{0:T(128)S(1)} %eq.62) | copy-start | bytes 772
  66.5 3.0 %copy-start.14 = (bf16[1024,512]{1,0:T(8,128)(2,1)S(1)}, bf16[1024,512]{1,0:T(8,128)(2,1)}, u32[]{:S(2)}) copy-start(bf16[1024,512]{1,0:T(8,128)(2,1)} %param.44) | copy-start | bytes 3145732
  84.8 0.6 copy-start.9
  90.4 4.0 %copy-start.11 = (bf16[1,1024,512]{2,1,0:T(8,128)(2,1)S(1)}, bf16[1,1024,512]{2,1,0:T(8,128)(2,1)}, u32[]{:S(2)}) copy-start(bf16[1,1024,512]{2,1,0:T(8,128)(2,1)} %param.40) | copy-start | bytes 3145732
  90.4 10.5 %copy-start.22 = (bf16[64,512]{1,0:T(8,128)(2,1)S(1)}, bf16[64,512]{1,0:T(8,128)(2,1)}, u32[]{:S(2)}) copy-start(bf16[64,512]{1,0:T(8,128)(2,1)} %copy-done.21) | copy-start | bytes 196612
  94.4 6.5 %copy-start.12 = (bf16[576,512]{1,0:T(8,128)(2,1)}, bf16[576,512]{1,0:T(8,128)(2,1)S(1)}, u32[]{:S(2)}) copy-start(bf16[576,512]{1,0:T(8,128)(2,1)S(1)} %fusion.10) | copy-start | bytes 1769476
  94.4 7.5 %copy-start.10 = (bf16[64,512]{1,0:T(8,128)(2,1)S(1)}, bf16[64,512]{1,0:T(8,128)(2,1)}, u32[]{:S(2)}) copy-start(bf16[64,512]{1,0:T(8,128)(2,1)} %copy-done.9) | copy-start | bytes 196612
  96.7 8.8 %collective-permute-start.2 = (bf16[128,512]{1,0:T(8,128)(2,1)}, bf16[128,512]{1,0:T(8,128)(2,1)}, u32[]{:S(2)}, u32[]{:S(2)}) collective-permute-start(bf16[128,512]{1,0:T(8,128)(2,1)} %get-tuple-element.49), channel_id=1, source_target_pairs={{0,1},{1,2},{2,3},{4,5},{5,6},{6,7},{8,9},{9,10},{10,11},{12,13},{... | collective-permute-start | bytes 393224 | tf_op jit(solution)/shard_map/ppermute | solution.py:54
  99.6 7.4 %collective-permute-start.3 = (bf16[128,512]{1,0:T(8,128)(2,1)}, bf16[128,512]{1,0:T(8,128)(2,1)}, u32[]{:S(2)}, u32[]{:S(2)}) collective-permute-start(bf16[128,512]{1,0:T(8,128)(2,1)} %get-tuple-element.48), channel_id=1, source_target_pairs={{1,0},{2,1},{3,2},{5,4},{6,5},{7,6},{9,8},{10,9},{11,10},{13,12},{... | collective-permute-start | bytes 393224 | tf_op jit(solution)/shard_map/ppermute | solution.py:55
  103.5 2.0 %copy-start.1 = (bf16[512,4096]{1,0:T(8,128)(2,1)}, bf16[512,4096]{1,0:T(8,128)(2,1)S(1)}, u32[]{:S(2)}) copy-start(bf16[512,4096]{1,0:T(8,128)(2,1)S(1)} %shard_map.302) | copy-start | bytes 12582916
  105.4 1.6 copy-start.23
  105.4 1.8 copy-start.24
  105.4 2.6 %copy-start.34 = (bf16[4,64]{1,0:T(4,128)(2,1)S(1)}, bf16[4,64]{1,0:T(4,128)(2,1)}, u32[]{:S(2)}) copy-start(bf16[4,64]{1,0:T(4,128)(2,1)} %param.26) | copy-start | bytes 1540
  105.4 2.7 %copy-start.42 = (s32[128]{0:T(128)S(1)}, s32[128]{0:T(128)}, u32[]{:S(2)}) copy-start(s32[128]{0:T(128)} %param.29) | copy-start | bytes 1540
  105.5 4.0 %copy-start.37 = (s32[128]{0:T(128)S(1)}, s32[128]{0:T(128)}, u32[]{:S(2)}) copy-start(s32[128]{0:T(128)} %param.30) | copy-start | bytes 1540
  105.5 15.8 %copy-start.16 = (f32[64,512]{1,0:T(8,128)S(1)}, f32[64,512]{1,0:T(8,128)}, u32[]{:S(2)}) copy-start(f32[64,512]{1,0:T(8,128)} %copy-done.15) | copy-start | bytes 393220
  105.5 15.8 %copy-start.27 = (f32[64]{0:T(128)S(1)}, f32[64]{0:T(128)}, u32[]{:S(2)}) copy-start(f32[64]{0:T(128)} %copy-done.26) | copy-start | bytes 772
  107.1 15.7 %copy-start.29 = (s32[64]{0:T(128)S(1)}, s32[64]{0:T(128)}, u32[]{:S(2)}) copy-start(s32[64]{0:T(128)} %copy-done.28) | copy-start | bytes 772
  108.2 26.9 %copy-start.32 = (s32[64]{0:T(128)S(1)}, s32[64]{0:T(128)}, u32[]{:S(2)}) copy-start(s32[64]{0:T(128)} %copy-done.31) | copy-start | bytes 772
  111.6 25.5 %copy-start.19 = (bf16[512,512]{1,0:T(8,128)(2,1)S(1)}, bf16[512,512]{1,0:T(8,128)(2,1)}, u32[]{:S(2)}) copy-start(bf16[512,512]{1,0:T(8,128)(2,1)} %param.37) | copy-start | bytes 1572868
  111.6 9.6 %all-to-all-start.3 = ((bf16[4,64,512]{2,1,0:T(8,128)(2,1)}), bf16[4,64,512]{2,1,0:T(8,128)(2,1)S(1)}, u32[]{:S(2)}, u32[]{:S(2)}) async-start(bf16[4,64,512]{2,1,0:T(8,128)(2,1)} %bitcast.105), calls=%async_computation.3 | async-start | bytes 524288 | tf_op jit(solution)/shard_map/all_to_all | solution.py:359
  123.6 10.4 %all-to-all-start.4 = ((bf16[16,4,512]{2,1,0:T(4,128)(2,1)}), bf16[16,4,512]{2,1,0:T(4,128)(2,1)S(1)}, u32[]{:S(2)}, u32[]{:S(2)}) async-start(bf16[16,4,512]{2,1,0:T(4,128)(2,1)} %all_to_all.46), calls=%async_computation.4 | async-start | bytes 131072 | tf_op jit(solution)/shard_map/all_to_all | solution.py:47
  127.3 60.6 %reduce-scatter.5.cloned.1.call-start = ((), (), s32[]{:S(2)}) async-start(), calls=%async_computation.8 | async-start | bytes 1310720 | tf_op jit(solution)/shard_map/reduce_scatter | solution.py:387
  135.1 4.1 %copy-start.8 = (bf16[64,512]{1,0:T(8,128)(2,1)S(1)}, bf16[64,512]{1,0:T(8,128)(2,1)}, u32[]{:S(2)}) copy-start(bf16[64,512]{1,0:T(8,128)(2,1)} %copy-done.7) | copy-start | bytes 196612
  137.0 2.1 %copy-start.2 = (bf16[512,512]{1,0:T(8,128)(2,1)}, bf16[512,512]{1,0:T(8,128)(2,1)S(1)}, u32[]{:S(2)}) copy-start(bf16[512,512]{1,0:T(8,128)(2,1)S(1)} %fusion.13.refs_2_) | copy-start | bytes 1572868
  137.1 2.1 %copy-start.4 = (bf16[512,512]{1,0:T(8,128)(2,1)S(1)}, bf16[512,512]{1,0:T(8,128)(2,1)}, u32[]{:S(2)}) copy-start(bf16[512,512]{1,0:T(8,128)(2,1)} %get-tuple-element.62.refs_8_) | copy-start | bytes 1572868
  137.1 2.1 %copy-start.5 = (bf16[512,256]{1,0:T(8,128)(2,1)S(1)}, bf16[512,256]{1,0:T(8,128)(2,1)}, u32[]{:S(2)}) copy-start(bf16[512,256]{1,0:T(8,128)(2,1)} %get-tuple-element.68.refs_9_) | copy-start | bytes 786436
  137.1 2.1 %copy-start.6 = (bf16[512,256]{1,0:T(8,128)(2,1)S(1)}, bf16[512,256]{1,0:T(8,128)(2,1)}, u32[]{:S(2)}) copy-start(bf16[512,256]{1,0:T(8,128)(2,1)} %get-tuple-element.69.refs_1_) | copy-start | bytes 786436
  139.2 1.1 copy-start.3
Sparse Core Ops, SparseCore 0:
  107.2 43.8 reduce-scatter.2
  153.5 34.4 reduce-scatter.4
